TPU v7x, 32 devices: a whole 2x2x4 slice. The times are simulated.
32 devices in a mesh: fsdp: 2 (over core), ctx: 4 (over z), dp: 4 (over y, x).
Axes of the slice: x: 2, y: 2, z: 4, core: 2. Of those that a mesh axis runs over, the one named last changes fastest.
Arguments:
- query_stream: bfloat16 [1, 512, 8192], P(None, 'ctx', ('fsdp', 'dp')), may hold values from -6 to 6
- key_stream: bfloat16 [1, 512, 8192], P(None, 'ctx', ('fsdp', 'dp')), may hold values from -6 to 6
- value_stream: bfloat16 [1, 512, 8192], P(None, 'ctx', ('fsdp', 'dp')), may hold values from -6 to 6
- document_starts: int32 [1, 512], replicated, may hold values 0 or 1
- medium_taps: bfloat16 [512, 128], P(None, 'fsdp'), may hold values from -0.5 to 0.5
- modal_rate: bfloat16 [512, 16], P('fsdp', 'dp'), may hold values from 3.886223e-05 to 0.032958984
- modal_residue: bfloat16 [512, 16], P('fsdp', 'dp'), may hold values from -4 to 4
- skip_gain: float32 [8192], P(('fsdp', 'dp')), may hold values from 0.5 to 1.5
Outputs:
- hyena_out: bfloat16 [1, 512, 8192], P(None, 'ctx', ('fsdp', 'dp'))
All inputs are finite; a program needn't handle non-finite values.
Results may differ from a plain program's by a relative error of at most 0.0085.
Values may be sent and summed in bfloat16 or wider, within the bound.
No kernel may reach another device: no remote copies, remote signals or barrier semaphores. Data moves between devices by JAX's collectives and lax.ppermute only.
A program may use at most 64 MiB of HBM per device.

v0:
```python
import jax
import jax.numpy as jnp
from jax import lax
from jax.sharding import PartitionSpec as P

GROUP_CH = 16


highest = lax.Precision.HIGHEST


def entering_2(array, axis, combine, identity):
    count, position = (lax.axis_size(axis), lax.axis_index(axis))
    everything = jax.tree.map(lambda part: lax.all_gather(part, axis), array)
    start = jax.tree.map(
        lambda part, zero: jnp.broadcast_to(jnp.asarray(zero, part.dtype), part.shape),
        array,
        identity,
    )

    def turn(k, before):
        reached = k < position
        new = combine(before, jax.tree.map(lambda part: part[k], everything))
        return jax.tree.map(lambda a, b: jnp.where(reached, a, b), new, before)

    return lax.fori_loop(0, count, turn, start)


def toeplitz_taps(filters, block_len):
    groups = filters.shape[0]
    line = jnp.concatenate(
        [
            jnp.zeros((groups, 1), filters.dtype),
            filters[:, ::-1],
            jnp.zeros((groups, block_len), filters.dtype),
        ],
        axis=1,
    )
    tiled = jnp.tile(line, (1, block_len))[:, : 2 * block_len * block_len]
    return tiled.reshape(groups, block_len, 2 * block_len)


def medium_conv(extended, padded_docs, filters):
    block_len = filters.shape[1]
    groups = filters.shape[0]
    channels = extended.shape[2]
    row_count = extended.shape[0] - block_len
    block_count = row_count // block_len
    matrix = toeplitz_taps(filters, block_len)
    previous = extended[:row_count].reshape(block_count, block_len, groups, channels)
    current = extended[block_len:].reshape(block_count, block_len, groups, channels)
    windows = jnp.concatenate([previous, current], axis=1)
    row_docs = padded_docs[block_len:].reshape(block_count, block_len)
    window_docs = jnp.concatenate(
        [padded_docs[:row_count].reshape(block_count, block_len), row_docs], axis=1
    )
    doc_masks = row_docs[:, :, None] == window_docs[:, None, :]
    nothing = jnp.zeros((), matrix.dtype)
    if block_count % 16 == 0 and block_count >= groups:

        def apply_part(inputs):
            mask_part, window_part = inputs
            masked = jnp.where(mask_part[:, None], matrix[None], nothing)
            return jnp.einsum(
                "ngtj,njgc->ntgc", masked, window_part, preferred_element_type=jnp.float32
            )

        outputs = lax.map(
            apply_part,
            (
                doc_masks.reshape(16, block_count // 16, block_len, 2 * block_len),
                windows.reshape(16, block_count // 16, 2 * block_len, groups, channels),
            ),
        )
        return outputs.reshape(row_count, groups, channels)
    if groups % 16 == 0:

        def apply_groups(inputs):
            matrix_part, window_part = inputs
            masked = jnp.where(doc_masks[:, None], matrix_part[None], nothing)
            return jnp.einsum(
                "ngtj,njgc->ntgc", masked, window_part, preferred_element_type=jnp.float32
            )

        split_windows = windows.reshape(
            block_count, 2 * block_len, 16, groups // 16, channels
        ).transpose(2, 0, 1, 3, 4)
        outputs = lax.map(
            apply_groups,
            (matrix.reshape(16, groups // 16, block_len, 2 * block_len), split_windows),
        )
        return outputs.transpose(1, 2, 0, 3, 4).reshape(row_count, groups, channels)
    masked = jnp.where(doc_masks[:, None], matrix[None], nothing)
    outputs = jnp.einsum("ngtj,njgc->ntgc", masked, windows, preferred_element_type=jnp.float32)
    return outputs.reshape(row_count, groups, channels)


def modal_blocks(values, doc_index, starts, decay_rate, scaled, carry_state, block_len):
    row_count = values.shape[0]
    block_count = row_count // block_len
    groups = values.shape[1]
    channels = values.shape[2]
    lag_steps = jnp.arange(block_len + 1, dtype=jnp.float32)
    powers = jnp.exp(-decay_rate[:, :, None] * lag_steps)
    kernel = jnp.einsum("gn,gnk->gk", scaled, powers[:, :, :block_len], precision=highest)
    positions = jnp.arange(block_len, dtype=jnp.int32)
    offsets = positions[:, None] - positions[None, :]
    causal = offsets >= 0
    toeplitz = toeplitz_taps(kernel, block_len)[:, :, block_len:]
    carry_weight = scaled[:, None, :] * jnp.transpose(powers[:, :, 1:], (0, 2, 1))
    end_weight = powers[:, :, :block_len][:, :, ::-1]
    full_decay = jnp.transpose(powers[:, :, block_len])

    def advance(state_now, inputs):
        block_values, block_docs, block_starts = inputs
        before = block_docs[0] - block_starts[0]
        continues = block_docs == before
        same_doc = causal & (block_docs[:, None] == block_docs[None, :])
        local_part = jnp.einsum(
            "gts,sgc->tgc",
            jnp.where(same_doc[None], toeplitz, 0.0),
            block_values,
            precision=highest,
        )
        carried = jnp.einsum(
            "gtn,ngc->tgc",
            jnp.where(continues[None, :, None], carry_weight, 0.0),
            state_now,
            precision=highest,
        )
        keep_mask = block_docs == block_docs[block_len - 1]
        emitted = jnp.einsum(
            "gns,sgc->ngc",
            jnp.where(keep_mask[None, None, :], end_weight, 0.0),
            block_values,
            precision=highest,
        )
        factor = jnp.where(continues[block_len - 1], full_decay, 0.0)
        return (factor[:, :, None] * state_now + emitted, local_part + carried)

    final_state, outputs = lax.scan(
        advance,
        carry_state,
        (
            values.reshape(block_count, block_len, groups, channels),
            doc_index.reshape(block_count, block_len),
            starts.reshape(block_count, block_len),
        ),
    )
    return (outputs.reshape(row_count, groups, channels), final_state)


def merge_carry(earlier, latter):
    decay_first, state_first = earlier
    decay_second, state_second = latter
    spread = state_first.reshape(decay_first.shape[0], decay_first.shape[1], -1)
    moved = (decay_second[:, :, None] * spread).reshape(state_first.shape)
    return (decay_first * decay_second, moved + state_second)


def body(
    query_stream,
    key_stream,
    value_stream,
    document_starts,
    medium_taps,
    modal_rate,
    modal_residue,
    skip_gain,
):
    tokens = query_stream.shape[1]
    local_width = query_stream.shape[2]
    fsdp_size = lax.axis_size("fsdp")
    dp_size = lax.axis_size("dp")
    dp_place = lax.axis_index("dp")
    block_len = medium_taps.shape[1] * fsdp_size
    ctx_size = lax.axis_size("ctx")
    ctx_place = lax.axis_index("ctx")
    groups_here = local_width // GROUP_CH
    product = (key_stream[0].astype(jnp.float32) * value_stream[0].astype(jnp.float32)).astype(
        jnp.bfloat16
    )
    starts = document_starts[0]
    doc_index = jnp.cumsum(starts)
    padded_docs = jnp.concatenate([jnp.full((block_len,), -1, jnp.int32), doc_index])
    quarters = medium_taps.reshape(fsdp_size, dp_size, groups_here, medium_taps.shape[1])
    halves = lax.dynamic_slice_in_dim(quarters, dp_place, 1, 1)[:, 0]
    channels = local_width // ctx_size
    per_device = channels // GROUP_CH
    own_rows = lax.dynamic_slice_in_dim(halves, ctx_place * per_device, per_device, 1)
    filters = lax.all_to_all(own_rows, "fsdp", split_axis=0, concat_axis=2, tiled=True)[0]
    outgoing = (
        product.reshape(tokens, ctx_size, channels)
        .transpose(1, 0, 2)
        .reshape(ctx_size, tokens * channels)
    )
    incoming = lax.all_to_all(outgoing, "ctx", split_axis=0, concat_axis=0, tiled=True)
    sequence = incoming.reshape(ctx_size * tokens, channels)
    extended = jnp.concatenate([jnp.zeros((block_len, channels), jnp.bfloat16), sequence]).reshape(
        -1, per_device, GROUP_CH
    )
    medium = medium_conv(extended, padded_docs, filters).astype(jnp.bfloat16)
    returned = lax.all_to_all(
        medium.reshape(ctx_size, tokens * channels), "ctx", split_axis=0, concat_axis=0, tiled=True
    )
    medium_local = (
        returned.reshape(ctx_size, tokens, channels).transpose(1, 0, 2).reshape(tokens, local_width)
    )
    gated_values = (query_stream[0].astype(jnp.float32) * medium_local.astype(jnp.float32)).astype(
        jnp.bfloat16
    )
    rate_all, residue_all = (
        lax.all_to_all(modal_rate, "dp", split_axis=0, concat_axis=1, tiled=True),
        lax.all_to_all(modal_residue, "dp", split_axis=0, concat_axis=1, tiled=True),
    )
    decay_rate = rate_all.astype(jnp.float32)
    mode_count = decay_rate.shape[1]
    scaled = residue_all.astype(jnp.float32) * jnp.sqrt(
        (1.0 - jnp.exp(-2.0 * decay_rate)) / mode_count
    )
    local_docs = lax.dynamic_slice_in_dim(doc_index, ctx_place * tokens, tokens, 0)
    local_starts = lax.dynamic_slice_in_dim(starts, ctx_place * tokens, tokens, 0)
    values = gated_values.astype(jnp.float32).reshape(tokens, groups_here, GROUP_CH)
    part_count = 4
    part_groups = groups_here // part_count
    split_values = values.reshape(tokens, part_count, part_groups, GROUP_CH).transpose(1, 0, 2, 3)

    def run_part(inputs):
        part_values, part_rate, part_scaled = inputs
        zero_state = jnp.zeros((mode_count, part_groups, GROUP_CH), jnp.float32)
        return modal_blocks(
            part_values, local_docs, local_starts, part_rate, part_scaled, zero_state, block_len
        )

    local_parts, end_parts = lax.map(
        run_part,
        (
            split_values,
            decay_rate.reshape(part_count, part_groups, mode_count),
            scaled.reshape(part_count, part_groups, mode_count),
        ),
    )
    local_long = local_parts.transpose(1, 0, 2, 3).reshape(tokens, local_width)
    end_states = end_parts.transpose(1, 0, 2, 3).reshape(mode_count, local_width)
    continues = local_docs == local_docs[0] - local_starts[0]
    factor = jnp.where(continues[tokens - 1], jnp.transpose(jnp.exp(-decay_rate * tokens)), 0.0)
    prefix_decay, entering = entering_2(
        (factor, end_states),
        "ctx",
        merge_carry,
        (jnp.ones_like(factor), jnp.zeros_like(end_states)),
    )
    lag_steps = jnp.arange(1, tokens + 1, dtype=jnp.float32)
    weights = scaled[:, :, None] * jnp.exp(-decay_rate[:, :, None] * lag_steps)
    masked = jnp.where(continues[None, None, :], weights, 0.0)
    carried = jnp.einsum(
        "gnt,ngc->tgc",
        masked,
        entering.reshape(mode_count, groups_here, GROUP_CH),
        precision=highest,
    )
    combined = (
        local_long
        + carried.reshape(tokens, local_width)
        + skip_gain[None, :] * gated_values.astype(jnp.float32)
    )
    return combined.astype(jnp.bfloat16)[None]


def solution(mesh):
    return jax.shard_map(
        body,
        mesh=mesh,
        in_specs=(
            P(None, "ctx", ("fsdp", "dp")),
            P(None, "ctx", ("fsdp", "dp")),
            P(None, "ctx", ("fsdp", "dp")),
            P(),
            P(None, "fsdp"),
            P("fsdp", "dp"),
            P("fsdp", "dp"),
            P(("fsdp", "dp")),
        ),
        out_specs=P(None, "ctx", ("fsdp", "dp")),
        check_vma=False,
    )
```

profile of v0, /device:TPU:8, one launch (start us, length us, event | category | flops | bytes accessed | tf_op | source)
XLA Modules:
  0.0 198.2 jit_solution(15075125949476915355)
XLA Ops:
  2.0 3.2 %all-to-all-start.1 = ((bf16[2,2,512]{2,1,0:T(2,128)(2,1)}), bf16[2,2,512]{2,1,0:T(2,128)(2,1)S(1)}, u32[]{:S(2)}, u32[]{:S(2)}) async-start(bf16[2,2,512]{2,1,0:T(2,128)(2,1)} %reshape.367), calls=%async_computation.1 | async-start | bytes 8192 | tf_op jit(solution)/shard_map/all_to_all | solution.py:191
  9.9 3.7 %all-to-all-start.4 = ((bf16[4,2,128]{2,1,0:T(2,128)(2,1)}), bf16[4,2,128]{2,1,0:T(2,128)(2,1)S(1)}, u32[]{:S(2)}, u32[]{:S(2)}) async-start(bf16[4,2,128]{2,1,0:T(2,128)(2,1)} %reshape.373), calls=%async_computation.4 | async-start | bytes 4096 | tf_op jit(solution)/shard_map/all_to_all | solution.py:213
  19.1 2.4 %reduce.6 = bf16[4,32768]{1,0:T(4,128)(2,1)S(1)} reduce(bf16[4,1,32768]{2,1,0:T(2,128)(2,1)S(1)} %all_to_all.51, bf16[]{:T(256)} %broadcast.200), dimensions={1}, to_apply=%all_to_all.51.reduce_sub_computation | reduce | bytes 524290 | tf_op jit(solution)/shard_map/all_to_all | solution.py:197
  25.7 4.2 %all-to-all-start.3 = ((bf16[4,2,128]{2,1,0:T(2,128)(2,1)}), bf16[4,2,128]{2,1,0:T(2,128)(2,1)S(1)}, u32[]{:S(2)}, u32[]{:S(2)}) async-start(bf16[4,2,128]{2,1,0:T(2,128)(2,1)} %reshape.371), calls=%async_computation.3 | async-start | bytes 4096 | tf_op jit(solution)/shard_map/all_to_all | solution.py:214
  30.1 4.3 %all-to-all-done.3 = bf16[4,2,128]{2,1,0:T(2,128)(2,1)S(1)} async-done(((bf16[4,2,128]{2,1,0:T(2,128)(2,1)}), bf16[4,2,128]{2,1,0:T(2,128)(2,1)S(1)}, u32[]{:S(2)}, u32[]{:S(2)}) %all-to-all-start.3) | async-done | bytes 2080 | tf_op jit(solution)/shard_map/all_to_all | solution.py:214
  34.4 5.3 %all-to-all-start = ((bf16[4,2,16384]{2,1,0:T(2,128)(2,1)}), bf16[4,2,16384]{2,1,0:T(2,128)(2,1)S(1)}, u32[]{:S(2)}, u32[]{:S(2)}) async-start(bf16[4,2,16384]{2,1,0:T(2,128)(2,1)} %reshape.365), calls=%async_computation | async-start | bytes 524288 | tf_op jit(solution)/shard_map/all_to_all | solution.py:197
  41.9 4.1 %all-to-all-done = bf16[4,2,16384]{2,1,0:T(2,128)(2,1)S(1)} async-done(((bf16[4,2,16384]{2,1,0:T(2,128)(2,1)}), bf16[4,2,16384]{2,1,0:T(2,128)(2,1)S(1)}, u32[]{:S(2)}, u32[]{:S(2)}) %all-to-all-start) | async-done | bytes 262176 | tf_op jit(solution)/shard_map/all_to_all | solution.py:197
  52.0 18.2 %while.45 = (s32[]{:T(128)}, bf16[16,4,128,1,16]{2,4,1,3,0:T(8,128)(2,1)S(1)}, bf16[16,4,256,1,16]{2,1,4,0,3:T(4,128)(2,1)S(1)}, bf16[16,1,128,256]{3,2,1,0:T(8,...) while((s32[]{:T(128)}, bf16[16,4,128,1,16]{2,4,1,3,0:T(8,128)(2,1)S(1)}, ...), condition=%wide.region_3.4_spmd.clone, body=%wide.region_2.3_spmd.clone.sunk | while | flops 4456450 | bytes 333921 | solution.py:88
  73.3 2.4 %reduce.7 = bf16[4,32768]{1,0:T(4,128)(2,1)S(1)} reduce(bf16[4,1,32768]{2,1,0:T(2,128)(2,1)S(1)} %convert_element_type.172, bf16[]{:T(256)} %broadcast.200), dimensions={1}, to_apply=%convert_element_type.172.reduce_sub_computation | reduce | bytes 524290 | tf_op jit(solution)/shard_map/convert_element_type | solution.py:202
  76.7 4.9 %all-to-all-start.2 = ((bf16[4,2,16384]{2,1,0:T(2,128)(2,1)}), bf16[4,2,16384]{2,1,0:T(2,128)(2,1)S(1)}, u32[]{:S(2)}, u32[]{:S(2)}) async-start(bf16[4,2,16384]{2,1,0:T(2,128)(2,1)} %reshape.369), calls=%async_computation.2 | async-start | bytes 524288 | tf_op jit(solution)/shard_map/all_to_all | solution.py:203
  82.3 13.3 %all-gather = f32[64,64]{1,0:T(8,128)S(1)} all-gather(f32[16,64]{1,0:T(8,128)S(1)} %select_bitcast_fusion), channel_id=2, replica_groups=mesh['fsdp'=2,'ctx'=4,'dp'=4] {'ctx'}, dimensions={0}, use_global_device_ids=true | all-gather | bytes 20480 | tf_op jit(solution)/shard_map/all_gather | solution.py:14
  98.7 81.1 %while.44 = (s32[]{:T(128)}, f32[4,128,16,16]{1,3,2,0:T(8,128)}, f32[4,16,16,16]{1,3,2,0:T(8,128)S(1)}, f32[4,128,16,16]{1,3,2,0:T(8,128)S(1)}, s32[128]{0:T(128...) while((s32[]{:T(128)}, f32[4,128,16,16]{1,3,2,0:T(8,128)}, ...), condition=%wide.region_5.6_spmd, body=%wide.region_4.5_spmd.sunk | while | flops 63812896 | bytes 26271760 | solution.py:235
  105.0 1.9 fusion.80
  109.5 2.5 %tile.25 = f32[16,32896]{1,0:T(8,128)} reshape(f32[16,128,257]{2,1,0:T(8,128)S(1)} %tile.24) | data formatting | bytes 4210688 | tf_op jit(solution)/shard_map/while/body/eval_jaxpr/tile | solution.py:39
  116.3 2.6 %fusion.83 = f32[4,128,16,16]{1,3,2,0:T(8,128)} fusion(f32[4,128,16,16]{1,3,2,0:T(8,128)} %get-tuple-element.543, s32[]{:T(128)S(6)} %copy.139, f32[16,16,128]{2,1,0:T(8,128)S(1)} %fusion.82, f32[16,16,128]{1,0,2:T(8,128)S(1)} %copy-done), kind=kOutput, calls=%fused_computation.7.clone.1 | convolution fusion | flops 6324224 | bytes 393220 | tf_op jit(solution)/shard_map/while/body/eval_jaxpr/while/body/eval_jaxpr/gtn,ngc->tgc/dot_general | solution.py:125
  129.8 2.5 %tile.25 = f32[16,32896]{1,0:T(8,128)} reshape(f32[16,128,257]{2,1,0:T(8,128)S(1)} %tile.24) | data formatting | bytes 4210688 | tf_op jit(solution)/shard_map/while/body/eval_jaxpr/tile | solution.py:39
  136.6 2.6 %fusion.83 = f32[4,128,16,16]{1,3,2,0:T(8,128)} fusion(f32[4,128,16,16]{1,3,2,0:T(8,128)} %get-tuple-element.543, s32[]{:T(128)S(6)} %copy.139, f32[16,16,128]{2,1,0:T(8,128)S(1)} %fusion.82, f32[16,16,128]{1,0,2:T(8,128)S(1)} %copy-done), kind=kOutput, calls=%fused_computation.7.clone.1 | convolution fusion | flops 6324224 | bytes 393220 | tf_op jit(solution)/shard_map/while/body/eval_jaxpr/while/body/eval_jaxpr/gtn,ngc->tgc/dot_general | solution.py:125
  150.0 2.5 %tile.25 = f32[16,32896]{1,0:T(8,128)} reshape(f32[16,128,257]{2,1,0:T(8,128)S(1)} %tile.24) | data formatting | bytes 4210688 | tf_op jit(solution)/shard_map/while/body/eval_jaxpr/tile | solution.py:39
  156.9 2.6 %fusion.83 = f32[4,128,16,16]{1,3,2,0:T(8,128)} fusion(f32[4,128,16,16]{1,3,2,0:T(8,128)} %get-tuple-element.543, s32[]{:T(128)S(6)} %copy.139, f32[16,16,128]{2,1,0:T(8,128)S(1)} %fusion.82, f32[16,16,128]{1,0,2:T(8,128)S(1)} %copy-done), kind=kOutput, calls=%fused_computation.7.clone.1 | convolution fusion | flops 6324224 | bytes 393220 | tf_op jit(solution)/shard_map/while/body/eval_jaxpr/while/body/eval_jaxpr/gtn,ngc->tgc/dot_general | solution.py:125
  165.8 1.9 fusion.80
  170.3 2.5 %tile.25 = f32[16,32896]{1,0:T(8,128)} reshape(f32[16,128,257]{2,1,0:T(8,128)S(1)} %tile.24) | data formatting | bytes 4210688 | tf_op jit(solution)/shard_map/while/body/eval_jaxpr/tile | solution.py:39
  177.2 2.6 %fusion.83 = f32[4,128,16,16]{1,3,2,0:T(8,128)} fusion(f32[4,128,16,16]{1,3,2,0:T(8,128)} %get-tuple-element.543, s32[]{:T(128)S(6)} %copy.139, f32[16,16,128]{2,1,0:T(8,128)S(1)} %fusion.82, f32[16,16,128]{1,0,2:T(8,128)S(1)} %copy-done), kind=kOutput, calls=%fused_computation.7.clone.1 | convolution fusion | flops 6324224 | bytes 393220 | tf_op jit(solution)/shard_map/while/body/eval_jaxpr/while/body/eval_jaxpr/gtn,ngc->tgc/dot_general | solution.py:125
  179.9 13.8 %all_gather.11 = f32[4,16,1024]{2,1,0:T(8,128)S(1)} all-gather(f32[1,16,1024]{2,1,0:T(8,128)S(1)} %copy.89), channel_id=1, replica_groups=mesh['fsdp'=2,'ctx'=4,'dp'=4] {'ctx'}, dimensions={0}, use_global_device_ids=true | all-gather | bytes 327680 | tf_op jit(solution)/shard_map/all_gather | solution.py:14
  193.7 2.2 %while.46 = (s32[]{:T(128)}, f32[16,1024]{1,0:T(8,128)S(1)}, s32[]{:T(128)}, f32[4,16,64]{2,1,0:T(8,128)S(1)}, f32[4,16,1024]{2,1,0:T(8,128)S(1)}, /*index=5*/s32[]{:T(128)}, s32[]{:T(128)}) while((s32[]{:T(128)}, f32[16,1024]{1,0:T(8,128)S(1)}, s32[]{:T(128)}, f32[4,16,64]{2,1,0:T(8,128)S(1)}, f32[4,16,1024]{2,1,0:T(8,128)S(1)}, ...), condition=%wide.region_7.8_spmd.clone, body=%wide.region_6.7_spmd.clone.sunk | while | flops 65540 | bytes 471153 | solution.py:26
  (322 shorter events, 110.5 us)
Async XLA Ops:
  0.0 17.9 %copy-start.10 = (bf16[1,128,1024]{2,1,0:T(8,128)(2,1)S(1)}, bf16[1,128,1024]{2,1,0:T(8,128)(2,1)}, u32[]{:S(2)}) copy-start(bf16[1,128,1024]{2,1,0:T(8,128)(2,1)} %param.14) | copy-start | bytes 786436
  2.0 8.0 %all-to-all-start.1 = ((bf16[2,2,512]{2,1,0:T(2,128)(2,1)}), bf16[2,2,512]{2,1,0:T(2,128)(2,1)S(1)}, u32[]{:S(2)}, u32[]{:S(2)}) async-start(bf16[2,2,512]{2,1,0:T(2,128)(2,1)} %reshape.367), calls=%async_computation.1 | async-start | bytes 8192 | tf_op jit(solution)/shard_map/all_to_all | solution.py:191
  9.9 15.8 %all-to-all-start.4 = ((bf16[4,2,128]{2,1,0:T(2,128)(2,1)}), bf16[4,2,128]{2,1,0:T(2,128)(2,1)S(1)}, u32[]{:S(2)}, u32[]{:S(2)}) async-start(bf16[4,2,128]{2,1,0:T(2,128)(2,1)} %reshape.373), calls=%async_computation.4 | async-start | bytes 4096 | tf_op jit(solution)/shard_map/all_to_all | solution.py:213
  25.7 8.7 %all-to-all-start.3 = ((bf16[4,2,128]{2,1,0:T(2,128)(2,1)}), bf16[4,2,128]{2,1,0:T(2,128)(2,1)S(1)}, u32[]{:S(2)}, u32[]{:S(2)}) async-start(bf16[4,2,128]{2,1,0:T(2,128)(2,1)} %reshape.371), calls=%async_computation.3 | async-start | bytes 4096 | tf_op jit(solution)/shard_map/all_to_all | solution.py:214
  34.4 11.6 %all-to-all-start = ((bf16[4,2,16384]{2,1,0:T(2,128)(2,1)}), bf16[4,2,16384]{2,1,0:T(2,128)(2,1)S(1)}, u32[]{:S(2)}, u32[]{:S(2)}) async-start(bf16[4,2,16384]{2,1,0:T(2,128)(2,1)} %reshape.365), calls=%async_computation | async-start | bytes 524288 | tf_op jit(solution)/shard_map/all_to_all | solution.py:197
  73.3 22.4 %copy-start.15 = (f32[4,16,16]{1,0,2:T(4,128)S(1)}, f32[4,16,16]{1,0,2:T(4,128)}, u32[]{:S(2)}) copy-start(f32[4,16,16]{1,0,2:T(4,128)} %reshape.343) | copy-start | bytes 12292
  76.7 19.0 %all-to-all-start.2 = ((bf16[4,2,16384]{2,1,0:T(2,128)(2,1)}), bf16[4,2,16384]{2,1,0:T(2,128)(2,1)S(1)}, u32[]{:S(2)}, u32[]{:S(2)}) async-start(bf16[4,2,16384]{2,1,0:T(2,128)(2,1)} %reshape.369), calls=%async_computation.2 | async-start | bytes 524288 | tf_op jit(solution)/shard_map/all_to_all | solution.py:203
  98.7 6.3 %copy-start.11 = (f32[4,16,16]{1,0,2:T(4,128)}, f32[4,16,16]{1,0,2:T(4,128)S(1)}, u32[]{:S(2)}) copy-start(f32[4,16,16]{1,0,2:T(4,128)S(1)} %get-tuple-element.558) | copy-start | bytes 12292 | tf_op jit(solution)/shard_map/while
  98.7 8.5 %copy-start.1 = (f32[4,128,16,16]{1,3,2,0:T(8,128)}, f32[4,128,16,16]{1,3,2,0:T(8,128)S(1)}, u32[]{:S(2)}) copy-start(f32[4,128,16,16]{1,3,2,0:T(8,128)S(1)} %get-tuple-element.556) | copy-start | bytes 1572868 | tf_op jit(solution)/shard_map/while
  114.2 4.7 %copy-start.7 = (f32[4,16,16,16]{1,3,2,0:T(8,128)S(1)}, f32[4,16,16,16]{1,3,2,0:T(8,128)}, u32[]{:S(2)}) copy-start(f32[4,16,16,16]{1,3,2,0:T(8,128)} %copy-done.6) | copy-start | bytes 196612 | tf_op jit(solution)/shard_map/while
  114.2 4.7 %copy-start.12 = (f32[4,16,16]{1,0,2:T(4,128)S(1)}, f32[4,16,16]{1,0,2:T(4,128)}, u32[]{:S(2)}) copy-start(f32[4,16,16]{1,0,2:T(4,128)} %copy-done.11) | copy-start | bytes 12292 | tf_op jit(solution)/shard_map/while
  119.0 6.3 %copy-start.11 = (f32[4,16,16]{1,0,2:T(4,128)}, f32[4,16,16]{1,0,2:T(4,128)S(1)}, u32[]{:S(2)}) copy-start(f32[4,16,16]{1,0,2:T(4,128)S(1)} %get-tuple-element.558) | copy-start | bytes 12292 | tf_op jit(solution)/shard_map/while
  119.0 8.5 %copy-start.1 = (f32[4,128,16,16]{1,3,2,0:T(8,128)}, f32[4,128,16,16]{1,3,2,0:T(8,128)S(1)}, u32[]{:S(2)}) copy-start(f32[4,128,16,16]{1,3,2,0:T(8,128)S(1)} %get-tuple-element.556) | copy-start | bytes 1572868 | tf_op jit(solution)/shard_map/while
  134.5 4.7 %copy-start.7 = (f32[4,16,16,16]{1,3,2,0:T(8,128)S(1)}, f32[4,16,16,16]{1,3,2,0:T(8,128)}, u32[]{:S(2)}) copy-start(f32[4,16,16,16]{1,3,2,0:T(8,128)} %copy-done.6) | copy-start | bytes 196612 | tf_op jit(solution)/shard_map/while
  134.5 4.7 %copy-start.12 = (f32[4,16,16]{1,0,2:T(4,128)S(1)}, f32[4,16,16]{1,0,2:T(4,128)}, u32[]{:S(2)}) copy-start(f32[4,16,16]{1,0,2:T(4,128)} %copy-done.11) | copy-start | bytes 12292 | tf_op jit(solution)/shard_map/while
  139.2 6.3 %copy-start.11 = (f32[4,16,16]{1,0,2:T(4,128)}, f32[4,16,16]{1,0,2:T(4,128)S(1)}, u32[]{:S(2)}) copy-start(f32[4,16,16]{1,0,2:T(4,128)S(1)} %get-tuple-element.558) | copy-start | bytes 12292 | tf_op jit(solution)/shard_map/while
  139.2 8.5 %copy-start.1 = (f32[4,128,16,16]{1,3,2,0:T(8,128)}, f32[4,128,16,16]{1,3,2,0:T(8,128)S(1)}, u32[]{:S(2)}) copy-start(f32[4,128,16,16]{1,3,2,0:T(8,128)S(1)} %get-tuple-element.556) | copy-start | bytes 1572868 | tf_op jit(solution)/shard_map/while
  154.8 4.7 %copy-start.7 = (f32[4,16,16,16]{1,3,2,0:T(8,128)S(1)}, f32[4,16,16,16]{1,3,2,0:T(8,128)}, u32[]{:S(2)}) copy-start(f32[4,16,16,16]{1,3,2,0:T(8,128)} %copy-done.6) | copy-start | bytes 196612 | tf_op jit(solution)/shard_map/while
  154.8 4.7 %copy-start.12 = (f32[4,16,16]{1,0,2:T(4,128)S(1)}, f32[4,16,16]{1,0,2:T(4,128)}, u32[]{:S(2)}) copy-start(f32[4,16,16]{1,0,2:T(4,128)} %copy-done.11) | copy-start | bytes 12292 | tf_op jit(solution)/shard_map/while
  159.5 6.3 %copy-start.11 = (f32[4,16,16]{1,0,2:T(4,128)}, f32[4,16,16]{1,0,2:T(4,128)S(1)}, u32[]{:S(2)}) copy-start(f32[4,16,16]{1,0,2:T(4,128)S(1)} %get-tuple-element.558) | copy-start | bytes 12292 | tf_op jit(solution)/shard_map/while
  159.5 8.5 %copy-start.1 = (f32[4,128,16,16]{1,3,2,0:T(8,128)}, f32[4,128,16,16]{1,3,2,0:T(8,128)S(1)}, u32[]{:S(2)}) copy-start(f32[4,128,16,16]{1,3,2,0:T(8,128)S(1)} %get-tuple-element.556) | copy-start | bytes 1572868 | tf_op jit(solution)/shard_map/while
  175.0 4.7 %copy-start.7 = (f32[4,16,16,16]{1,3,2,0:T(8,128)S(1)}, f32[4,16,16,16]{1,3,2,0:T(8,128)}, u32[]{:S(2)}) copy-start(f32[4,16,16,16]{1,3,2,0:T(8,128)} %copy-done.6) | copy-start | bytes 196612 | tf_op jit(solution)/shard_map/while
  175.0 4.7 %copy-start.12 = (f32[4,16,16]{1,0,2:T(4,128)S(1)}, f32[4,16,16]{1,0,2:T(4,128)}, u32[]{:S(2)}) copy-start(f32[4,16,16]{1,0,2:T(4,128)} %copy-done.11) | copy-start | bytes 12292 | tf_op jit(solution)/shard_map/while
  193.7 2.4 %copy-start.19 = (f32[128]{0:T(128)S(1)}, f32[128]{0:T(128)}, u32[]{:S(2)}) copy-start(f32[128]{0:T(128)} %iota_add_fusion) | copy-start | bytes 1540
  (26 other events, 37.6 us)
where the time goes:
time: 202 us; the launch traced here: 198 us
  local copies, waits for them, and re-layouts  74.6 us (37%)
  matrix products  34.7 us (17%)
  other arithmetic  30.1 us (15%)
  blocking collectives  27.1 us (13%)
  starting transfers between devices  21.4 us (11%)
  waiting for transfers between devices  8.47 us (4%)
    all_gather x2, blocking collectives, entering_2(): everything = jax.tree.map(lambda part: lax.all_gather(part, axis), array)  27.1 us
    broadcast_in_dim x16, local copies, waits for them, and re-layouts, apply_groups(): masked = jnp.where(doc_masks[:, None], matrix_part[None], nothing)  13.6 us
    another operation x10, local copies, waits for them, and re-layouts, toeplitz_taps(): tiled = jnp.tile(line, (1, block_len))[:, :2 * block_len * block_len]  12.8 us
    dot_general x4, matrix products, advance(): jnp.einsum('gtn,ngc->tgc', jnp.where(continues[None, :, None], carry_weig...  10.4 us
    dot_general x4, matrix products, modal_blocks(): jnp.einsum('gn,gnk->gk', scaled, powers[:, :, :block_len], precision=high...  7.58 us
    unnamed x39, local copies, waits for them, and re-layouts  7.18 us
    while x60, local copies, waits for them, and re-layouts  7.03 us
    dot_general x4, matrix products, advance(): jnp.einsum('gts,sgc->tgc', jnp.where(same_doc[None], toeplitz, 0.0), bloc...  6.87 us
  transfers between devices with their start and end apart: 5, of which 2 were waited for; matrix products, arithmetic and copies ran while one was open for 9% of the time, Pallas kernels for 0%

commit v1 on v0

v1 whole, which is shorter than its diff:
```python
import functools

import jax
import jax.numpy as jnp
from jax import lax
from jax.experimental import pallas as pl
from jax.experimental.pallas import tpu as pltpu
from jax.sharding import PartitionSpec as P

GROUP_CH = 16
LANES = 128
VMEM_BYTES = 32 * 1024 * 1024


def iota(shape, dim):
    return lax.broadcasted_iota(jnp.int32, shape, dim)


def dot(a, b, contract=((1,), (0,))):
    return lax.dot_general(a, b, (contract, ((), ())), preferred_element_type=jnp.float32)


def prepare_kernel(key_ref, value_ref, rate_ref, residue_ref, product_ref, modal_ref):
    product_ref[...] = (
        key_ref[...].astype(jnp.float32) * value_ref[...].astype(jnp.float32)
    ).astype(jnp.bfloat16)
    rate = rate_ref[...].astype(jnp.float32)
    residue = residue_ref[...].astype(jnp.float32)
    gap = jnp.zeros((8 - rate.shape[0], rate.shape[1]), jnp.float32)
    modal_ref[...] = jnp.concatenate([rate, gap, residue, gap], axis=0).astype(jnp.bfloat16)


def build_kernel(
    dp_size,
    ctx_size,
    place_ref,
    taps_ref,
    other_taps_ref,
    modal_ref,
    *rest,
):
    modal_parts = rest[: dp_size - 1]
    starts_ref, medium_ref, long_ref, end_ref, carry_ref, through_ref, before_ref, rows_ref = rest[
        dp_size - 1 :
    ]
    fsdp_place, ctx_place, dp_place = place_ref[0], place_ref[1], place_ref[2]
    groups, block = medium_ref.shape[0], medium_ref.shape[1]
    width = through_ref.shape[1]
    modes = width // groups
    half = taps_ref.shape[0]

    own = starts_ref[:, pl.ds(pl.multiple_of(ctx_place * block, block), block)].astype(jnp.float32)
    prior_place = jnp.maximum(ctx_place - 1, 0)
    prior = starts_ref[:, pl.ds(pl.multiple_of(prior_place * block, block), block)].astype(
        jnp.float32
    )
    row, col = iota((block, block), 0), iota((block, block), 1)
    doc_col = jnp.sum(
        jnp.where(col <= row, jnp.broadcast_to(own, (block, block)), 0.0), axis=1, keepdims=True
    )
    both = jnp.concatenate(
        [jnp.broadcast_to(own, (8, block)), jnp.broadcast_to(prior, (8, block))], axis=0
    ).astype(jnp.bfloat16)
    doc_row = dot(both, (row <= col).astype(jnp.bfloat16))[0:1]
    after_row = dot(both, (row > col).astype(jnp.bfloat16))[8:9]
    total = jnp.sum(own, axis=1, keepdims=True)
    prior_total = jnp.sum(prior, axis=1, keepdims=True)
    current_mask = (row >= col) & (doc_col == doc_row)
    previous_mask = (col > row) & (doc_col == 0.0) & (after_row == 0.0) & (ctx_place > 0)
    continues = doc_col == 0.0
    keeps = doc_col == total

    pieces = jnp.concatenate([modal_ref[...]] + [part[...] for part in modal_parts], axis=0)
    per_part = modes // dp_size
    lines = pieces.shape[0]
    line, mode = iota((2 * modes, lines), 1), iota((2 * modes, lines), 0)
    within = line % 16
    held = jnp.where(mode < modes, within, within - 8)
    owner = jnp.bitwise_xor(dp_place, line // 16)
    wanted = owner * per_part + held == jnp.where(mode < modes, mode, mode - modes)
    select = ((held >= 0) & (held < per_part) & wanted).astype(jnp.bfloat16)
    ordered = dot(select, pieces).astype(jnp.bfloat16)
    spread = (
        iota((pieces.shape[1], width), 0)
        == dp_place * groups + iota((pieces.shape[1], width), 1) // modes
    ).astype(jnp.bfloat16)
    by_channel = dot(ordered, spread)
    rate = by_channel[:modes]
    scaled = by_channel[modes:] * jnp.sqrt((1.0 - jnp.exp(-2.0 * rate)) / modes)
    through = jnp.exp(-rate * block)
    through_ref[...] = through * (total == 0.0).astype(jnp.float32)
    before_ref[...] = jnp.where(
        ctx_place == ctx_size - 1, through * (prior_total == 0.0).astype(jnp.float32), 1.0
    )
    on_line = iota((modes, width), 0) == iota((modes, width), 1) % modes
    rate_line = jnp.sum(jnp.where(on_line, rate, 0.0), axis=0, keepdims=True)
    scaled_line = jnp.sum(jnp.where(on_line, scaled, 0.0), axis=0, keepdims=True)

    token = iota((block, width), 0).astype(jnp.float32)
    carry_ref[...] = jnp.where(
        continues, scaled_line * jnp.exp(-rate_line * (token + 1.0)), 0.0
    ).astype(jnp.bfloat16)
    end_weight = jnp.where(keeps, jnp.exp(-rate_line * (block - 1.0 - token)), 0.0)
    for slab in range(width // LANES):
        lanes = slice(slab * LANES, (slab + 1) * LANES)
        end_ref[lanes, :] = jnp.transpose(end_weight[:, lanes]).astype(jnp.bfloat16)

    lag = ((block - iota((block, width), 0)) % block).astype(jnp.float32)
    response = scaled_line * jnp.exp(-rate_line * lag)
    high = response.astype(jnp.bfloat16)
    low = (response - high.astype(jnp.float32)).astype(jnp.bfloat16)
    member = (iota((groups, width), 0) == iota((groups, width), 1) // modes).astype(jnp.bfloat16)
    rows_ref[groups:, :] = dot(member, high, ((1,), (1,))) + dot(member, low, ((1,), (1,)))
    first = fsdp_place * dp_size * groups + dp_place * groups
    tap, lane = iota((half, block), 0), iota((half, block), 1)
    lag_of_lane = (block - lane) % block
    own_place = (tap + fsdp_place * half == lag_of_lane).astype(jnp.bfloat16)
    other_place = (tap + (1 - fsdp_place) * half == lag_of_lane).astype(jnp.bfloat16)
    own_rows = (
        iota((taps_ref.shape[1], groups), 0) == first + iota((taps_ref.shape[1], groups), 1)
    ).astype(jnp.bfloat16)
    own_taps = dot(taps_ref[...], own_rows).astype(jnp.bfloat16)
    other_taps = dot(other_taps_ref[...], own_rows).astype(jnp.bfloat16)
    rows_ref[:groups, :] = dot(own_taps, own_place, ((0,), (0,))) + dot(
        other_taps, other_place, ((0,), (0,))
    )

    def lay(group, _):
        medium_row = rows_ref[pl.ds(group, 1), :]
        turned = pltpu.roll(
            jnp.broadcast_to(medium_row, (block, block)), 0, 1, stride=1, stride_axis=0
        )
        medium_ref[group, :, :block] = jnp.where(previous_mask, turned, 0.0).astype(jnp.bfloat16)
        medium_ref[group, :, block:] = jnp.where(current_mask, turned, 0.0).astype(jnp.bfloat16)
        long_row = rows_ref[pl.ds(groups + group, 1), :]
        turned = pltpu.roll(
            jnp.broadcast_to(long_row, (block, block)), 0, 1, stride=1, stride_axis=0
        )
        long_ref[group] = jnp.where(current_mask, turned, 0.0).astype(jnp.bfloat16)
        return 0

    lax.fori_loop(0, groups, lay, 0, unroll=4)


def grouped(matrices, values):
    count, out, rows = matrices.shape
    product = dot(matrices.reshape(count * out, rows), values)
    lane = iota((out, LANES), 1) // GROUP_CH
    result = product[:out]
    for k in range(1, count):
        result = jnp.where(lane == k, product[k * out : (k + 1) * out], result)
    return result


def gate_kernel(halo_ref, product_ref, query_ref, medium_ref, end_ref, gated_ref, state_ref):
    width = product_ref.shape[1]
    modes = state_ref.shape[0]
    per_slab = LANES // GROUP_CH
    diagonal = iota((LANES, LANES), 0) // modes == iota((LANES, LANES), 1) // GROUP_CH
    for slab in range(width // LANES):
        lanes = slice(slab * LANES, (slab + 1) * LANES)
        window = jnp.concatenate([halo_ref[:, lanes], product_ref[:, lanes]], axis=0)
        medium = grouped(medium_ref[slab * per_slab : (slab + 1) * per_slab], window)
        gated = (
            query_ref[:, lanes].astype(jnp.float32)
            * medium.astype(jnp.bfloat16).astype(jnp.float32)
        ).astype(jnp.bfloat16)
        gated_ref[:, lanes] = gated
        spread = jnp.where(diagonal, dot(end_ref[lanes, :], gated), 0.0)
        state_ref[:, lanes] = jnp.sum(spread.reshape(per_slab, modes, LANES), axis=0).astype(
            state_ref.dtype
        )


def local_kernel(gated_ref, long_ref, gain_ref, part_ref):
    width = gated_ref.shape[1]
    per_slab = LANES // GROUP_CH
    for slab in range(width // LANES):
        lanes = slice(slab * LANES, (slab + 1) * LANES)
        gated = gated_ref[:, lanes]
        part_ref[:, lanes] = grouped(
            long_ref[slab * per_slab : (slab + 1) * per_slab], gated
        ) + gain_ref[:, lanes] * gated.astype(jnp.float32)


def finish_kernel(part_ref, carry_ref, near_ref, far_ref, before_ref, out_ref):
    width = part_ref.shape[1]
    modes = near_ref.shape[0]
    per_slab = LANES // GROUP_CH
    diagonal = iota((LANES, LANES), 0) // modes == iota((LANES, LANES), 1) // GROUP_CH
    entering = near_ref[...].astype(jnp.float32) + before_ref[...] * far_ref[...].astype(
        jnp.float32
    )
    for slab in range(width // LANES):
        lanes = slice(slab * LANES, (slab + 1) * LANES)
        state = jnp.concatenate([entering[:, lanes]] * per_slab, axis=0)
        spread = jnp.where(diagonal, state, 0.0).astype(jnp.bfloat16)
        out_ref[:, lanes] = (part_ref[:, lanes] + dot(carry_ref[:, lanes], spread)).astype(
            out_ref.dtype
        )


def call(kernel, outs, *args, scalars=0, scratch=()):
    specs = [pl.BlockSpec(memory_space=pltpu.SMEM)] * scalars + [
        pl.BlockSpec(memory_space=pltpu.VMEM)
    ] * (len(args) - scalars)
    return pl.pallas_call(
        kernel,
        out_shape=[jax.ShapeDtypeStruct(shape, dtype) for shape, dtype in outs],
        in_specs=specs,
        out_specs=[pl.BlockSpec(memory_space=pltpu.VMEM)] * len(outs),
        scratch_shapes=list(scratch),
        compiler_params=pltpu.CompilerParams(vmem_limit_bytes=VMEM_BYTES),
    )(*args)


def shifted(array, axis, distance):
    size = lax.axis_size(axis)
    return lax.ppermute(array, axis, [(i, i + distance) for i in range(size - distance)])


def entering_states(state, through, before):
    size = lax.axis_size("ctx")
    if size == 4:
        near = lax.ppermute(state, "ctx", [(0, 1), (2, 3)])
        both = (state.astype(jnp.float32) + through * near.astype(jnp.float32)).astype(state.dtype)
        far = lax.ppermute(both, "ctx", [(1, 2)]) + lax.ppermute(both, "ctx", [(1, 3)])
        return near, far
    total, factor, distance = state.astype(jnp.float32), through, 1
    while distance < size:
        total = total + factor * shifted(total, "ctx", distance)
        factor = factor * shifted(factor, "ctx", distance)
        distance *= 2
    near = shifted(total, "ctx", 1)
    return near, jnp.zeros_like(near)


def body(
    query_stream,
    key_stream,
    value_stream,
    document_starts,
    medium_taps,
    modal_rate,
    modal_residue,
    skip_gain,
):
    tokens, width = query_stream.shape[1:]
    groups = width // GROUP_CH
    fsdp_size, dp_size = lax.axis_size("fsdp"), lax.axis_size("dp")
    ctx_size = lax.axis_size("ctx")
    modes = modal_rate.shape[1] * dp_size
    assert fsdp_size == 2 and tokens == medium_taps.shape[1] * fsdp_size
    assert modes == GROUP_CH and modal_rate.shape[1] <= 8
    place = jnp.stack([lax.axis_index("fsdp"), lax.axis_index("ctx"), lax.axis_index("dp")])
    taps = medium_taps.T
    half = jnp.bfloat16
    product, modal = call(
        prepare_kernel,
        [((tokens, width), half), ((16, modal_rate.shape[0]), half)],
        key_stream[0],
        value_stream[0],
        modal_rate.T,
        modal_residue.T,
    )
    halo = shifted(product, "ctx", 1)
    other_taps = lax.ppermute(taps, "fsdp", [(0, 1), (1, 0)])
    modal_parts = [
        lax.ppermute(modal, "dp", [(i, i ^ k) for i in range(dp_size)]) for k in range(1, dp_size)
    ]
    medium, long, end, carry, through, before = call(
        functools.partial(build_kernel, dp_size, ctx_size),
        [
            ((groups, tokens, 2 * tokens), half),
            ((groups, tokens, tokens), half),
            ((width, tokens), half),
            ((tokens, width), half),
            ((modes, width), jnp.float32),
            ((modes, width), jnp.float32),
        ],
        place,
        taps,
        other_taps,
        modal,
        *modal_parts,
        document_starts,
        scalars=1,
        scratch=[pltpu.VMEM((2 * groups, tokens), jnp.float32)],
    )
    gated, state = call(
        gate_kernel,
        [((tokens, width), half), ((modes, width), half)],
        halo,
        product,
        query_stream[0],
        medium,
        end,
    )
    near, far = entering_states(state, through, before)
    (part,) = call(
        local_kernel, [((tokens, width), jnp.float32)], gated, long, skip_gain.reshape(1, width)
    )
    (out,) = call(finish_kernel, [((tokens, width), half)], part, carry, near, far, before)
    return out[None]


def solution(mesh):
    return jax.shard_map(
        body,
        mesh=mesh,
        in_specs=(
            P(None, "ctx", ("fsdp", "dp")),
            P(None, "ctx", ("fsdp", "dp")),
            P(None, "ctx", ("fsdp", "dp")),
            P(),
            P(None, "fsdp"),
            P("fsdp", "dp"),
            P("fsdp", "dp"),
            P(("fsdp", "dp")),
        ),
        out_specs=P(None, "ctx", ("fsdp", "dp")),
        check_vma=False,
    )
```

time: 202 us -> 36.1 us (0.18)
  the two profiles are of different devices: /device:TPU:8 before, /device:TPU:16 now
where the time goes in v1:
time: 36.1 us; the launch traced here: 35.7 us
  waiting for transfers between devices  10.8 us (30%)
  starting transfers between devices  10.3 us (29%)
  Pallas kernels  8.69 us (24%)
  local copies, waits for them, and re-layouts  5.75 us (16%)
    pallas_call x5, Pallas kernels, call(): pl.pallas_call(kernel, out_shape=[jax.ShapeDtypeStruct(shape, dtype) for...  8.69 us
    ppermute x1, waiting for transfers between devices, entering_states(): lax.ppermute(both, 'ctx', [(1, 2)]) + lax.ppermute(both, 'ctx', [(1, 3)])  6.16 us
    unnamed x16, local copies, waits for them, and re-layouts  5.75 us
    ppermute x3, starting transfers between devices, body(): lax.ppermute(modal, 'dp', [(i, i ^ k) for i in range(dp_size)])  3.55 us
    ppermute x1, starting transfers between devices, shifted(): lax.ppermute(array, axis, [(i, i + distance) for i in range(size - distan...  3.48 us
    ppermute x3, waiting for transfers between devices, body(): lax.ppermute(modal, 'dp', [(i, i ^ k) for i in range(dp_size)])  3.04 us
    ppermute x1, waiting for transfers between devices, entering_states(): near = lax.ppermute(state, 'ctx', [(0, 1), (2, 3)])  1.58 us
    ppermute x1, starting transfers between devices, entering_states(): lax.ppermute(both, 'ctx', [(1, 2)]) + lax.ppermute(both, 'ctx', [(1, 3)])  1.29 us
  transfers between devices with their start and end apart: 8, of which 5 were waited for; matrix products, arithmetic and copies ran while one was open for 0% of the time, Pallas kernels for 13%

profile of v1, /device:TPU:16, one launch (start us, length us, event | category | flops | bytes accessed | tf_op | source)
XLA Modules:
  0.0 35.7 jit_solution(6377375750501676603)
XLA Ops:
  0.0 1.0 %copy-done.1 = bf16[1,128,1024]{2,1,0:T(8,128)(2,1)S(1)} copy-done((bf16[1,128,1024]{2,1,0:T(8,128)(2,1)S(1)}, bf16[1,128,1024]{2,1,0:T(8,128)(2,1)}, u32[]{:S(2)}) %copy-start.1) | copy-done | bytes 262168
  1.0 0.9 %copy-done.2 = bf16[1,128,1024]{2,1,0:T(8,128)(2,1)S(1)} copy-done((bf16[1,128,1024]{2,1,0:T(8,128)(2,1)S(1)}, bf16[1,128,1024]{2,1,0:T(8,128)(2,1)}, u32[]{:S(2)}) %copy-start.2) | copy-done | bytes 262168
  1.9 0.7 %copy-done.5 = bf16[256,4]{0,1:T(4,128)(2,1)S(1)} copy-done((bf16[256,4]{0,1:T(4,128)(2,1)S(1)}, bf16[256,4]{0,1:T(4,128)(2,1)}, u32[]{:S(2)}) %copy-start.5) | copy-done | bytes 2072
  2.6 0.7 %copy-done.6 = bf16[256,4]{0,1:T(4,128)(2,1)S(1)} copy-done((bf16[256,4]{0,1:T(4,128)(2,1)S(1)}, bf16[256,4]{0,1:T(4,128)(2,1)}, u32[]{:S(2)}) %copy-start.6) | copy-done | bytes 2072
  3.3 3.5 %collective-permute-start = (bf16[128,1024]{1,0:T(8,128)(2,1)S(1)}, bf16[128,1024]{1,0:T(8,128)(2,1)S(1)}, u32[]{:S(2)}, u32[]{:S(2)}) collective-permute-start(bf16[128,1024]{1,0:T(8,128)(2,1)S(1)} %get-tuple-element.15.product_ref), channel_id=1, source_target_pairs={{0,4},{4,8},{8,12},{1,5},{5,9},{9,13},{2,6},{6,10},{10,14},{3,7},{... | collective-permute-start | bytes 786440 | tf_op jit(solution)/shard_map/ppermute | solution.py:219
  6.8 2.5 %collective-permute-start.4 = (bf16[16,256]{1,0:T(8,128)(2,1)S(1)}, bf16[16,256]{1,0:T(8,128)(2,1)S(1)}, u32[]{:S(2)}, u32[]{:S(2)}) collective-permute-start(bf16[16,256]{1,0:T(8,128)(2,1)S(1)} %get-tuple-element.16.modal_ref), channel_id=1, source_target_pairs={{0,3},{1,2},{2,1},{3,0},{4,7},{5,6},{6,5},{7,4},{8,11},{9,10},{10,... | collective-permute-start | bytes 24584 | tf_op jit(solution)/shard_map/ppermute | solution.py:269
  9.4 0.5 %collective-permute-start.3 = (bf16[16,256]{1,0:T(8,128)(2,1)S(1)}, bf16[16,256]{1,0:T(8,128)(2,1)S(1)}, u32[]{:S(2)}, u32[]{:S(2)}) collective-permute-start(bf16[16,256]{1,0:T(8,128)(2,1)S(1)} %get-tuple-element.16.modal_ref), channel_id=1, source_target_pairs={{0,2},{1,3},{2,0},{3,1},{4,6},{5,7},{6,4},{7,5},{8,10},{9,11},{10,... | collective-permute-start | bytes 24584 | tf_op jit(solution)/shard_map/ppermute | solution.py:269
  9.9 0.5 %collective-permute-start.2 = (bf16[16,256]{1,0:T(8,128)(2,1)S(1)}, bf16[16,256]{1,0:T(8,128)(2,1)S(1)}, u32[]{:S(2)}, u32[]{:S(2)}) collective-permute-start(bf16[16,256]{1,0:T(8,128)(2,1)S(1)} %get-tuple-element.16.modal_ref), channel_id=1, source_target_pairs={{0,1},{1,0},{2,3},{3,2},{4,5},{5,4},{6,7},{7,6},{8,9},{9,8},{10,11... | collective-permute-start | bytes 24584 | tf_op jit(solution)/shard_map/ppermute | solution.py:269
  10.4 0.1 pad_add_fusion.place_ref
  10.5 1.0 %collective-permute-done.4.rest_2_ = bf16[16,256]{1,0:T(8,128)(2,1)S(1)} collective-permute-done((bf16[16,256]{1,0:T(8,128)(2,1)S(1)}, bf16[16,256]{1,0:T(8,128)(2,1)S(1)}, u32[]{:S(2)}, u32[]{:S(2)}) %collective-permute-start.4) | collective-permute-done | bytes 8224 | tf_op jit(solution)/shard_map/ppermute | solution.py:269
  11.5 1.5 %collective-permute-done.3.rest_1_ = bf16[16,256]{1,0:T(8,128)(2,1)S(1)} collective-permute-done((bf16[16,256]{1,0:T(8,128)(2,1)S(1)}, bf16[16,256]{1,0:T(8,128)(2,1)S(1)}, u32[]{:S(2)}, u32[]{:S(2)}) %collective-permute-start.3) | collective-permute-done | bytes 8224 | tf_op jit(solution)/shard_map/ppermute | solution.py:269
  13.0 0.5 %collective-permute-done.2.rest_0_ = bf16[16,256]{1,0:T(8,128)(2,1)S(1)} collective-permute-done((bf16[16,256]{1,0:T(8,128)(2,1)S(1)}, bf16[16,256]{1,0:T(8,128)(2,1)S(1)}, u32[]{:S(2)}, u32[]{:S(2)}) %collective-permute-start.2) | collective-permute-done | bytes 8224 | tf_op jit(solution)/shard_map/ppermute | solution.py:269
  13.5 0.8 %copy-done.3 = bf16[512,64]{0,1:T(8,128)(2,1)S(1)} copy-done((bf16[512,64]{0,1:T(8,128)(2,1)S(1)}, bf16[512,64]{0,1:T(8,128)(2,1)}, u32[]{:S(2)}) %copy-start.3) | copy-done | bytes 65560
  14.4 0.7 %copy-done.7 = s32[1,512]{1,0:T(1,128)S(1)} copy-done((s32[1,512]{1,0:T(1,128)S(1)}, s32[1,512]{1,0:T(1,128)}, u32[]{:S(2)}) %copy-start.7) | copy-done | bytes 2072
  15.0 3.9 %shard_map.83 = (bf16[64,128,256]{2,1,0:T(8,128)(2,1)S(1)}, bf16[64,128,128]{2,1,0:T(8,128)(2,1)S(1)}, bf16[1024,128]{1,0:T(8,128)(2,1)S(1)}, bf16[128,1024]{1,0...) custom-call(s32[3]{0:T(128)S(1)} %pad_add_fusion.place_ref, bf16[64,512]{1,0:T(8,128)(2,1)S(1)} %bitcast.15, ...), custom_call_target="tpu_custom_call" | custom-call | tf_op jit(solution)/shard_map/pallas_call | solution.py:207
  19.0 0.9 %copy-done = bf16[1,128,1024]{2,1,0:T(8,128)(2,1)S(1)} copy-done((bf16[1,128,1024]{2,1,0:T(8,128)(2,1)S(1)}, bf16[1,128,1024]{2,1,0:T(8,128)(2,1)}, u32[]{:S(2)}) %copy-start) | copy-done | bytes 262168
  19.9 3.1 %shard_map.84 = (bf16[128,1024]{1,0:T(8,128)(2,1)S(1)}, bf16[16,1024]{1,0:T(8,128)(2,1)S(1)}) custom-call(bf16[128,1024]{1,0:T(8,128)(2,1)S(1)} %collective-permute-done.halo_ref, bf16[128,1024]{1,0:T(8,128)(2,1)S(1)} %get-tuple-element.15.product_ref, bf16[128,1024]{1,0:T(8,128)(2,1)S(1)} %bitcast.11, ...), custom_call_target="tpu_custom_call" | custom-call | tf_op jit(solution)/shard_map/pallas_call | solution.py:207
  23.0 1.3 %collective-permute-start.5 = (bf16[16,1024]{1,0:T(8,128)(2,1)S(1)}, bf16[16,1024]{1,0:T(8,128)(2,1)S(1)}, u32[]{:S(2)}, u32[]{:S(2)}) collective-permute-start(bf16[16,1024]{1,0:T(8,128)(2,1)S(1)} %get-tuple-element.22), channel_id=1, source_target_pairs={{0,4},{8,12},{1,5},{9,13},{2,6},{10,14},{3,7},{11,15},{16,20},{24,... | collective-permute-start | bytes 98312 | tf_op jit(solution)/shard_map/ppermute | solution.py:225
  24.3 1.6 %collective-permute-done.5.near_ref = bf16[16,1024]{1,0:T(8,128)(2,1)S(1)} collective-permute-done((bf16[16,1024]{1,0:T(8,128)(2,1)S(1)}, bf16[16,1024]{1,0:T(8,128)(2,1)S(1)}, u32[]{:S(2)}, u32[]{:S(2)}) %collective-permute-start.5) | collective-permute-done | bytes 32800 | tf_op jit(solution)/shard_map/ppermute | solution.py:225
  25.9 0.7 %collective-permute-start.7 = (bf16[16,1024]{1,0:T(8,128)(2,1)S(1)}, bf16[16,1024]{1,0:T(8,128)(2,1)S(1)}, u32[]{:S(2)}, u32[]{:S(2)}) collective-permute-start(bf16[16,1024]{1,0:T(8,128)(2,1)S(1)} %add_convert_fusion), channel_id=1, source_target_pairs={{4,12},{5,13},{6,14},{7,15},{20,28},{21,29},{22,30},{23,31}} | collective-permute-start | bytes 98312 | tf_op jit(solution)/shard_map/ppermute | solution.py:227
  26.6 1.3 %collective-permute-start.6 = (bf16[16,1024]{1,0:T(8,128)(2,1)S(1)}, bf16[16,1024]{1,0:T(8,128)(2,1)S(1)}, u32[]{:S(2)}, u32[]{:S(2)}) collective-permute-start(bf16[16,1024]{1,0:T(8,128)(2,1)S(1)} %add_convert_fusion), channel_id=1, source_target_pairs={{4,8},{5,9},{6,10},{7,11},{20,24},{21,25},{22,26},{23,27}} | collective-permute-start | bytes 98312 | tf_op jit(solution)/shard_map/ppermute | solution.py:227
  27.9 0.7 %shard_map.85.part_ref = f32[128,1024]{1,0:T(8,128)S(1)} custom-call(bf16[128,1024]{1,0:T(8,128)(2,1)S(1)} %get-tuple-element.19.gated_ref, bf16[64,128,128]{2,1,0:T(8,128)(2,1)S(1)} %get-tuple-element.20.long_ref, f32[1,1024]{1,0:T(1,128)S(1)} %bitcast.16), custom_call_target="tpu_custom_call" | custom-call | tf_op jit(solution)/shard_map/pallas_call | solution.py:207
  28.6 6.2 %collective-permute-done.6 = bf16[16,1024]{1,0:T(8,128)(2,1)S(1)} collective-permute-done((bf16[16,1024]{1,0:T(8,128)(2,1)S(1)}, bf16[16,1024]{1,0:T(8,128)(2,1)S(1)}, u32[]{:S(2)}, u32[]{:S(2)}) %collective-permute-start.6) | collective-permute-done | bytes 32800 | tf_op jit(solution)/shard_map/ppermute | solution.py:227
  34.8 0.9 %shard_map.86 = bf16[128,1024]{1,0:T(8,128)(2,1)} custom-call(f32[128,1024]{1,0:T(8,128)S(1)} %shard_map.85.part_ref, bf16[128,1024]{1,0:T(8,128)(2,1)S(1)} %get-tuple-element.21.carry_ref, bf16[16,1024]{1,0:T(8,128)(2,1)S(1)} %collective-permute-done.5.near_ref, bf16[16,1024]{1,0:T(8,128)(2,1)S(1)} %add.7.far_ref, f32[16,1024]{1,0:T(8,128)S(1)} %get-tuple-element.24.before_ref), custom_call_target="tpu_custom_call" | custom-call | tf_op jit(solution)/shard_map/pallas_call | solution.py:207
  (16 shorter events, 0.1 us)
Async XLA Ops:
  0.0 27.9 %copy-start.4 = (f32[1024]{0:T(1024)S(1)}, f32[1024]{0:T(1024)}, u32[]{:S(2)}) copy-start(f32[1024]{0:T(1024)} %param.15) | copy-start | bytes 12292
  0.0 1.0 %copy-start.1 = (bf16[1,128,1024]{2,1,0:T(8,128)(2,1)S(1)}, bf16[1,128,1024]{2,1,0:T(8,128)(2,1)}, u32[]{:S(2)}) copy-start(bf16[1,128,1024]{2,1,0:T(8,128)(2,1)} %param.9) | copy-start | bytes 786436
  1.0 0.9 %copy-start.2 = (bf16[1,128,1024]{2,1,0:T(8,128)(2,1)S(1)}, bf16[1,128,1024]{2,1,0:T(8,128)(2,1)}, u32[]{:S(2)}) copy-start(bf16[1,128,1024]{2,1,0:T(8,128)(2,1)} %param.10) | copy-start | bytes 786436
  1.9 0.7 %copy-start.5 = (bf16[256,4]{0,1:T(4,128)(2,1)S(1)}, bf16[256,4]{0,1:T(4,128)(2,1)}, u32[]{:S(2)}) copy-start(bf16[256,4]{0,1:T(4,128)(2,1)} %param.13) | copy-start | bytes 6148
  2.6 0.7 %copy-start.6 = (bf16[256,4]{0,1:T(4,128)(2,1)S(1)}, bf16[256,4]{0,1:T(4,128)(2,1)}, u32[]{:S(2)}) copy-start(bf16[256,4]{0,1:T(4,128)(2,1)} %param.14) | copy-start | bytes 6148
  3.3 15.6 %collective-permute-start = (bf16[128,1024]{1,0:T(8,128)(2,1)S(1)}, bf16[128,1024]{1,0:T(8,128)(2,1)S(1)}, u32[]{:S(2)}, u32[]{:S(2)}) collective-permute-start(bf16[128,1024]{1,0:T(8,128)(2,1)S(1)} %get-tuple-element.15.product_ref), channel_id=1, source_target_pairs={{0,4},{4,8},{8,12},{1,5},{5,9},{9,13},{2,6},{6,10},{10,14},{3,7},{... | collective-permute-start | bytes 786440 | tf_op jit(solution)/shard_map/ppermute | solution.py:219
  6.8 4.6 %collective-permute-start.4 = (bf16[16,256]{1,0:T(8,128)(2,1)S(1)}, bf16[16,256]{1,0:T(8,128)(2,1)S(1)}, u32[]{:S(2)}, u32[]{:S(2)}) collective-permute-start(bf16[16,256]{1,0:T(8,128)(2,1)S(1)} %get-tuple-element.16.modal_ref), channel_id=1, source_target_pairs={{0,3},{1,2},{2,1},{3,0},{4,7},{5,6},{6,5},{7,4},{8,11},{9,10},{10,... | collective-permute-start | bytes 24584 | tf_op jit(solution)/shard_map/ppermute | solution.py:269
  9.4 3.7 %collective-permute-start.3 = (bf16[16,256]{1,0:T(8,128)(2,1)S(1)}, bf16[16,256]{1,0:T(8,128)(2,1)S(1)}, u32[]{:S(2)}, u32[]{:S(2)}) collective-permute-start(bf16[16,256]{1,0:T(8,128)(2,1)S(1)} %get-tuple-element.16.modal_ref), channel_id=1, source_target_pairs={{0,2},{1,3},{2,0},{3,1},{4,6},{5,7},{6,4},{7,5},{8,10},{9,11},{10,... | collective-permute-start | bytes 24584 | tf_op jit(solution)/shard_map/ppermute | solution.py:269
  9.9 3.7 %collective-permute-start.2 = (bf16[16,256]{1,0:T(8,128)(2,1)S(1)}, bf16[16,256]{1,0:T(8,128)(2,1)S(1)}, u32[]{:S(2)}, u32[]{:S(2)}) collective-permute-start(bf16[16,256]{1,0:T(8,128)(2,1)S(1)} %get-tuple-element.16.modal_ref), channel_id=1, source_target_pairs={{0,1},{1,0},{2,3},{3,2},{4,5},{5,4},{6,7},{7,6},{8,9},{9,8},{10,11... | collective-permute-start | bytes 24584 | tf_op jit(solution)/shard_map/ppermute | solution.py:269
  10.4 3.1 %collective-permute-start.1 = (bf16[64,512]{1,0:T(8,128)(2,1)}, bf16[64,512]{1,0:T(8,128)(2,1)S(1)}, u32[]{:S(2)}, u32[]{:S(2)}) collective-permute-start(bf16[64,512]{1,0:T(8,128)(2,1)} %bitcast.14), channel_id=1, source_target_pairs={{0,16},{16,0},{1,17},{17,1},{2,18},{18,2},{3,19},{19,3},{4,20},{20... | collective-permute-start | bytes 196616 | tf_op jit(solution)/shard_map/ppermute | solution.py:267
  13.5 0.8 %copy-start.3 = (bf16[512,64]{0,1:T(8,128)(2,1)S(1)}, bf16[512,64]{0,1:T(8,128)(2,1)}, u32[]{:S(2)}) copy-start(bf16[512,64]{0,1:T(8,128)(2,1)} %param.12) | copy-start | bytes 196612
  14.4 0.7 %copy-start.7 = (s32[1,512]{1,0:T(1,128)S(1)}, s32[1,512]{1,0:T(1,128)}, u32[]{:S(2)}) copy-start(s32[1,512]{1,0:T(1,128)} %rest_3_.1) | copy-start | bytes 6148
  18.9 1.0 %copy-start = (bf16[1,128,1024]{2,1,0:T(8,128)(2,1)S(1)}, bf16[1,128,1024]{2,1,0:T(8,128)(2,1)}, u32[]{:S(2)}) copy-start(bf16[1,128,1024]{2,1,0:T(8,128)(2,1)} %param.8) | copy-start | bytes 786436
  23.0 2.9 %collective-permute-start.5 = (bf16[16,1024]{1,0:T(8,128)(2,1)S(1)}, bf16[16,1024]{1,0:T(8,128)(2,1)S(1)}, u32[]{:S(2)}, u32[]{:S(2)}) collective-permute-start(bf16[16,1024]{1,0:T(8,128)(2,1)S(1)} %get-tuple-element.22), channel_id=1, source_target_pairs={{0,4},{8,12},{1,5},{9,13},{2,6},{10,14},{3,7},{11,15},{16,20},{24,... | collective-permute-start | bytes 98312 | tf_op jit(solution)/shard_map/ppermute | solution.py:225
  25.9 2.7 %collective-permute-start.7 = (bf16[16,1024]{1,0:T(8,128)(2,1)S(1)}, bf16[16,1024]{1,0:T(8,128)(2,1)S(1)}, u32[]{:S(2)}, u32[]{:S(2)}) collective-permute-start(bf16[16,1024]{1,0:T(8,128)(2,1)S(1)} %add_convert_fusion), channel_id=1, source_target_pairs={{4,12},{5,13},{6,14},{7,15},{20,28},{21,29},{22,30},{23,31}} | collective-permute-start | bytes 98312 | tf_op jit(solution)/shard_map/ppermute | solution.py:227
  26.6 8.2 %collective-permute-start.6 = (bf16[16,1024]{1,0:T(8,128)(2,1)S(1)}, bf16[16,1024]{1,0:T(8,128)(2,1)S(1)}, u32[]{:S(2)}, u32[]{:S(2)}) collective-permute-start(bf16[16,1024]{1,0:T(8,128)(2,1)S(1)} %add_convert_fusion), channel_id=1, source_target_pairs={{4,8},{5,9},{6,10},{7,11},{20,24},{21,25},{22,26},{23,27}} | collective-permute-start | bytes 98312 | tf_op jit(solution)/shard_map/ppermute | solution.py:227

commit v2 on v1

--- a/solution.py
+++ b/solution.py
@@ -20,7 +20,45 @@
     return lax.dot_general(a, b, (contract, ((), ())), preferred_element_type=jnp.float32)
 
 
-def prepare_kernel(key_ref, value_ref, rate_ref, residue_ref, product_ref, modal_ref):
+def prepare_kernel(
+    key_hbm,
+    value_hbm,
+    rate_hbm,
+    residue_hbm,
+    query_hbm,
+    taps_hbm,
+    starts_hbm,
+    gain_hbm,
+    product_ref,
+    modal_ref,
+    query_ref,
+    taps_ref,
+    starts_ref,
+    gain_ref,
+    key_ref,
+    value_ref,
+    rate_ref,
+    residue_ref,
+    arrived,
+):
+    pairs = (
+        (key_hbm, key_ref),
+        (value_hbm, value_ref),
+        (rate_hbm, rate_ref),
+        (residue_hbm, residue_ref),
+        (query_hbm, query_ref),
+        (taps_hbm, taps_ref),
+        (starts_hbm, starts_ref),
+        (gain_hbm, gain_ref),
+    )
+    copies = [
+        pltpu.make_async_copy(source, target, arrived.at[i])
+        for i, (source, target) in enumerate(pairs)
+    ]
+    for copy in copies:
+        copy.start()
+    for copy in copies[:4]:
+        copy.wait()
     product_ref[...] = (
         key_ref[...].astype(jnp.float32) * value_ref[...].astype(jnp.float32)
     ).astype(jnp.bfloat16)
@@ -28,32 +66,19 @@
     residue = residue_ref[...].astype(jnp.float32)
     gap = jnp.zeros((8 - rate.shape[0], rate.shape[1]), jnp.float32)
     modal_ref[...] = jnp.concatenate([rate, gap, residue, gap], axis=0).astype(jnp.bfloat16)
-
-
-def build_kernel(
-    dp_size,
-    ctx_size,
-    place_ref,
-    taps_ref,
-    other_taps_ref,
-    modal_ref,
-    *rest,
-):
-    modal_parts = rest[: dp_size - 1]
-    starts_ref, medium_ref, long_ref, end_ref, carry_ref, through_ref, before_ref, rows_ref = rest[
-        dp_size - 1 :
+    for copy in copies[4:]:
+        copy.wait()
+
+
+def block_starts(starts_ref, ctx_place, block):
+    prior_place = jnp.maximum(ctx_place - 1, 0)
+    return [
+        starts_ref[:, pl.ds(pl.multiple_of(place * block, block), block)].astype(jnp.float32)
+        for place in (ctx_place, prior_place)
     ]
-    fsdp_place, ctx_place, dp_place = place_ref[0], place_ref[1], place_ref[2]
-    groups, block = medium_ref.shape[0], medium_ref.shape[1]
-    width = through_ref.shape[1]
-    modes = width // groups
-    half = taps_ref.shape[0]
-
-    own = starts_ref[:, pl.ds(pl.multiple_of(ctx_place * block, block), block)].astype(jnp.float32)
-    prior_place = jnp.maximum(ctx_place - 1, 0)
-    prior = starts_ref[:, pl.ds(pl.multiple_of(prior_place * block, block), block)].astype(
-        jnp.float32
-    )
+
+
+def document_masks(own, prior, block):
     row, col = iota((block, block), 0), iota((block, block), 1)
     doc_col = jnp.sum(
         jnp.where(col <= row, jnp.broadcast_to(own, (block, block)), 0.0), axis=1, keepdims=True
@@ -63,10 +88,59 @@
     ).astype(jnp.bfloat16)
     doc_row = dot(both, (row <= col).astype(jnp.bfloat16))[0:1]
     after_row = dot(both, (row > col).astype(jnp.bfloat16))[8:9]
+    current = (row >= col) & (doc_col == doc_row)
+    previous = (col > row) & (doc_col == 0.0) & (after_row == 0.0)
+    return doc_col, current, previous
+
+
+def circulant(row, block):
+    return pltpu.roll(
+        jnp.broadcast_to(row, (block, block)), 0, 1, stride=1, stride_axis=0
+    ).astype(jnp.bfloat16)
+
+
+def medium_kernel(
+    dp_size, place_ref, taps_ref, other_taps_ref, starts_ref, medium_ref, rows_ref
+):
+    fsdp_place, ctx_place, dp_place = place_ref[0], place_ref[1], place_ref[2]
+    groups, block = medium_ref.shape[0], medium_ref.shape[1]
+    half = taps_ref.shape[0]
+    own, prior = block_starts(starts_ref, ctx_place, block)
+    _, current, previous = document_masks(own, prior, block)
+    current = current.astype(jnp.bfloat16)
+    previous = (previous & (ctx_place > 0)).astype(jnp.bfloat16)
+    first = fsdp_place * dp_size * groups + dp_place * groups
+    tap, lane = iota((half, block), 0), iota((half, block), 1)
+    lag_of_lane = (block - lane) % block
+    own_place = (tap + fsdp_place * half == lag_of_lane).astype(jnp.bfloat16)
+    other_place = (tap + (1 - fsdp_place) * half == lag_of_lane).astype(jnp.bfloat16)
+    own_rows = (
+        iota((taps_ref.shape[1], groups), 0) == first + iota((taps_ref.shape[1], groups), 1)
+    ).astype(jnp.bfloat16)
+    own_taps = dot(taps_ref[...], own_rows).astype(jnp.bfloat16)
+    other_taps = dot(other_taps_ref[...], own_rows).astype(jnp.bfloat16)
+    rows_ref[...] = dot(own_taps, own_place, ((0,), (0,))) + dot(
+        other_taps, other_place, ((0,), (0,))
+    )
+    for group in range(groups):
+        turned = circulant(rows_ref[group : group + 1, :], block)
+        medium_ref[group, :, :block] = turned * previous
+        medium_ref[group, :, block:] = turned * current
+
+
+def modal_kernel(dp_size, ctx_size, place_ref, modal_ref, *rest):
+    modal_parts = rest[: dp_size - 1]
+    starts_ref, long_ref, end_ref, carry_ref, *factor_refs, rows_ref = rest[dp_size - 1 :]
+    through_ref, before_ref = factor_refs
+    ctx_place, dp_place = place_ref[1], place_ref[2]
+    groups, block = long_ref.shape[0], long_ref.shape[1]
+    width = through_ref.shape[1]
+    modes = width // groups
+    own, prior = block_starts(starts_ref, ctx_place, block)
+    doc_col, current, _ = document_masks(own, prior, block)
+    current = current.astype(jnp.bfloat16)
     total = jnp.sum(own, axis=1, keepdims=True)
     prior_total = jnp.sum(prior, axis=1, keepdims=True)
-    current_mask = (row >= col) & (doc_col == doc_row)
-    previous_mask = (col > row) & (doc_col == 0.0) & (after_row == 0.0) & (ctx_place > 0)
     continues = doc_col == 0.0
     keeps = doc_col == total
 
@@ -100,46 +174,18 @@
     carry_ref[...] = jnp.where(
         continues, scaled_line * jnp.exp(-rate_line * (token + 1.0)), 0.0
     ).astype(jnp.bfloat16)
-    end_weight = jnp.where(keeps, jnp.exp(-rate_line * (block - 1.0 - token)), 0.0)
-    for slab in range(width // LANES):
-        lanes = slice(slab * LANES, (slab + 1) * LANES)
-        end_ref[lanes, :] = jnp.transpose(end_weight[:, lanes]).astype(jnp.bfloat16)
+    end_ref[...] = jnp.where(keeps, jnp.exp(-rate_line * (block - 1.0 - token)), 0.0).astype(
+        jnp.bfloat16
+    )
 
     lag = ((block - iota((block, width), 0)) % block).astype(jnp.float32)
     response = scaled_line * jnp.exp(-rate_line * lag)
     high = response.astype(jnp.bfloat16)
     low = (response - high.astype(jnp.float32)).astype(jnp.bfloat16)
     member = (iota((groups, width), 0) == iota((groups, width), 1) // modes).astype(jnp.bfloat16)
-    rows_ref[groups:, :] = dot(member, high, ((1,), (1,))) + dot(member, low, ((1,), (1,)))
-    first = fsdp_place * dp_size * groups + dp_place * groups
-    tap, lane = iota((half, block), 0), iota((half, block), 1)
-    lag_of_lane = (block - lane) % block
-    own_place = (tap + fsdp_place * half == lag_of_lane).astype(jnp.bfloat16)
-    other_place = (tap + (1 - fsdp_place) * half == lag_of_lane).astype(jnp.bfloat16)
-    own_rows = (
-        iota((taps_ref.shape[1], groups), 0) == first + iota((taps_ref.shape[1], groups), 1)
-    ).astype(jnp.bfloat16)
-    own_taps = dot(taps_ref[...], own_rows).astype(jnp.bfloat16)
-    other_taps = dot(other_taps_ref[...], own_rows).astype(jnp.bfloat16)
-    rows_ref[:groups, :] = dot(own_taps, own_place, ((0,), (0,))) + dot(
-        other_taps, other_place, ((0,), (0,))
-    )
-
-    def lay(group, _):
-        medium_row = rows_ref[pl.ds(group, 1), :]
-        turned = pltpu.roll(
-            jnp.broadcast_to(medium_row, (block, block)), 0, 1, stride=1, stride_axis=0
-        )
-        medium_ref[group, :, :block] = jnp.where(previous_mask, turned, 0.0).astype(jnp.bfloat16)
-        medium_ref[group, :, block:] = jnp.where(current_mask, turned, 0.0).astype(jnp.bfloat16)
-        long_row = rows_ref[pl.ds(groups + group, 1), :]
-        turned = pltpu.roll(
-            jnp.broadcast_to(long_row, (block, block)), 0, 1, stride=1, stride_axis=0
-        )
-        long_ref[group] = jnp.where(current_mask, turned, 0.0).astype(jnp.bfloat16)
-        return 0
-
-    lax.fori_loop(0, groups, lay, 0, unroll=4)
+    rows_ref[...] = dot(member, high, ((1,), (1,))) + dot(member, low, ((1,), (1,)))
+    for group in range(groups):
+        long_ref[group] = circulant(rows_ref[group : group + 1, :], block) * current
 
 
 def grouped(matrices, values):
@@ -157,16 +203,18 @@
     modes = state_ref.shape[0]
     per_slab = LANES // GROUP_CH
     diagonal = iota((LANES, LANES), 0) // modes == iota((LANES, LANES), 1) // GROUP_CH
-    for slab in range(width // LANES):
-        lanes = slice(slab * LANES, (slab + 1) * LANES)
+    slabs = [slice(at, at + LANES) for at in range(0, width, LANES)]
+    for slab, lanes in enumerate(slabs):
         window = jnp.concatenate([halo_ref[:, lanes], product_ref[:, lanes]], axis=0)
         medium = grouped(medium_ref[slab * per_slab : (slab + 1) * per_slab], window)
-        gated = (
+        gated_ref[:, lanes] = (
             query_ref[:, lanes].astype(jnp.float32)
             * medium.astype(jnp.bfloat16).astype(jnp.float32)
         ).astype(jnp.bfloat16)
-        gated_ref[:, lanes] = gated
-        spread = jnp.where(diagonal, dot(end_ref[lanes, :], gated), 0.0)
+    for lanes in slabs:
+        spread = jnp.where(
+            diagonal, dot(end_ref[:, lanes], gated_ref[:, lanes], ((0,), (0,))), 0.0
+        )
         state_ref[:, lanes] = jnp.sum(spread.reshape(per_slab, modes, LANES), axis=0).astype(
             state_ref.dtype
         )
@@ -200,14 +248,12 @@
         )
 
 
-def call(kernel, outs, *args, scalars=0, scratch=()):
-    specs = [pl.BlockSpec(memory_space=pltpu.SMEM)] * scalars + [
-        pl.BlockSpec(memory_space=pltpu.VMEM)
-    ] * (len(args) - scalars)
+def call(kernel, outs, *args, spaces=None, scratch=()):
+    spaces = spaces or [pltpu.VMEM] * len(args)
     return pl.pallas_call(
         kernel,
         out_shape=[jax.ShapeDtypeStruct(shape, dtype) for shape, dtype in outs],
-        in_specs=specs,
+        in_specs=[pl.BlockSpec(memory_space=space) for space in spaces],
         out_specs=[pl.BlockSpec(memory_space=pltpu.VMEM)] * len(outs),
         scratch_shapes=list(scratch),
         compiler_params=pltpu.CompilerParams(vmem_limit_bytes=VMEM_BYTES),
@@ -255,50 +301,68 @@
     place = jnp.stack([lax.axis_index("fsdp"), lax.axis_index("ctx"), lax.axis_index("dp")])
     taps = medium_taps.T
     half = jnp.bfloat16
-    product, modal = call(
-        prepare_kernel,
-        [((tokens, width), half), ((16, modal_rate.shape[0]), half)],
+    rows = modal_rate.shape[0]
+    inputs = [
         key_stream[0],
         value_stream[0],
         modal_rate.T,
         modal_residue.T,
+        query_stream[0],
+        taps,
+        document_starts,
+        skip_gain.reshape(1, width),
+    ]
+    product, modal, query, own_taps, starts, gain = call(
+        prepare_kernel,
+        [((tokens, width), half), ((16, rows), half)] + [(a.shape, a.dtype) for a in inputs[4:]],
+        *[pltpu.with_memory_space_constraint(a, pltpu.HBM) for a in inputs],
+        spaces=[pltpu.HBM] * len(inputs),
+        scratch=[pltpu.VMEM(a.shape, a.dtype) for a in inputs[:4]]
+        + [pltpu.SemaphoreType.DMA((len(inputs),))],
     )
     halo = shifted(product, "ctx", 1)
     other_taps = lax.ppermute(taps, "fsdp", [(0, 1), (1, 0)])
     modal_parts = [
         lax.ppermute(modal, "dp", [(i, i ^ k) for i in range(dp_size)]) for k in range(1, dp_size)
     ]
-    medium, long, end, carry, through, before = call(
-        functools.partial(build_kernel, dp_size, ctx_size),
+    (medium,) = call(
+        functools.partial(medium_kernel, dp_size),
+        [((groups, tokens, 2 * tokens), half)],
+        place,
+        own_taps,
+        other_taps,
+        starts,
+        spaces=[pltpu.SMEM] + [pltpu.VMEM] * 3,
+        scratch=[pltpu.VMEM((groups, tokens), jnp.float32)],
+    )
+    long, end, carry, through, before = call(
+        functools.partial(modal_kernel, dp_size, ctx_size),
         [
-            ((groups, tokens, 2 * tokens), half),
             ((groups, tokens, tokens), half),
-            ((width, tokens), half),
+            ((tokens, width), half),
             ((tokens, width), half),
             ((modes, width), jnp.float32),
             ((modes, width), jnp.float32),
         ],
         place,
-        taps,
-        other_taps,
         modal,
         *modal_parts,
-        document_starts,
-        scalars=1,
-        scratch=[pltpu.VMEM((2 * groups, tokens), jnp.float32)],
+        starts,
+        spaces=[pltpu.SMEM] + [pltpu.VMEM] * (dp_size + 1),
+        scratch=[pltpu.VMEM((groups, tokens), jnp.float32)],
     )
     gated, state = call(
         gate_kernel,
         [((tokens, width), half), ((modes, width), half)],
         halo,
         product,
-        query_stream[0],
+        query,
         medium,
         end,
     )
     near, far = entering_states(state, through, before)
     (part,) = call(
-        local_kernel, [((tokens, width), jnp.float32)], gated, long, skip_gain.reshape(1, width)
+        local_kernel, [((tokens, width), jnp.float32)], gated, long, gain
     )
     (out,) = call(finish_kernel, [((tokens, width), half)], part, carry, near, far, before)
     return out[None]

time: 36.1 us -> 29.6 us (0.82)
  local copies, waits for them, and re-layouts: 5.75 us -> 0 us
  Pallas kernels: 8.69 us -> 8 us
    unnamed x16 -> x0, local copies, waits for them, and re-layouts: 5.75 us -> none
    pallas_call x5 -> x6, Pallas kernels: 8.69 us -> 8 us  [call(): pl.pallas_call(kernel, out_shape=[jax.ShapeDtypeStruct(shape, dtype) for...]
  transfers between devices with their start and end apart: 8 -> 8, of which waited for: 5 -> 5; matrix products, arithmetic and copies ran while one was open for 0% -> 0% of each run, Pallas kernels for 13% -> 15%
where the time goes in v2:
time: 29.6 us; the launch traced here: 29.4 us
  waiting for transfers between devices  10.8 us (36%)
  starting transfers between devices  10.4 us (35%)
  Pallas kernels  8 us (27%)
    pallas_call x6, Pallas kernels, call(): pl.pallas_call(kernel, out_shape=[jax.ShapeDtypeStruct(shape, dtype) for...  8 us
    ppermute x1, waiting for transfers between devices, entering_states(): lax.ppermute(both, 'ctx', [(1, 2)]) + lax.ppermute(both, 'ctx', [(1, 3)])  6.18 us
    ppermute x3, starting transfers between devices, body(): lax.ppermute(modal, 'dp', [(i, i ^ k) for i in range(dp_size)])  3.55 us
    ppermute x1, starting transfers between devices, shifted(): lax.ppermute(array, axis, [(i, i + distance) for i in range(size - distan...  3.48 us
    ppermute x3, waiting for transfers between devices, body(): lax.ppermute(modal, 'dp', [(i, i ^ k) for i in range(dp_size)])  3.04 us
    ppermute x1, waiting for transfers between devices, entering_states(): near = lax.ppermute(state, 'ctx', [(0, 1), (2, 3)])  1.58 us
    ppermute x1, starting transfers between devices, entering_states(): lax.ppermute(both, 'ctx', [(1, 2)]) + lax.ppermute(both, 'ctx', [(1, 3)])  1.29 us
    ppermute x1, starting transfers between devices, entering_states(): near = lax.ppermute(state, 'ctx', [(0, 1), (2, 3)])  1.29 us
  transfers between devices with their start and end apart: 8, of which 5 were waited for; matrix products, arithmetic and copies ran while one was open for 0% of the time, Pallas kernels for 15%

profile of v2, /device:TPU:16, one launch (start us, length us, event | category | flops | bytes accessed | tf_op | source)
XLA Modules:
  0.0 29.4 jit_solution(10961948589449345958)
XLA Ops:
  0.0 1.2 %shard_map.82 = (bf16[128,1024]{1,0:T(8,128)(2,1)S(1)}, bf16[16,256]{1,0:T(8,128)(2,1)S(1)}, bf16[128,1024]{1,0:T(8,128)(2,1)S(1)}, bf16[64,512]{1,0:T(8,128)(2,...) custom-call(bf16[128,1024]{1,0:T(8,128)(2,1)} %bitcast.11, bf16[128,1024]{1,0:T(8,128)(2,1)} %bitcast.12, ...), custom_call_target="tpu_custom_call" | custom-call | tf_op jit(solution)/shard_map/pallas_call | solution.py:253
  1.2 3.5 %collective-permute-start = (bf16[128,1024]{1,0:T(8,128)(2,1)S(1)}, bf16[128,1024]{1,0:T(8,128)(2,1)S(1)}, u32[]{:S(2)}, u32[]{:S(2)}) collective-permute-start(bf16[128,1024]{1,0:T(8,128)(2,1)S(1)} %get-tuple-element.18.product_ref), channel_id=1, source_target_pairs={{0,4},{4,8},{8,12},{1,5},{5,9},{9,13},{2,6},{6,10},{10,14},{3,7},{... | collective-permute-start | bytes 786440 | tf_op jit(solution)/shard_map/ppermute | solution.py:265
  4.7 0.1 collective-permute-start.1
  4.8 2.5 %collective-permute-start.4 = (bf16[16,256]{1,0:T(8,128)(2,1)S(1)}, bf16[16,256]{1,0:T(8,128)(2,1)S(1)}, u32[]{:S(2)}, u32[]{:S(2)}) collective-permute-start(bf16[16,256]{1,0:T(8,128)(2,1)S(1)} %get-tuple-element.22.modal_ref), channel_id=1, source_target_pairs={{0,3},{1,2},{2,1},{3,0},{4,7},{5,6},{6,5},{7,4},{8,11},{9,10},{10,... | collective-permute-start | bytes 24584 | tf_op jit(solution)/shard_map/ppermute | solution.py:326
  7.3 0.5 %collective-permute-start.3 = (bf16[16,256]{1,0:T(8,128)(2,1)S(1)}, bf16[16,256]{1,0:T(8,128)(2,1)S(1)}, u32[]{:S(2)}, u32[]{:S(2)}) collective-permute-start(bf16[16,256]{1,0:T(8,128)(2,1)S(1)} %get-tuple-element.22.modal_ref), channel_id=1, source_target_pairs={{0,2},{1,3},{2,0},{3,1},{4,6},{5,7},{6,4},{7,5},{8,10},{9,11},{10,... | collective-permute-start | bytes 24584 | tf_op jit(solution)/shard_map/ppermute | solution.py:326
  7.8 0.5 %collective-permute-start.2 = (bf16[16,256]{1,0:T(8,128)(2,1)S(1)}, bf16[16,256]{1,0:T(8,128)(2,1)S(1)}, u32[]{:S(2)}, u32[]{:S(2)}) collective-permute-start(bf16[16,256]{1,0:T(8,128)(2,1)S(1)} %get-tuple-element.22.modal_ref), channel_id=1, source_target_pairs={{0,1},{1,0},{2,3},{3,2},{4,5},{5,4},{6,7},{7,6},{8,9},{9,8},{10,11... | collective-permute-start | bytes 24584 | tf_op jit(solution)/shard_map/ppermute | solution.py:326
  8.4 0.1 pad_add_fusion.place_ref
  8.4 1.0 %collective-permute-done.4.rest_2_ = bf16[16,256]{1,0:T(8,128)(2,1)S(1)} collective-permute-done((bf16[16,256]{1,0:T(8,128)(2,1)S(1)}, bf16[16,256]{1,0:T(8,128)(2,1)S(1)}, u32[]{:S(2)}, u32[]{:S(2)}) %collective-permute-start.4) | collective-permute-done | bytes 8224 | tf_op jit(solution)/shard_map/ppermute | solution.py:326
  9.4 1.5 %collective-permute-done.3.rest_1_ = bf16[16,256]{1,0:T(8,128)(2,1)S(1)} collective-permute-done((bf16[16,256]{1,0:T(8,128)(2,1)S(1)}, bf16[16,256]{1,0:T(8,128)(2,1)S(1)}, u32[]{:S(2)}, u32[]{:S(2)}) %collective-permute-start.3) | collective-permute-done | bytes 8224 | tf_op jit(solution)/shard_map/ppermute | solution.py:326
  11.0 0.5 %collective-permute-done.2.rest_0_ = bf16[16,256]{1,0:T(8,128)(2,1)S(1)} collective-permute-done((bf16[16,256]{1,0:T(8,128)(2,1)S(1)}, bf16[16,256]{1,0:T(8,128)(2,1)S(1)}, u32[]{:S(2)}, u32[]{:S(2)}) %collective-permute-start.2) | collective-permute-done | bytes 8224 | tf_op jit(solution)/shard_map/ppermute | solution.py:326
  11.5 2.1 %shard_map.84 = (bf16[64,128,128]{2,1,0:T(8,128)(2,1)S(1)}, bf16[128,1024]{1,0:T(8,128)(2,1)S(1)}, bf16[128,1024]{1,0:T(8,128)(2,1)S(1)}, f32[16,1024]{1,0:T(8,128)S(1)}, f32[16,1024]{1,0:T(8,128)S(1)}) custom-call(s32[3]{0:T(128)S(1)} %pad_add_fusion.place_ref, bf16[16,256]{1,0:T(8,128)(2,1)S(1)} %get-tuple-element.22.modal_ref, ...), custom_call_target="tpu_custom_call" | custom-call | tf_op jit(solution)/shard_map/pallas_call | solution.py:253
  13.6 0.0 collective-permute-done.1.other_taps_ref
  13.6 1.6 %shard_map.83.medium_ref = bf16[64,128,256]{2,1,0:T(8,128)(2,1)S(1)} custom-call(s32[3]{0:T(128)S(1)} %pad_add_fusion.place_ref, bf16[64,512]{1,0:T(8,128)(2,1)S(1)} %get-tuple-element.20.taps_ref, bf16[64,512]{1,0:T(8,128)(2,1)S(1)} %collective-permute-done.1.other_taps_ref, s32[1,512]{1,0:T(1,128)S(1)} %get-tuple-element.21.starts_ref.rest_3_), custom_call_target="tpu_custom_call" | custom-call | tf_op jit(solution)/shard_map/pallas_call | solution.py:253
  15.2 0.0 collective-permute-done.halo_ref
  15.2 1.4 %shard_map.85 = (bf16[128,1024]{1,0:T(8,128)(2,1)S(1)}, bf16[16,1024]{1,0:T(8,128)(2,1)S(1)}) custom-call(bf16[128,1024]{1,0:T(8,128)(2,1)S(1)} %collective-permute-done.halo_ref, bf16[128,1024]{1,0:T(8,128)(2,1)S(1)} %get-tuple-element.18.product_ref, bf16[128,1024]{1,0:T(8,128)(2,1)S(1)} %get-tuple-element.19.query_ref, ...), custom_call_target="tpu_custom_call" | custom-call | tf_op jit(solution)/shard_map/pallas_call | solution.py:253
  16.7 1.3 %collective-permute-start.5 = (bf16[16,1024]{1,0:T(8,128)(2,1)S(1)}, bf16[16,1024]{1,0:T(8,128)(2,1)S(1)}, u32[]{:S(2)}, u32[]{:S(2)}) collective-permute-start(bf16[16,1024]{1,0:T(8,128)(2,1)S(1)} %get-tuple-element.28), channel_id=1, source_target_pairs={{0,4},{8,12},{1,5},{9,13},{2,6},{10,14},{3,7},{11,15},{16,20},{24,... | collective-permute-start | bytes 98312 | tf_op jit(solution)/shard_map/ppermute | solution.py:271
  18.0 1.6 %collective-permute-done.5.near_ref = bf16[16,1024]{1,0:T(8,128)(2,1)S(1)} collective-permute-done((bf16[16,1024]{1,0:T(8,128)(2,1)S(1)}, bf16[16,1024]{1,0:T(8,128)(2,1)S(1)}, u32[]{:S(2)}, u32[]{:S(2)}) %collective-permute-start.5) | collective-permute-done | bytes 32800 | tf_op jit(solution)/shard_map/ppermute | solution.py:271
  19.6 0.7 %collective-permute-start.7 = (bf16[16,1024]{1,0:T(8,128)(2,1)S(1)}, bf16[16,1024]{1,0:T(8,128)(2,1)S(1)}, u32[]{:S(2)}, u32[]{:S(2)}) collective-permute-start(bf16[16,1024]{1,0:T(8,128)(2,1)S(1)} %add_convert_fusion), channel_id=1, source_target_pairs={{4,12},{5,13},{6,14},{7,15},{20,28},{21,29},{22,30},{23,31}} | collective-permute-start | bytes 98312 | tf_op jit(solution)/shard_map/ppermute | solution.py:273
  20.2 1.3 %collective-permute-start.6 = (bf16[16,1024]{1,0:T(8,128)(2,1)S(1)}, bf16[16,1024]{1,0:T(8,128)(2,1)S(1)}, u32[]{:S(2)}, u32[]{:S(2)}) collective-permute-start(bf16[16,1024]{1,0:T(8,128)(2,1)S(1)} %add_convert_fusion), channel_id=1, source_target_pairs={{4,8},{5,9},{6,10},{7,11},{20,24},{21,25},{22,26},{23,27}} | collective-permute-start | bytes 98312 | tf_op jit(solution)/shard_map/ppermute | solution.py:273
  21.5 0.7 %shard_map.86.part_ref = f32[128,1024]{1,0:T(8,128)S(1)} custom-call(bf16[128,1024]{1,0:T(8,128)(2,1)S(1)} %get-tuple-element.24.gated_ref, bf16[64,128,128]{2,1,0:T(8,128)(2,1)S(1)} %get-tuple-element.25.long_ref, f32[1,1024]{1,0:T(1,128)S(1)} %get-tuple-element.26.gain_ref), custom_call_target="tpu_custom_call" | custom-call | tf_op jit(solution)/shard_map/pallas_call | solution.py:253
  22.2 0.0 collective-permute-done.7
  22.2 6.2 %collective-permute-done.6 = bf16[16,1024]{1,0:T(8,128)(2,1)S(1)} collective-permute-done((bf16[16,1024]{1,0:T(8,128)(2,1)S(1)}, bf16[16,1024]{1,0:T(8,128)(2,1)S(1)}, u32[]{:S(2)}, u32[]{:S(2)}) %collective-permute-start.6) | collective-permute-done | bytes 32800 | tf_op jit(solution)/shard_map/ppermute | solution.py:273
  28.4 0.9 %shard_map.87 = bf16[128,1024]{1,0:T(8,128)(2,1)} custom-call(f32[128,1024]{1,0:T(8,128)S(1)} %shard_map.86.part_ref, bf16[128,1024]{1,0:T(8,128)(2,1)S(1)} %get-tuple-element.27.carry_ref, bf16[16,1024]{1,0:T(8,128)(2,1)S(1)} %collective-permute-done.5.near_ref, bf16[16,1024]{1,0:T(8,128)(2,1)S(1)} %add.7.far_ref, f32[16,1024]{1,0:T(8,128)S(1)} %get-tuple-element.30.before_ref), custom_call_target="tpu_custom_call" | custom-call | tf_op jit(solution)/shard_map/pallas_call | solution.py:253
  (2 shorter events, 0.0 us)
Async XLA Ops:
  1.2 14.0 %collective-permute-start = (bf16[128,1024]{1,0:T(8,128)(2,1)S(1)}, bf16[128,1024]{1,0:T(8,128)(2,1)S(1)}, u32[]{:S(2)}, u32[]{:S(2)}) collective-permute-start(bf16[128,1024]{1,0:T(8,128)(2,1)S(1)} %get-tuple-element.18.product_ref), channel_id=1, source_target_pairs={{0,4},{4,8},{8,12},{1,5},{5,9},{9,13},{2,6},{6,10},{10,14},{3,7},{... | collective-permute-start | bytes 786440 | tf_op jit(solution)/shard_map/ppermute | solution.py:265
  4.7 8.9 %collective-permute-start.1 = (bf16[64,512]{1,0:T(8,128)(2,1)}, bf16[64,512]{1,0:T(8,128)(2,1)S(1)}, u32[]{:S(2)}, u32[]{:S(2)}) collective-permute-start(bf16[64,512]{1,0:T(8,128)(2,1)} %bitcast.15), channel_id=1, source_target_pairs={{0,16},{16,0},{1,17},{17,1},{2,18},{18,2},{3,19},{19,3},{4,20},{20... | collective-permute-start | bytes 196616 | tf_op jit(solution)/shard_map/ppermute | solution.py:324
  4.8 4.6 %collective-permute-start.4 = (bf16[16,256]{1,0:T(8,128)(2,1)S(1)}, bf16[16,256]{1,0:T(8,128)(2,1)S(1)}, u32[]{:S(2)}, u32[]{:S(2)}) collective-permute-start(bf16[16,256]{1,0:T(8,128)(2,1)S(1)} %get-tuple-element.22.modal_ref), channel_id=1, source_target_pairs={{0,3},{1,2},{2,1},{3,0},{4,7},{5,6},{6,5},{7,4},{8,11},{9,10},{10,... | collective-permute-start | bytes 24584 | tf_op jit(solution)/shard_map/ppermute | solution.py:326
  7.3 3.7 %collective-permute-start.3 = (bf16[16,256]{1,0:T(8,128)(2,1)S(1)}, bf16[16,256]{1,0:T(8,128)(2,1)S(1)}, u32[]{:S(2)}, u32[]{:S(2)}) collective-permute-start(bf16[16,256]{1,0:T(8,128)(2,1)S(1)} %get-tuple-element.22.modal_ref), channel_id=1, source_target_pairs={{0,2},{1,3},{2,0},{3,1},{4,6},{5,7},{6,4},{7,5},{8,10},{9,11},{10,... | collective-permute-start | bytes 24584 | tf_op jit(solution)/shard_map/ppermute | solution.py:326
  7.8 3.7 %collective-permute-start.2 = (bf16[16,256]{1,0:T(8,128)(2,1)S(1)}, bf16[16,256]{1,0:T(8,128)(2,1)S(1)}, u32[]{:S(2)}, u32[]{:S(2)}) collective-permute-start(bf16[16,256]{1,0:T(8,128)(2,1)S(1)} %get-tuple-element.22.modal_ref), channel_id=1, source_target_pairs={{0,1},{1,0},{2,3},{3,2},{4,5},{5,4},{6,7},{7,6},{8,9},{9,8},{10,11... | collective-permute-start | bytes 24584 | tf_op jit(solution)/shard_map/ppermute | solution.py:326
  16.7 2.9 %collective-permute-start.5 = (bf16[16,1024]{1,0:T(8,128)(2,1)S(1)}, bf16[16,1024]{1,0:T(8,128)(2,1)S(1)}, u32[]{:S(2)}, u32[]{:S(2)}) collective-permute-start(bf16[16,1024]{1,0:T(8,128)(2,1)S(1)} %get-tuple-element.28), channel_id=1, source_target_pairs={{0,4},{8,12},{1,5},{9,13},{2,6},{10,14},{3,7},{11,15},{16,20},{24,... | collective-permute-start | bytes 98312 | tf_op jit(solution)/shard_map/ppermute | solution.py:271
  19.6 2.7 %collective-permute-start.7 = (bf16[16,1024]{1,0:T(8,128)(2,1)S(1)}, bf16[16,1024]{1,0:T(8,128)(2,1)S(1)}, u32[]{:S(2)}, u32[]{:S(2)}) collective-permute-start(bf16[16,1024]{1,0:T(8,128)(2,1)S(1)} %add_convert_fusion), channel_id=1, source_target_pairs={{4,12},{5,13},{6,14},{7,15},{20,28},{21,29},{22,30},{23,31}} | collective-permute-start | bytes 98312 | tf_op jit(solution)/shard_map/ppermute | solution.py:273
  20.2 8.2 %collective-permute-start.6 = (bf16[16,1024]{1,0:T(8,128)(2,1)S(1)}, bf16[16,1024]{1,0:T(8,128)(2,1)S(1)}, u32[]{:S(2)}, u32[]{:S(2)}) collective-permute-start(bf16[16,1024]{1,0:T(8,128)(2,1)S(1)} %add_convert_fusion), channel_id=1, source_target_pairs={{4,8},{5,9},{6,10},{7,11},{20,24},{21,25},{22,26},{23,27}} | collective-permute-start | bytes 98312 | tf_op jit(solution)/shard_map/ppermute | solution.py:273

commit v3 on v2

v3 whole, which is shorter than its diff:
```python
import functools

import jax
import jax.numpy as jnp
from jax import lax
from jax.experimental import pallas as pl
from jax.experimental.pallas import tpu as pltpu
from jax.sharding import PartitionSpec as P

GROUP_CH = 16
LANES = 128
VMEM_BYTES = 32 * 1024 * 1024


def iota(shape, dim):
    return lax.broadcasted_iota(jnp.int32, shape, dim)


def dot(a, b, contract=((1,), (0,))):
    return lax.dot_general(a, b, (contract, ((), ())), preferred_element_type=jnp.float32)


def prepare_kernel(
    key_hbm,
    value_hbm,
    rate_hbm,
    residue_hbm,
    query_hbm,
    taps_hbm,
    starts_hbm,
    gain_hbm,
    product_ref,
    modal_ref,
    query_ref,
    taps_ref,
    starts_ref,
    gain_ref,
    key_ref,
    value_ref,
    rate_ref,
    residue_ref,
    arrived,
):
    pairs = (
        (key_hbm, key_ref),
        (value_hbm, value_ref),
        (rate_hbm, rate_ref),
        (residue_hbm, residue_ref),
        (query_hbm, query_ref),
        (taps_hbm, taps_ref),
        (starts_hbm, starts_ref),
        (gain_hbm, gain_ref),
    )
    copies = [
        pltpu.make_async_copy(source, target, arrived.at[i])
        for i, (source, target) in enumerate(pairs)
    ]
    for copy in copies:
        copy.start()
    for copy in copies[:4]:
        copy.wait()
    product_ref[...] = (
        key_ref[...].astype(jnp.float32) * value_ref[...].astype(jnp.float32)
    ).astype(jnp.bfloat16)
    rate = rate_ref[...].astype(jnp.float32)
    residue = residue_ref[...].astype(jnp.float32)
    gap = jnp.zeros((8 - rate.shape[0], rate.shape[1]), jnp.float32)
    modal_ref[...] = jnp.concatenate([rate, gap, residue, gap], axis=0).astype(jnp.bfloat16)
    for copy in copies[4:]:
        copy.wait()


def block_starts(starts_ref, ctx_place, block):
    prior_place = jnp.maximum(ctx_place - 1, 0)
    return [
        starts_ref[:, pl.ds(pl.multiple_of(place * block, block), block)].astype(jnp.float32)
        for place in (ctx_place, prior_place)
    ]


def document_masks(own, prior, block):
    row, col = iota((block, block), 0), iota((block, block), 1)
    both = jnp.concatenate(
        [jnp.broadcast_to(own, (8, block)), jnp.broadcast_to(prior, (8, block))], axis=0
    ).astype(jnp.bfloat16)
    upto = (row <= col).astype(jnp.bfloat16)
    doc_row = dot(both, upto)[0:1]
    after_row = dot(both, (row > col).astype(jnp.bfloat16))[8:9]
    doc_col = dot(
        upto, jnp.broadcast_to(own, (block, block)).astype(jnp.bfloat16), ((0,), (1,))
    )
    current = (row >= col) & (doc_col == doc_row)
    previous = (col > row) & (doc_col == 0.0) & (after_row == 0.0)
    return doc_col, current, previous


def circulant(row, block):
    return pltpu.roll(
        jnp.broadcast_to(row, (block, block)), 0, 1, stride=1, stride_axis=0
    ).astype(jnp.bfloat16)


def medium_kernel(
    taps_ref,
    other_taps_ref,
    starts_ref,
    previous_ref,
    current_ref,
    same_ref,
    doc_ref,
    rows_ref,
):
    fsdp_place, ctx_place, dp_place = (lax.axis_index(axis) for axis in ("fsdp", "ctx", "dp"))
    groups, block = previous_ref.shape[0], previous_ref.shape[1]
    half = taps_ref.shape[0]
    first = (fsdp_place * lax.axis_size("dp") + dp_place) * groups
    base = pl.multiple_of(first // LANES * LANES, LANES)
    tap, lane = iota((half, block), 0), iota((half, block), 1)
    lag_of_lane = (block - lane) % block
    own_place = (tap + fsdp_place * half == lag_of_lane).astype(jnp.bfloat16)
    other_place = (tap + (1 - fsdp_place) * half == lag_of_lane).astype(jnp.bfloat16)
    rows_ref[...] = dot(taps_ref[:, pl.ds(base, LANES)], own_place, ((0,), (0,))) + dot(
        other_taps_ref[:, pl.ds(base, LANES)], other_place, ((0,), (0,))
    )
    own, prior = block_starts(starts_ref, ctx_place, block)
    doc_col, current, previous = document_masks(own, prior, block)
    current = current.astype(jnp.bfloat16)
    previous = (previous & (ctx_place > 0)).astype(jnp.bfloat16)
    same_ref[...] = current
    doc_ref[...] = doc_col
    for group in range(groups):
        turned = circulant(rows_ref[pl.ds(first - base + group, 1), :], block)
        previous_ref[group] = turned * previous
        current_ref[group] = turned * current


def slabs_of(width):
    return [slice(at, at + LANES) for at in range(0, width, LANES)]


def gated_by(query, medium):
    return (
        query.astype(jnp.float32) * medium.astype(jnp.bfloat16).astype(jnp.float32)
    ).astype(jnp.bfloat16)


def end_states(end_ref, gated_ref, state_ref):
    modes, width = state_ref.shape
    per_slab = LANES // GROUP_CH
    diagonal = iota((LANES, LANES), 0) // modes == iota((LANES, LANES), 1) // GROUP_CH
    for lanes in slabs_of(width):
        spread = jnp.where(
            diagonal, dot(end_ref[:, lanes], gated_ref[:, lanes], ((0,), (0,))), 0.0
        )
        state_ref[:, lanes] = jnp.sum(spread.reshape(per_slab, modes, LANES), axis=0).astype(
            state_ref.dtype
        )


def own_kernel(product_ref, query_ref, current_ref, medium_ref, gated_ref):
    per_slab = LANES // GROUP_CH
    for slab, lanes in enumerate(slabs_of(product_ref.shape[1])):
        medium = grouped(
            current_ref[slab * per_slab : (slab + 1) * per_slab], product_ref[:, lanes]
        )
        medium_ref[:, lanes] = medium
        gated_ref[:, lanes] = gated_by(query_ref[:, lanes], medium)


def modal_kernel(
    modal_ref,
    modal_rest_ref,
    starts_ref,
    doc_ref,
    gated_ref,
    end_ref,
    rate_ref,
    scaled_ref,
    through_ref,
    first_ref,
    far_ref,
    state_ref,
):
    ctx_place, dp_place = lax.axis_index("ctx"), lax.axis_index("dp")
    block, width = end_ref.shape
    modes = through_ref.shape[0]
    groups = width // modes
    per_part = modes // lax.axis_size("dp")
    first = dp_place * groups
    base = pl.multiple_of(first // LANES * LANES, LANES)
    pieces = jnp.concatenate(
        [modal_ref[:, pl.ds(base, LANES)], modal_rest_ref[:, pl.ds(base, LANES)]], axis=0
    )
    lines = pieces.shape[0]
    line, mode = iota((2 * modes, lines), 1), iota((2 * modes, lines), 0)
    within = line % 16
    held = jnp.where(mode < modes, within, within - 8)
    owner = jnp.bitwise_xor(dp_place, line // 16)
    wanted = owner * per_part + held == jnp.where(mode < modes, mode, mode - modes)
    select = ((held >= 0) & (held < per_part) & wanted).astype(jnp.bfloat16)
    ordered = dot(select, pieces).astype(jnp.bfloat16)
    spread = (
        iota((LANES, width), 0) == first - base + iota((LANES, width), 1) // modes
    ).astype(jnp.bfloat16)
    by_channel = dot(ordered, spread)
    rate = by_channel[:modes]
    on_line = iota((modes, width), 0) == iota((modes, width), 1) % modes
    rate_line = jnp.sum(jnp.where(on_line, rate, 0.0), axis=0, keepdims=True)
    token = iota((block, LANES), 0).astype(jnp.float32)
    keeps = doc_ref[...] == doc_ref[block - 1 : block, :]
    for lanes in slabs_of(width):
        weight = jnp.exp(-rate_line[:, lanes] * (block - 1.0 - token))
        end_ref[:, lanes] = jnp.where(keeps, weight, 0.0).astype(jnp.bfloat16)
    end_states(end_ref, gated_ref, state_ref)
    scaled = by_channel[modes:] * jnp.sqrt((1.0 - jnp.exp(-2.0 * rate)) / modes)
    rate_ref[...] = rate_line
    scaled_ref[...] = jnp.sum(jnp.where(on_line, scaled, 0.0), axis=0, keepdims=True)
    decay = jnp.exp(-rate * block)
    own, prior = block_starts(starts_ref, ctx_place, block)
    none_own = jnp.sum(own, axis=1, keepdims=True) == 0.0
    none_prior = jnp.sum(prior, axis=1, keepdims=True) == 0.0
    through_ref[...] = jnp.where(none_own, decay, 0.0)
    first_ref[...] = jnp.where(none_own & (ctx_place == 1), decay, 0.0)
    far_ref[...] = jnp.where(none_prior, decay, 0.0)


def long_kernel(rate_ref, scaled_ref, current_ref, doc_ref, long_ref, carry_ref, rows_ref):
    groups, block = long_ref.shape[0], long_ref.shape[1]
    width = carry_ref.shape[1]
    modes = width // groups
    lag = ((block - iota((block, width), 0)) % block).astype(jnp.float32)
    response = scaled_ref[...] * jnp.exp(-rate_ref[...] * lag)
    high = response.astype(jnp.bfloat16)
    low = (response - high.astype(jnp.float32)).astype(jnp.bfloat16)
    member = (iota((groups, width), 0) == iota((groups, width), 1) // modes).astype(jnp.bfloat16)
    rows_ref[...] = dot(member, high, ((1,), (1,))) + dot(member, low, ((1,), (1,)))
    token = iota((block, LANES), 0).astype(jnp.float32)
    continues = doc_ref[...] == 0.0
    for at in range(0, width, LANES):
        lanes = slice(at, at + LANES)
        weight = scaled_ref[:, lanes] * jnp.exp(-rate_ref[:, lanes] * (token + 1.0))
        carry_ref[:, lanes] = jnp.where(continues, weight, 0.0).astype(jnp.bfloat16)
    current = current_ref[...]
    for group in range(groups):
        long_ref[group] = circulant(rows_ref[group : group + 1, :], block) * current


def grouped(matrices, values):
    count, out, rows = matrices.shape
    product = dot(matrices.reshape(count * out, rows), values)
    lane = iota((out, LANES), 1) // GROUP_CH
    result = product[:out]
    for k in range(1, count):
        result = jnp.where(lane == k, product[k * out : (k + 1) * out], result)
    return result


def gate_kernel(
    halo_ref, query_ref, previous_ref, medium_ref, end_ref, _, gated_ref, state_ref
):
    per_slab = LANES // GROUP_CH
    for slab, lanes in enumerate(slabs_of(halo_ref.shape[1])):
        medium = medium_ref[:, lanes] + grouped(
            previous_ref[slab * per_slab : (slab + 1) * per_slab], halo_ref[:, lanes]
        )
        gated_ref[:, lanes] = gated_by(query_ref[:, lanes], medium)
    end_states(end_ref, gated_ref, state_ref)


def local_kernel(gated_ref, long_ref, gain_ref, part_ref):
    width = gated_ref.shape[1]
    per_slab = LANES // GROUP_CH
    for slab in range(width // LANES):
        lanes = slice(slab * LANES, (slab + 1) * LANES)
        gated = gated_ref[:, lanes]
        part_ref[:, lanes] = grouped(
            long_ref[slab * per_slab : (slab + 1) * per_slab], gated
        ) + gain_ref[:, lanes] * gated.astype(jnp.float32)


def finish_kernel(
    four, part_ref, carry_ref, first_ref, near_ref, far_ref, through_ref, out_ref
):
    width = part_ref.shape[1]
    modes = near_ref.shape[0]
    per_slab = LANES // GROUP_CH
    diagonal = iota((LANES, LANES), 0) // modes == iota((LANES, LANES), 1) // GROUP_CH
    entering = near_ref[...].astype(jnp.float32)
    if four:
        place = lax.axis_index("ctx")
        entering += jnp.where(place == 3, through_ref[...] * far_ref[...].astype(jnp.float32), 0.0)
        entering += jnp.where(place == 1, first_ref[...].astype(jnp.float32), 0.0)
    for slab in range(width // LANES):
        lanes = slice(slab * LANES, (slab + 1) * LANES)
        state = jnp.concatenate([entering[:, lanes]] * per_slab, axis=0)
        spread = jnp.where(diagonal, state, 0.0).astype(jnp.bfloat16)
        out_ref[:, lanes] = (part_ref[:, lanes] + dot(carry_ref[:, lanes], spread)).astype(
            out_ref.dtype
        )


def call(kernel, outs, *args, spaces=None, scratch=(), micros=0.3):
    spaces = spaces or [pltpu.VMEM] * len(args)
    return pl.pallas_call(
        kernel,
        out_shape=[jax.ShapeDtypeStruct(shape, dtype) for shape, dtype in outs],
        in_specs=[pl.BlockSpec(memory_space=space) for space in spaces],
        out_specs=[pl.BlockSpec(memory_space=pltpu.VMEM)] * len(outs),
        scratch_shapes=list(scratch),
        cost_estimate=pl.CostEstimate(
            flops=int(micros * 1e9), bytes_accessed=0, transcendentals=0
        ),
        compiler_params=pltpu.CompilerParams(vmem_limit_bytes=VMEM_BYTES),
    )(*args)


def shifted(array, axis, distance):
    size = lax.axis_size(axis)
    return lax.ppermute(array, axis, [(i, i + distance) for i in range(size - distance)])


def exchanged(array, axis, bit):
    return lax.ppermute(array, axis, [(i, i ^ bit) for i in range(lax.axis_size(axis))])


def entering_states(state, through):
    size = lax.axis_size("ctx")
    total, factor, distance = state.astype(jnp.float32), through, 1
    while distance < size:
        total = total + factor * shifted(total, "ctx", distance)
        factor = factor * shifted(factor, "ctx", distance)
        distance *= 2
    return shifted(total, "ctx", 1)


def body(
    query_stream,
    key_stream,
    value_stream,
    document_starts,
    medium_taps,
    modal_rate,
    modal_residue,
    skip_gain,
):
    tokens, width = query_stream.shape[1:]
    groups = width // GROUP_CH
    fsdp_size, dp_size = lax.axis_size("fsdp"), lax.axis_size("dp")
    ctx_size = lax.axis_size("ctx")
    modes = modal_rate.shape[1] * dp_size
    assert fsdp_size == 2 and tokens == medium_taps.shape[1] * fsdp_size
    assert modes == GROUP_CH and modal_rate.shape[1] <= 8
    taps = medium_taps.T
    half = jnp.bfloat16
    rows = modal_rate.shape[0]
    inputs = [
        key_stream[0],
        value_stream[0],
        modal_rate.T,
        modal_residue.T,
        query_stream[0],
        taps,
        document_starts,
        skip_gain.reshape(1, width),
    ]
    product, modal, query, own_taps, starts, gain = call(
        prepare_kernel,
        [((tokens, width), half), ((16, rows), half)] + [(a.shape, a.dtype) for a in inputs[4:]],
        *[pltpu.with_memory_space_constraint(a, pltpu.HBM) for a in inputs],
        spaces=[pltpu.HBM] * len(inputs),
        scratch=[pltpu.VMEM(a.shape, a.dtype) for a in inputs[:4]]
        + [pltpu.SemaphoreType.DMA((len(inputs),))],
    )
    halo = lax.ppermute(product, "ctx", [(i, (i + 1) % ctx_size) for i in range(ctx_size)])
    other_taps = exchanged(taps, "fsdp", 1)
    bit = 1
    while 2 * bit < dp_size:
        modal = jnp.concatenate([modal, exchanged(modal, "dp", bit)], axis=0)
        bit *= 2
    modal_rest = exchanged(modal, "dp", bit)
    square = ((groups, tokens, tokens), half)
    previous, current, same, documents = call(
        medium_kernel,
        [square, square, ((tokens, tokens), half), ((tokens, tokens), jnp.float32)],
        own_taps,
        other_taps,
        starts,
        scratch=[pltpu.VMEM((LANES, tokens), jnp.float32)],
    )
    medium, gated_own = call(
        own_kernel,
        [((tokens, width), jnp.float32), ((tokens, width), half)],
        product,
        query,
        current,
    )
    line, states = ((1, width), jnp.float32), ((modes, width), jnp.float32)
    end, rate, scaled, through, first_through, far_through, state_own = call(
        modal_kernel,
        [((tokens, width), half), line, line, states, states, states, ((modes, width), half)],
        modal,
        modal_rest,
        starts,
        documents,
        gated_own,
    )
    four = ctx_size == 4
    first = exchanged(state_own, "ctx", 1) if four else state_own
    long, carry = call(
        long_kernel,
        [square, ((tokens, width), half)],
        rate,
        scaled,
        same,
        documents,
        scratch=[pltpu.VMEM((groups, tokens), jnp.float32)],
    )
    gated, state = call(
        gate_kernel,
        [((tokens, width), half), ((modes, width), half)],
        halo,
        query,
        previous,
        medium,
        end,
        carry,
    )
    if four:
        both = state.astype(jnp.float32) + first_through * first.astype(jnp.float32)
        both = both.astype(half)
        far = exchanged(both, "ctx", 2)
        near = lax.ppermute(both, "ctx", [(1, 2), (2, 3)])
    else:
        near = far = entering_states(state, through)
    (part,) = call(local_kernel, [((tokens, width), jnp.float32)], gated, long, gain)
    (out,) = call(
        functools.partial(finish_kernel, four),
        [((tokens, width), half)],
        part,
        carry,
        first,
        near,
        far,
        far_through,
    )
    return out[None]


def solution(mesh):
    return jax.shard_map(
        body,
        mesh=mesh,
        in_specs=(
            P(None, "ctx", ("fsdp", "dp")),
            P(None, "ctx", ("fsdp", "dp")),
            P(None, "ctx", ("fsdp", "dp")),
            P(),
            P(None, "fsdp"),
            P("fsdp", "dp"),
            P("fsdp", "dp"),
            P(("fsdp", "dp")),
        ),
        out_specs=P(None, "ctx", ("fsdp", "dp")),
        check_vma=False,
    )
```

time: 29.6 us -> 21.5 us (0.73)
  the two profiles are of different devices: /device:TPU:16 before, /device:TPU:0 now
where the time goes in v3:
time: 21.5 us; the launch traced here: 21.4 us
  starting transfers between devices  11.8 us (55%)
  Pallas kernels  7.69 us (36%)
  waiting for transfers between devices  1.83 us (9%)
    ppermute x5, starting transfers between devices, exchanged(): lax.ppermute(array, axis, [(i, i ^ bit) for i in range(lax.axis_size(axis...  9.53 us
    pallas_call x8, Pallas kernels, call(): pl.pallas_call(kernel, out_shape=[jax.ShapeDtypeStruct(shape, dtype) for...  7.69 us
    ppermute x1, starting transfers between devices, body(): lax.ppermute(product, 'ctx', [(i, (i + 1) % ctx_size) for i in range(ctx_...  1.58 us
    ppermute x5, waiting for transfers between devices, exchanged(): lax.ppermute(array, axis, [(i, i ^ bit) for i in range(lax.axis_size(axis...  1.17 us
    ppermute x1, waiting for transfers between devices, body(): lax.ppermute(product, 'ctx', [(i, (i + 1) % ctx_size) for i in range(ctx_...  0.66 us
    ppermute x1, starting transfers between devices, body(): near = lax.ppermute(both, 'ctx', [(1, 2), (2, 3)])  0.65 us
  transfers between devices with their start and end apart: 7, of which 3 were waited for; matrix products, arithmetic and copies ran while one was open for 0% of the time, Pallas kernels for 32%

profile of v3, /device:TPU:0, one launch (start us, length us, event | category | flops | bytes accessed | tf_op | source)
XLA Modules:
  0.0 21.4 jit_solution(15355887956865810937)
XLA Ops:
  0.0 0.5 %collective-permute-start.1 = (bf16[64,512]{1,0:T(8,128)(2,1)}, bf16[64,512]{1,0:T(8,128)(2,1)S(1)}, u32[]{:S(2)}, u32[]{:S(2)}) collective-permute-start(bf16[64,512]{1,0:T(8,128)(2,1)} %bitcast.11), channel_id=1, source_target_pairs={{0,16},{16,0},{1,17},{17,1},{2,18},{18,2},{3,19},{19,3},{4,20},{20... | collective-permute-start | bytes 196616 | tf_op jit(solution)/shard_map/ppermute | solution.py:323
  0.5 1.2 %shard_map.82 = (bf16[128,1024]{1,0:T(8,128)(2,1)S(1)}, bf16[16,256]{1,0:T(8,128)(2,1)S(1)}, bf16[128,1024]{1,0:T(8,128)(2,1)S(1)}, bf16[64,512]{1,0:T(8,128)(2,...) custom-call(bf16[128,1024]{1,0:T(8,128)(2,1)} %bitcast.8, bf16[128,1024]{1,0:T(8,128)(2,1)} %bitcast.9, ...), custom_call_target="tpu_custom_call" | custom-call | flops 300000000 | tf_op jit(solution)/shard_map/pallas_call | solution.py:304
  1.7 2.6 %collective-permute-start.2 = (bf16[16,256]{1,0:T(8,128)(2,1)S(1)}, bf16[16,256]{1,0:T(8,128)(2,1)S(1)}, u32[]{:S(2)}, u32[]{:S(2)}) collective-permute-start(bf16[16,256]{1,0:T(8,128)(2,1)S(1)} %get-tuple-element.34), channel_id=1, source_target_pairs={{0,1},{1,0},{2,3},{3,2},{4,5},{5,4},{6,7},{7,6},{8,9},{9,8},{10,11... | collective-permute-start | bytes 24584 | tf_op jit(solution)/shard_map/ppermute | solution.py:323
  4.2 1.6 %collective-permute-start = (bf16[128,1024]{1,0:T(8,128)(2,1)S(1)}, bf16[128,1024]{1,0:T(8,128)(2,1)S(1)}, u32[]{:S(2)}, u32[]{:S(2)}) collective-permute-start(bf16[128,1024]{1,0:T(8,128)(2,1)S(1)} %get-tuple-element.27.product_ref), channel_id=1, source_target_pairs={{0,4},{4,8},{8,12},{12,0},{1,5},{5,9},{9,13},{13,1},{2,6},{6,10},{... | collective-permute-start | bytes 786440 | tf_op jit(solution)/shard_map/ppermute | solution.py:374
  5.8 0.1 collective-permute-done.2
  5.9 2.0 %collective-permute-start.3 = (bf16[32,256]{1,0:T(8,128)(2,1)S(1)}, bf16[32,256]{1,0:T(8,128)(2,1)S(1)}, u32[]{:S(2)}, u32[]{:S(2)}) collective-permute-start(bf16[32,256]{1,0:T(8,128)(2,1)S(1)} %constant_dynamic-update-slice_fusion.modal_ref), channel_id=1, source_target_pairs={{0,2},{1,3},{2,0},{3,1},{4,6},{5,7},{6,4},{7,5},{8,10},{9,11},{10,... | collective-permute-start | bytes 49160 | tf_op jit(solution)/shard_map/ppermute | solution.py:323
  7.9 0.0 collective-permute-done.1.other_taps_ref
  7.9 1.0 %shard_map.83 = (bf16[64,128,128]{2,1,0:T(8,128)(2,1)S(1)}, bf16[64,128,128]{2,1,0:T(8,128)(2,1)S(1)}, bf16[128,128]{1,0:T(8,128)(2,1)S(1)}, f32[128,128]{1,0:T(8,128)S(1)}) custom-call(bf16[64,512]{1,0:T(8,128)(2,1)S(1)} %get-tuple-element.29.taps_ref, bf16[64,512]{1,0:T(8,128)(2,1)S(1)} %collective-permute-done.1.other_taps_ref, ...), custom_call_target="tpu_custom_call" | custom-call | flops 300000000 | tf_op jit(solution)/shard_map/pallas_call | solution.py:304
  8.9 0.7 %shard_map.84 = (f32[128,1024]{1,0:T(8,128)S(1)}, bf16[128,1024]{1,0:T(8,128)(2,1)S(1)}) custom-call(bf16[128,1024]{1,0:T(8,128)(2,1)S(1)} %get-tuple-element.27.product_ref, bf16[128,1024]{1,0:T(8,128)(2,1)S(1)} %get-tuple-element.28.query_ref, bf16[64,128,128]{2,1,0:T(8,128)(2,1)S(1)} %get-tuple-element.32.current_ref), custom_call_target="tpu_custom_call" | custom-call | flops 300000000 | tf_op jit(solution)/shard_map/pallas_call | solution.py:304
  9.6 0.0 collective-permute-done.3.modal_rest_ref
  9.6 1.2 %shard_map.85 = (bf16[128,1024]{1,0:T(8,128)(2,1)S(1)}, f32[1,1024]{1,0:T(1,128)S(1)}, f32[1,1024]{1,0:T(1,128)S(1)}, f32[16,1024]{1,0:T(8,128)}, f32[16,1024]{1...) custom-call(bf16[32,256]{1,0:T(8,128)(2,1)S(1)} %constant_dynamic-update-slice_fusion.modal_ref, ...), custom_call_target="tpu_custom_call" | custom-call | flops 300000000 | tf_op jit(solution)/shard_map/pallas_call | solution.py:304
  10.9 2.1 %collective-permute-start.4 = (bf16[16,1024]{1,0:T(8,128)(2,1)S(1)}, bf16[16,1024]{1,0:T(8,128)(2,1)S(1)}, u32[]{:S(2)}, u32[]{:S(2)}) collective-permute-start(bf16[16,1024]{1,0:T(8,128)(2,1)S(1)} %get-tuple-element.45), channel_id=1, source_target_pairs={{0,4},{4,0},{8,12},{12,8},{1,5},{5,1},{9,13},{13,9},{2,6},{6,2},{1... | collective-permute-start | bytes 98312 | tf_op jit(solution)/shard_map/ppermute | solution.py:323
  12.9 1.0 %shard_map.86 = (bf16[64,128,128]{2,1,0:T(8,128)(2,1)S(1)}, bf16[128,1024]{1,0:T(8,128)(2,1)S(1)}) custom-call(f32[1,1024]{1,0:T(1,128)S(1)} %get-tuple-element.38.rate_ref, f32[1,1024]{1,0:T(1,128)S(1)} %get-tuple-element.39.scaled_ref, bf16[128,128]{1,0:T(8,128)(2,1)S(1)} %get-tuple-element.40.current_ref, f32[128,128]{1,0:T(8,128)S(1)} %get-tuple-element.35.doc_ref), custom_call_target="tpu_custom_call" | custom-call | flops 300000000 | tf_op jit(solution)/shard_map/pallas_call | solution.py:304
  14.0 0.7 %collective-permute-done.halo_ref = bf16[128,1024]{1,0:T(8,128)(2,1)S(1)} collective-permute-done((bf16[128,1024]{1,0:T(8,128)(2,1)S(1)}, bf16[128,1024]{1,0:T(8,128)(2,1)S(1)}, u32[]{:S(2)}, u32[]{:S(2)}) %collective-permute-start) | collective-permute-done | bytes 262176 | tf_op jit(solution)/shard_map/ppermute | solution.py:374
  14.6 0.9 %shard_map.87 = (bf16[128,1024]{1,0:T(8,128)(2,1)S(1)}, bf16[16,1024]{1,0:T(8,128)(2,1)S(1)}) custom-call(bf16[128,1024]{1,0:T(8,128)(2,1)S(1)} %collective-permute-done.halo_ref, bf16[128,1024]{1,0:T(8,128)(2,1)S(1)} %get-tuple-element.28.query_ref, bf16[64,128,128]{2,1,0:T(8,128)(2,1)S(1)} %get-tuple-element.31.previous_ref, ...), custom_call_target="tpu_custom_call" | custom-call | flops 300000000 | tf_op jit(solution)/shard_map/pallas_call | solution.py:304
  15.5 0.0 collective-permute-done.4.first_ref
  15.5 2.4 %collective-permute-start.6 = (bf16[16,1024]{1,0:T(8,128)(2,1)S(1)}, bf16[16,1024]{1,0:T(8,128)(2,1)S(1)}, u32[]{:S(2)}, u32[]{:S(2)}) collective-permute-start(bf16[16,1024]{1,0:T(8,128)(2,1)S(1)} %add_convert_fusion), channel_id=1, source_target_pairs={{0,8},{4,12},{8,0},{12,4},{1,9},{5,13},{9,1},{13,5},{2,10},{6,14},... | collective-permute-start | bytes 98312 | tf_op jit(solution)/shard_map/ppermute | solution.py:323
  17.9 0.7 %collective-permute-start.5 = (bf16[16,1024]{1,0:T(8,128)(2,1)S(1)}, bf16[16,1024]{1,0:T(8,128)(2,1)S(1)}, u32[]{:S(2)}, u32[]{:S(2)}) collective-permute-start(bf16[16,1024]{1,0:T(8,128)(2,1)S(1)} %add_convert_fusion), channel_id=1, source_target_pairs={{4,8},{8,12},{5,9},{9,13},{6,10},{10,14},{7,11},{11,15},{20,24},{2... | collective-permute-start | bytes 98312 | tf_op jit(solution)/shard_map/ppermute | solution.py:432
  18.6 0.7 %shard_map.88.part_ref = f32[128,1024]{1,0:T(8,128)S(1)} custom-call(bf16[128,1024]{1,0:T(8,128)(2,1)S(1)} %get-tuple-element.42.gated_ref, bf16[64,128,128]{2,1,0:T(8,128)(2,1)S(1)} %get-tuple-element.43.long_ref, f32[1,1024]{1,0:T(1,128)S(1)} %get-tuple-element.44.gain_ref), custom_call_target="tpu_custom_call" | custom-call | flops 300000000 | tf_op jit(solution)/shard_map/pallas_call | solution.py:304
  19.3 1.1 %collective-permute-done.6.far_ref = bf16[16,1024]{1,0:T(8,128)(2,1)S(1)} collective-permute-done((bf16[16,1024]{1,0:T(8,128)(2,1)S(1)}, bf16[16,1024]{1,0:T(8,128)(2,1)S(1)}, u32[]{:S(2)}, u32[]{:S(2)}) %collective-permute-start.6) | collective-permute-done | bytes 32800 | tf_op jit(solution)/shard_map/ppermute | solution.py:323
  20.4 0.0 collective-permute-done.5.near_ref
  20.4 0.9 %shard_map.89 = bf16[128,1024]{1,0:T(8,128)(2,1)} custom-call(f32[128,1024]{1,0:T(8,128)S(1)} %shard_map.88.part_ref, bf16[128,1024]{1,0:T(8,128)(2,1)S(1)} %get-tuple-element.41._.carry_ref, bf16[16,1024]{1,0:T(8,128)(2,1)S(1)} %collective-permute-done.4.first_ref, bf16[16,1024]{1,0:T(8,128)(2,1)S(1)} %collective-permute-done.5.near_ref, ...), custom_call_target="tpu_custom_call" | custom-call | flops 300000000 | tf_op jit(solution)/shard_map/pallas_call | solution.py:304
  (3 shorter events, 0.0 us)
Async XLA Ops:
  0.0 7.9 %collective-permute-start.1 = (bf16[64,512]{1,0:T(8,128)(2,1)}, bf16[64,512]{1,0:T(8,128)(2,1)S(1)}, u32[]{:S(2)}, u32[]{:S(2)}) collective-permute-start(bf16[64,512]{1,0:T(8,128)(2,1)} %bitcast.11), channel_id=1, source_target_pairs={{0,16},{16,0},{1,17},{17,1},{2,18},{18,2},{3,19},{19,3},{4,20},{20... | collective-permute-start | bytes 196616 | tf_op jit(solution)/shard_map/ppermute | solution.py:323
  1.7 4.2 %collective-permute-start.2 = (bf16[16,256]{1,0:T(8,128)(2,1)S(1)}, bf16[16,256]{1,0:T(8,128)(2,1)S(1)}, u32[]{:S(2)}, u32[]{:S(2)}) collective-permute-start(bf16[16,256]{1,0:T(8,128)(2,1)S(1)} %get-tuple-element.34), channel_id=1, source_target_pairs={{0,1},{1,0},{2,3},{3,2},{4,5},{5,4},{6,7},{7,6},{8,9},{9,8},{10,11... | collective-permute-start | bytes 24584 | tf_op jit(solution)/shard_map/ppermute | solution.py:323
  4.2 10.4 %collective-permute-start = (bf16[128,1024]{1,0:T(8,128)(2,1)S(1)}, bf16[128,1024]{1,0:T(8,128)(2,1)S(1)}, u32[]{:S(2)}, u32[]{:S(2)}) collective-permute-start(bf16[128,1024]{1,0:T(8,128)(2,1)S(1)} %get-tuple-element.27.product_ref), channel_id=1, source_target_pairs={{0,4},{4,8},{8,12},{12,0},{1,5},{5,9},{9,13},{13,1},{2,6},{6,10},{... | collective-permute-start | bytes 786440 | tf_op jit(solution)/shard_map/ppermute | solution.py:374
  5.9 3.8 %collective-permute-start.3 = (bf16[32,256]{1,0:T(8,128)(2,1)S(1)}, bf16[32,256]{1,0:T(8,128)(2,1)S(1)}, u32[]{:S(2)}, u32[]{:S(2)}) collective-permute-start(bf16[32,256]{1,0:T(8,128)(2,1)S(1)} %constant_dynamic-update-slice_fusion.modal_ref), channel_id=1, source_target_pairs={{0,2},{1,3},{2,0},{3,1},{4,6},{5,7},{6,4},{7,5},{8,10},{9,11},{10,... | collective-permute-start | bytes 49160 | tf_op jit(solution)/shard_map/ppermute | solution.py:323
  10.9 4.7 %collective-permute-start.4 = (bf16[16,1024]{1,0:T(8,128)(2,1)S(1)}, bf16[16,1024]{1,0:T(8,128)(2,1)S(1)}, u32[]{:S(2)}, u32[]{:S(2)}) collective-permute-start(bf16[16,1024]{1,0:T(8,128)(2,1)S(1)} %get-tuple-element.45), channel_id=1, source_target_pairs={{0,4},{4,0},{8,12},{12,8},{1,5},{5,1},{9,13},{13,9},{2,6},{6,2},{1... | collective-permute-start | bytes 98312 | tf_op jit(solution)/shard_map/ppermute | solution.py:323
  15.5 4.9 %collective-permute-start.6 = (bf16[16,1024]{1,0:T(8,128)(2,1)S(1)}, bf16[16,1024]{1,0:T(8,128)(2,1)S(1)}, u32[]{:S(2)}, u32[]{:S(2)}) collective-permute-start(bf16[16,1024]{1,0:T(8,128)(2,1)S(1)} %add_convert_fusion), channel_id=1, source_target_pairs={{0,8},{4,12},{8,0},{12,4},{1,9},{5,13},{9,1},{13,5},{2,10},{6,14},... | collective-permute-start | bytes 98312 | tf_op jit(solution)/shard_map/ppermute | solution.py:323
  17.9 2.5 %collective-permute-start.5 = (bf16[16,1024]{1,0:T(8,128)(2,1)S(1)}, bf16[16,1024]{1,0:T(8,128)(2,1)S(1)}, u32[]{:S(2)}, u32[]{:S(2)}) collective-permute-start(bf16[16,1024]{1,0:T(8,128)(2,1)S(1)} %add_convert_fusion), channel_id=1, source_target_pairs={{4,8},{8,12},{5,9},{9,13},{6,10},{10,14},{7,11},{11,15},{20,24},{2... | collective-permute-start | bytes 98312 | tf_op jit(solution)/shard_map/ppermute | solution.py:432

commit v4 on v3

--- a/solution.py
+++ b/solution.py
@@ -31,6 +31,8 @@
     gain_hbm,
     product_ref,
     modal_ref,
+    spread_ref,
+    select_ref,
     query_ref,
     taps_ref,
     starts_ref,
@@ -57,6 +59,20 @@
     ]
     for copy in copies:
         copy.start()
+    dp_place = lax.axis_index("dp")
+    modes, width = select_ref.shape[0] // 2, spread_ref.shape[1]
+    per_part = rate_ref.shape[0]
+    lines = select_ref.shape[1]
+    line, mode = iota((2 * modes, lines), 1), iota((2 * modes, lines), 0)
+    within = line % 16
+    held = jnp.where(mode < modes, within, within - 8)
+    owner = jnp.bitwise_xor(dp_place, line // 16)
+    wanted = owner * per_part + held == jnp.where(mode < modes, mode, mode - modes)
+    select_ref[...] = ((held >= 0) & (held < per_part) & wanted).astype(jnp.bfloat16)
+    first = dp_place * (width // modes) % LANES
+    spread_ref[...] = (
+        iota((LANES, width), 0) == first + iota((LANES, width), 1) // modes
+    ).astype(jnp.bfloat16)
     for copy in copies[:4]:
         copy.wait()
     product_ref[...] = (
@@ -96,8 +112,14 @@
 
 def circulant(row, block):
     return pltpu.roll(
-        jnp.broadcast_to(row, (block, block)), 0, 1, stride=1, stride_axis=0
+        jnp.broadcast_to(row, (block // 2, block)), 0, 1, stride=1, stride_axis=0
     ).astype(jnp.bfloat16)
+
+
+def folded(mask, block):
+    half = block // 2
+    lower = pltpu.roll(mask[half:], half, 1)
+    return [mask[:half].astype(jnp.bfloat16), lower.astype(jnp.bfloat16)]
 
 
 def medium_kernel(
@@ -124,14 +146,17 @@
     )
     own, prior = block_starts(starts_ref, ctx_place, block)
     doc_col, current, previous = document_masks(own, prior, block)
-    current = current.astype(jnp.bfloat16)
-    previous = (previous & (ctx_place > 0)).astype(jnp.bfloat16)
-    same_ref[...] = current
+    current = folded(current.astype(jnp.float32), block)
+    previous = folded((previous & (ctx_place > 0)).astype(jnp.float32), block)
+    halves = [slice(0, block // 2), slice(block // 2, block)]
     doc_ref[...] = doc_col
+    for part, rows in enumerate(halves):
+        same_ref[rows, :] = current[part]
     for group in range(groups):
         turned = circulant(rows_ref[pl.ds(first - base + group, 1), :], block)
-        previous_ref[group] = turned * previous
-        current_ref[group] = turned * current
+        for part, rows in enumerate(halves):
+            previous_ref[group, rows, :] = turned * previous[part]
+            current_ref[group, rows, :] = turned * current[part]
 
 
 def slabs_of(width):
@@ -167,54 +192,84 @@
         gated_ref[:, lanes] = gated_by(query_ref[:, lanes], medium)
 
 
+def on_line(modes, width):
+    return iota((modes, width), 0) == iota((modes, width), 1) % modes
+
+
 def modal_kernel(
     modal_ref,
     modal_rest_ref,
-    starts_ref,
+    select_ref,
+    spread_ref,
     doc_ref,
     gated_ref,
     end_ref,
-    rate_ref,
-    scaled_ref,
+    channels_ref,
+    state_ref,
+):
+    block, width = end_ref.shape
+    modes = state_ref.shape[0]
+    first = lax.axis_index("dp") * (width // modes)
+    base = pl.multiple_of(first // LANES * LANES, LANES)
+    pieces = jnp.concatenate(
+        [modal_ref[:, pl.ds(base, LANES)], modal_rest_ref[:, pl.ds(base, LANES)]], axis=0
+    )
+    ordered = dot(select_ref[...], pieces)
+    by_channel = dot(ordered.astype(jnp.bfloat16), spread_ref[...])
+    channels_ref[...] = by_channel
+    rate_line = jnp.sum(
+        jnp.where(on_line(modes, width), by_channel[:modes], 0.0), axis=0, keepdims=True
+    )
+    left = (block - 1 - iota((block, LANES), 0)).astype(jnp.float32)
+    keeps = doc_ref[...] == doc_ref[block - 1 : block, :]
+    for lanes in slabs_of(width):
+        weight = jnp.exp(-rate_line[:, lanes] * left)
+        end_ref[:, lanes] = jnp.where(keeps, weight, 0.0).astype(jnp.bfloat16)
+    end_states(end_ref, gated_ref, state_ref)
+
+
+def long_kernel(
+    channels_ref,
+    starts_ref,
+    same_ref,
+    doc_ref,
+    long_ref,
+    carry_ref,
     through_ref,
     first_ref,
     far_ref,
-    state_ref,
-):
-    ctx_place, dp_place = lax.axis_index("ctx"), lax.axis_index("dp")
-    block, width = end_ref.shape
-    modes = through_ref.shape[0]
-    groups = width // modes
-    per_part = modes // lax.axis_size("dp")
-    first = dp_place * groups
-    base = pl.multiple_of(first // LANES * LANES, LANES)
-    pieces = jnp.concatenate(
-        [modal_ref[:, pl.ds(base, LANES)], modal_rest_ref[:, pl.ds(base, LANES)]], axis=0
-    )
-    lines = pieces.shape[0]
-    line, mode = iota((2 * modes, lines), 1), iota((2 * modes, lines), 0)
-    within = line % 16
-    held = jnp.where(mode < modes, within, within - 8)
-    owner = jnp.bitwise_xor(dp_place, line // 16)
-    wanted = owner * per_part + held == jnp.where(mode < modes, mode, mode - modes)
-    select = ((held >= 0) & (held < per_part) & wanted).astype(jnp.bfloat16)
-    ordered = dot(select, pieces).astype(jnp.bfloat16)
-    spread = (
-        iota((LANES, width), 0) == first - base + iota((LANES, width), 1) // modes
-    ).astype(jnp.bfloat16)
-    by_channel = dot(ordered, spread)
-    rate = by_channel[:modes]
-    on_line = iota((modes, width), 0) == iota((modes, width), 1) % modes
-    rate_line = jnp.sum(jnp.where(on_line, rate, 0.0), axis=0, keepdims=True)
-    token = iota((block, LANES), 0).astype(jnp.float32)
-    keeps = doc_ref[...] == doc_ref[block - 1 : block, :]
+    rows_ref,
+):
+    groups, block = long_ref.shape[0], long_ref.shape[1]
+    modes, width = through_ref.shape
+    ctx_place = lax.axis_index("ctx")
+    rate = channels_ref[:modes]
+    scaled = channels_ref[modes:] * jnp.sqrt((1.0 - jnp.exp(-2.0 * rate)) / modes)
+    chosen = on_line(modes, width)
+    rate_line = jnp.sum(jnp.where(chosen, rate, 0.0), axis=0, keepdims=True)
+    scaled_line = jnp.sum(jnp.where(chosen, scaled, 0.0), axis=0, keepdims=True)
+    lag = ((block - iota((block, LANES), 0)) % block).astype(jnp.float32)
+    response = jnp.zeros((groups, block), jnp.float32)
     for lanes in slabs_of(width):
-        weight = jnp.exp(-rate_line[:, lanes] * (block - 1.0 - token))
-        end_ref[:, lanes] = jnp.where(keeps, weight, 0.0).astype(jnp.bfloat16)
-    end_states(end_ref, gated_ref, state_ref)
-    scaled = by_channel[modes:] * jnp.sqrt((1.0 - jnp.exp(-2.0 * rate)) / modes)
-    rate_ref[...] = rate_line
-    scaled_ref[...] = jnp.sum(jnp.where(on_line, scaled, 0.0), axis=0, keepdims=True)
+        terms = scaled_line[:, lanes] * jnp.exp(-rate_line[:, lanes] * lag)
+        high = terms.astype(jnp.bfloat16)
+        low = (terms - high.astype(jnp.float32)).astype(jnp.bfloat16)
+        member = (
+            iota((groups, LANES), 0) == (lanes.start + iota((groups, LANES), 1)) // modes
+        ).astype(jnp.bfloat16)
+        response += dot(member, high, ((1,), (1,))) + dot(member, low, ((1,), (1,)))
+    rows_ref[...] = response
+    since = (iota((block, LANES), 0) + 1).astype(jnp.float32)
+    continues = doc_ref[...] == 0.0
+    for lanes in slabs_of(width):
+        weight = scaled_line[:, lanes] * jnp.exp(-rate_line[:, lanes] * since)
+        carry_ref[:, lanes] = jnp.where(continues, weight, 0.0).astype(jnp.bfloat16)
+    halves = [slice(0, block // 2), slice(block // 2, block)]
+    same = [same_ref[rows, :] for rows in halves]
+    for group in range(groups):
+        turned = circulant(rows_ref[group : group + 1, :], block)
+        for part, rows in enumerate(halves):
+            long_ref[group, rows, :] = turned * same[part]
     decay = jnp.exp(-rate * block)
     own, prior = block_starts(starts_ref, ctx_place, block)
     none_own = jnp.sum(own, axis=1, keepdims=True) == 0.0
@@ -224,35 +279,20 @@
     far_ref[...] = jnp.where(none_prior, decay, 0.0)
 
 
-def long_kernel(rate_ref, scaled_ref, current_ref, doc_ref, long_ref, carry_ref, rows_ref):
-    groups, block = long_ref.shape[0], long_ref.shape[1]
-    width = carry_ref.shape[1]
-    modes = width // groups
-    lag = ((block - iota((block, width), 0)) % block).astype(jnp.float32)
-    response = scaled_ref[...] * jnp.exp(-rate_ref[...] * lag)
-    high = response.astype(jnp.bfloat16)
-    low = (response - high.astype(jnp.float32)).astype(jnp.bfloat16)
-    member = (iota((groups, width), 0) == iota((groups, width), 1) // modes).astype(jnp.bfloat16)
-    rows_ref[...] = dot(member, high, ((1,), (1,))) + dot(member, low, ((1,), (1,)))
-    token = iota((block, LANES), 0).astype(jnp.float32)
-    continues = doc_ref[...] == 0.0
-    for at in range(0, width, LANES):
-        lanes = slice(at, at + LANES)
-        weight = scaled_ref[:, lanes] * jnp.exp(-rate_ref[:, lanes] * (token + 1.0))
-        carry_ref[:, lanes] = jnp.where(continues, weight, 0.0).astype(jnp.bfloat16)
-    current = current_ref[...]
-    for group in range(groups):
-        long_ref[group] = circulant(rows_ref[group : group + 1, :], block) * current
-
-
 def grouped(matrices, values):
-    count, out, rows = matrices.shape
-    product = dot(matrices.reshape(count * out, rows), values)
-    lane = iota((out, LANES), 1) // GROUP_CH
-    result = product[:out]
-    for k in range(1, count):
-        result = jnp.where(lane == k, product[k * out : (k + 1) * out], result)
-    return result
+    count, rows, _ = matrices.shape
+    half = rows // 2
+    lane = iota((half, LANES), 1) // GROUP_CH
+    results = []
+    for part in range(2):
+        turned = values if part == 0 else jnp.concatenate([values[half:], values[:half]], axis=0)
+        chosen = matrices[:, part * half : (part + 1) * half].reshape(count * half, rows)
+        product = dot(chosen, turned)
+        result = product[:half]
+        for k in range(1, count):
+            result = jnp.where(lane == k, product[k * half : (k + 1) * half], result)
+        results.append(result)
+    return jnp.concatenate(results, axis=0)
 
 
 def gate_kernel(
@@ -279,7 +319,7 @@
 
 
 def finish_kernel(
-    four, part_ref, carry_ref, first_ref, near_ref, far_ref, through_ref, out_ref
+    four, part_ref, carry_ref, first_ref, far_ref, near_ref, through_ref, out_ref
 ):
     width = part_ref.shape[1]
     modes = near_ref.shape[0]
@@ -288,6 +328,7 @@
     entering = near_ref[...].astype(jnp.float32)
     if four:
         place = lax.axis_index("ctx")
+        entering = jnp.where(place >= 2, entering, 0.0)
         entering += jnp.where(place == 3, through_ref[...] * far_ref[...].astype(jnp.float32), 0.0)
         entering += jnp.where(place == 1, first_ref[...].astype(jnp.float32), 0.0)
     for slab in range(width // LANES):
@@ -321,6 +362,17 @@
 
 def exchanged(array, axis, bit):
     return lax.ppermute(array, axis, [(i, i ^ bit) for i in range(lax.axis_size(axis))])
+
+
+def cycled(array, cycle):
+    fsdp_size, ctx_size = lax.axis_size("fsdp"), lax.axis_size("ctx")
+    after = dict(zip(cycle, cycle[1:] + cycle[:1]))
+    moves = []
+    for core in range(fsdp_size):
+        for place in range(ctx_size):
+            other = (core, after[place]) if place in after else (core ^ 1, place)
+            moves.append((core * ctx_size + place, other[0] * ctx_size + other[1]))
+    return lax.ppermute(array, ("fsdp", "ctx"), moves)
 
 
 def entering_states(state, through):
@@ -363,9 +415,15 @@
         document_starts,
         skip_gain.reshape(1, width),
     ]
-    product, modal, query, own_taps, starts, gain = call(
+    product, modal, spread, select, query, own_taps, starts, gain = call(
         prepare_kernel,
-        [((tokens, width), half), ((16, rows), half)] + [(a.shape, a.dtype) for a in inputs[4:]],
+        [
+            ((tokens, width), half),
+            ((16, rows), half),
+            ((LANES, width), half),
+            ((2 * modes, 16 * dp_size), half),
+        ]
+        + [(a.shape, a.dtype) for a in inputs[4:]],
         *[pltpu.with_memory_space_constraint(a, pltpu.HBM) for a in inputs],
         spaces=[pltpu.HBM] * len(inputs),
         scratch=[pltpu.VMEM(a.shape, a.dtype) for a in inputs[:4]]
@@ -394,26 +452,33 @@
         query,
         current,
     )
-    line, states = ((1, width), jnp.float32), ((modes, width), jnp.float32)
-    end, rate, scaled, through, first_through, far_through, state_own = call(
+    states = ((modes, width), jnp.float32)
+    end, channels, state_own = call(
         modal_kernel,
-        [((tokens, width), half), line, line, states, states, states, ((modes, width), half)],
+        [
+            ((tokens, width), half),
+            ((2 * modes, width), jnp.float32),
+            ((modes, width), half),
+        ],
         modal,
         modal_rest,
-        starts,
+        select,
+        spread,
         documents,
         gated_own,
     )
     four = ctx_size == 4
-    first = exchanged(state_own, "ctx", 1) if four else state_own
-    long, carry = call(
+    first = cycled(state_own, [0, 1]) if four else state_own
+    long, carry, through, first_through, far_through = call(
         long_kernel,
-        [square, ((tokens, width), half)],
-        rate,
-        scaled,
+        [square, ((tokens, width), half), states, states, states],
+        channels,
+        starts,
         same,
         documents,
-        scratch=[pltpu.VMEM((groups, tokens), jnp.float32)],
+        scratch=[
+            pltpu.VMEM((groups, tokens), jnp.float32),
+        ],
     )
     gated, state = call(
         gate_kernel,
@@ -428,8 +493,8 @@
     if four:
         both = state.astype(jnp.float32) + first_through * first.astype(jnp.float32)
         both = both.astype(half)
-        far = exchanged(both, "ctx", 2)
-        near = lax.ppermute(both, "ctx", [(1, 2), (2, 3)])
+        near = cycled(both, [1, 2, 3])
+        far = cycled(both, [1, 3, 2])
     else:
         near = far = entering_states(state, through)
     (part,) = call(local_kernel, [((tokens, width), jnp.float32)], gated, long, gain)
@@ -439,8 +504,8 @@
         part,
         carry,
         first,
+        far,
         near,
-        far,
         far_through,
     )
     return out[None]

time: 21.5 us -> 19.6 us (0.912)
  the two profiles are of different devices: /device:TPU:0 before, /device:TPU:24 now
where the time goes in v4:
time: 19.6 us; the launch traced here: 19.4 us
  Pallas kernels  7.48 us (38%)
  waiting for transfers between devices  6.42 us (33%)
  starting transfers between devices  5.45 us (28%)
    pallas_call x8, Pallas kernels, call(): pl.pallas_call(kernel, out_shape=[jax.ShapeDtypeStruct(shape, dtype) for...  7.48 us
    ppermute x3, waiting for transfers between devices, cycled(): return lax.ppermute(array, ('fsdp', 'ctx'), moves)  3.59 us
    ppermute x3, starting transfers between devices, exchanged(): lax.ppermute(array, axis, [(i, i ^ bit) for i in range(lax.axis_size(axis...  3.08 us
    ppermute x3, waiting for transfers between devices, exchanged(): lax.ppermute(array, axis, [(i, i ^ bit) for i in range(lax.axis_size(axis...  2.5 us
    ppermute x3, starting transfers between devices, cycled(): return lax.ppermute(array, ('fsdp', 'ctx'), moves)  2.15 us
  transfers between devices with their start and end apart: 7, of which 5 were waited for; matrix products, arithmetic and copies ran while one was open for 0% of the time, Pallas kernels for 34%

profile of v4, /device:TPU:24, one launch (start us, length us, event | category | flops | bytes accessed | tf_op | source)
XLA Modules:
  0.0 19.4 jit_solution(11672410613419142772)
XLA Ops:
  0.0 0.0 collective-permute-start.1
  0.0 1.2 %shard_map.82 = (bf16[128,1024]{1,0:T(8,128)(2,1)S(1)}, bf16[16,256]{1,0:T(8,128)(2,1)S(1)}, bf16[128,1024]{1,0:T(8,128)(2,1)S(1)}, bf16[32,64]{1,0:T(8,128)(2,1...) custom-call(bf16[128,1024]{1,0:T(8,128)(2,1)} %bitcast.8, ...), custom_call_target="tpu_custom_call" | custom-call | flops 300000000 | tf_op jit(solution)/shard_map/pallas_call | solution.py:345
  1.2 1.6 %collective-permute-start.2 = (bf16[16,256]{1,0:T(8,128)(2,1)S(1)}, bf16[16,256]{1,0:T(8,128)(2,1)S(1)}, u32[]{:S(2)}, u32[]{:S(2)}) collective-permute-start(bf16[16,256]{1,0:T(8,128)(2,1)S(1)} %get-tuple-element.35), channel_id=1, source_target_pairs={{0,1},{1,0},{2,3},{3,2},{4,5},{5,4},{6,7},{7,6},{8,9},{9,8},{10,11... | collective-permute-start | bytes 24584 | tf_op jit(solution)/shard_map/ppermute | solution.py:364
  2.8 0.2 %collective-permute-start = (bf16[128,1024]{1,0:T(8,128)(2,1)S(1)}, bf16[128,1024]{1,0:T(8,128)(2,1)S(1)}, u32[]{:S(2)}, u32[]{:S(2)}) collective-permute-start(bf16[128,1024]{1,0:T(8,128)(2,1)S(1)} %get-tuple-element.28.product_ref), channel_id=1, source_target_pairs={{0,4},{4,8},{8,12},{12,0},{1,5},{5,9},{9,13},{13,1},{2,6},{6,10},{... | collective-permute-start | bytes 786440 | tf_op jit(solution)/shard_map/ppermute | solution.py:432
  3.0 1.9 %collective-permute-done.2 = bf16[16,256]{1,0:T(8,128)(2,1)S(1)} collective-permute-done((bf16[16,256]{1,0:T(8,128)(2,1)S(1)}, bf16[16,256]{1,0:T(8,128)(2,1)S(1)}, u32[]{:S(2)}, u32[]{:S(2)}) %collective-permute-start.2) | collective-permute-done | bytes 8224 | tf_op jit(solution)/shard_map/ppermute | solution.py:364
  4.9 1.5 %collective-permute-start.3 = (bf16[32,256]{1,0:T(8,128)(2,1)S(1)}, bf16[32,256]{1,0:T(8,128)(2,1)S(1)}, u32[]{:S(2)}, u32[]{:S(2)}) collective-permute-start(bf16[32,256]{1,0:T(8,128)(2,1)S(1)} %constant_dynamic-update-slice_fusion.modal_ref), channel_id=1, source_target_pairs={{0,2},{1,3},{2,0},{3,1},{4,6},{5,7},{6,4},{7,5},{8,10},{9,11},{10,... | collective-permute-start | bytes 49160 | tf_op jit(solution)/shard_map/ppermute | solution.py:364
  6.5 0.0 collective-permute-done.1.other_taps_ref
  6.5 0.9 %shard_map.83 = (bf16[64,128,128]{2,1,0:T(8,128)(2,1)S(1)}, bf16[64,128,128]{2,1,0:T(8,128)(2,1)S(1)}, bf16[128,128]{1,0:T(8,128)(2,1)S(1)}, f32[128,128]{1,0:T(8,128)S(1)}) custom-call(bf16[64,512]{1,0:T(8,128)(2,1)S(1)} %get-tuple-element.30.taps_ref, bf16[64,512]{1,0:T(8,128)(2,1)S(1)} %collective-permute-done.1.other_taps_ref, ...), custom_call_target="tpu_custom_call" | custom-call | flops 300000000 | tf_op jit(solution)/shard_map/pallas_call | solution.py:345
  7.4 0.7 %shard_map.84 = (f32[128,1024]{1,0:T(8,128)S(1)}, bf16[128,1024]{1,0:T(8,128)(2,1)S(1)}) custom-call(bf16[128,1024]{1,0:T(8,128)(2,1)S(1)} %get-tuple-element.28.product_ref, bf16[128,1024]{1,0:T(8,128)(2,1)S(1)} %get-tuple-element.29.query_ref, bf16[64,128,128]{2,1,0:T(8,128)(2,1)S(1)} %get-tuple-element.33.current_ref), custom_call_target="tpu_custom_call" | custom-call | flops 300000000 | tf_op jit(solution)/shard_map/pallas_call | solution.py:345
  8.1 0.6 %collective-permute-done.3.modal_rest_ref = bf16[32,256]{1,0:T(8,128)(2,1)S(1)} collective-permute-done((bf16[32,256]{1,0:T(8,128)(2,1)S(1)}, bf16[32,256]{1,0:T(8,128)(2,1)S(1)}, u32[]{:S(2)}, u32[]{:S(2)}) %collective-permute-start.3) | collective-permute-done | bytes 16416 | tf_op jit(solution)/shard_map/ppermute | solution.py:364
  8.7 0.6 %shard_map.85 = (bf16[128,1024]{1,0:T(8,128)(2,1)S(1)}, f32[32,1024]{1,0:T(8,128)S(1)}, bf16[16,1024]{1,0:T(8,128)(2,1)S(1)}) custom-call(bf16[32,256]{1,0:T(8,128)(2,1)S(1)} %constant_dynamic-update-slice_fusion.modal_ref, bf16[32,256]{1,0:T(8,128)(2,1)S(1)} %collective-permute-done.3.modal_rest_ref, bf16[32,64]{1,0:T(8,128)(2,1)S(1)} %get-tuple-element.36.select_ref, ...), custom_call_target="tpu_custom_call" | custom-call | flops 300000000 | tf_op jit(solution)/shard_map/pallas_call | solution.py:345
  9.3 0.1 collective-permute-start.4
  9.4 1.5 %shard_map.86 = (bf16[64,128,128]{2,1,0:T(8,128)(2,1)S(1)}, bf16[128,1024]{1,0:T(8,128)(2,1)S(1)}, f32[16,1024]{1,0:T(8,128)}, f32[16,1024]{1,0:T(8,128)S(1)}, f32[16,1024]{1,0:T(8,128)S(1)}) custom-call(f32[32,1024]{1,0:T(8,128)S(1)} %get-tuple-element.41.channels_ref, s32[1,512]{1,0:T(1,128)S(1)} %get-tuple-element.31.starts_ref, ...), custom_call_target="tpu_custom_call" | custom-call | flops 300000000 | tf_op jit(solution)/shard_map/pallas_call | solution.py:345
  10.9 0.3 %collective-permute-done.halo_ref = bf16[128,1024]{1,0:T(8,128)(2,1)S(1)} collective-permute-done((bf16[128,1024]{1,0:T(8,128)(2,1)S(1)}, bf16[128,1024]{1,0:T(8,128)(2,1)S(1)}, u32[]{:S(2)}, u32[]{:S(2)}) %collective-permute-start) | collective-permute-done | bytes 262176 | tf_op jit(solution)/shard_map/ppermute | solution.py:432
  11.2 0.9 %shard_map.87 = (bf16[128,1024]{1,0:T(8,128)(2,1)S(1)}, bf16[16,1024]{1,0:T(8,128)(2,1)S(1)}) custom-call(bf16[128,1024]{1,0:T(8,128)(2,1)S(1)} %collective-permute-done.halo_ref, bf16[128,1024]{1,0:T(8,128)(2,1)S(1)} %get-tuple-element.29.query_ref, bf16[64,128,128]{2,1,0:T(8,128)(2,1)S(1)} %get-tuple-element.32.previous_ref, ...), custom_call_target="tpu_custom_call" | custom-call | flops 300000000 | tf_op jit(solution)/shard_map/pallas_call | solution.py:345
  12.1 0.0 collective-permute-done.4.first_ref
  12.1 1.6 %collective-permute-start.6 = (bf16[16,1024]{1,0:T(8,128)(2,1)S(1)}, bf16[16,1024]{1,0:T(8,128)(2,1)S(1)}, u32[]{:S(2)}, u32[]{:S(2)}) collective-permute-start(bf16[16,1024]{1,0:T(8,128)(2,1)S(1)} %add_convert_fusion), channel_id=1, source_target_pairs={{0,16},{4,8},{8,12},{12,4},{16,0},{20,24},{24,28},{28,20},{1,17},{... | collective-permute-start | bytes 98312 | tf_op jit(solution)/shard_map/ppermute | solution.py:375
  13.7 0.5 %collective-permute-start.5 = (bf16[16,1024]{1,0:T(8,128)(2,1)S(1)}, bf16[16,1024]{1,0:T(8,128)(2,1)S(1)}, u32[]{:S(2)}, u32[]{:S(2)}) collective-permute-start(bf16[16,1024]{1,0:T(8,128)(2,1)S(1)} %add_convert_fusion), channel_id=1, source_target_pairs={{0,16},{4,12},{8,4},{12,8},{16,0},{20,28},{24,20},{28,24},{1,17},{... | collective-permute-start | bytes 98312 | tf_op jit(solution)/shard_map/ppermute | solution.py:375
  14.2 0.7 %shard_map.88.part_ref = f32[128,1024]{1,0:T(8,128)S(1)} custom-call(bf16[128,1024]{1,0:T(8,128)(2,1)S(1)} %get-tuple-element.44.gated_ref, bf16[64,128,128]{2,1,0:T(8,128)(2,1)S(1)} %get-tuple-element.45.long_ref, f32[1,1024]{1,0:T(1,128)S(1)} %get-tuple-element.46.gain_ref), custom_call_target="tpu_custom_call" | custom-call | flops 300000000 | tf_op jit(solution)/shard_map/pallas_call | solution.py:345
  14.9 1.5 %collective-permute-done.6.near_ref = bf16[16,1024]{1,0:T(8,128)(2,1)S(1)} collective-permute-done((bf16[16,1024]{1,0:T(8,128)(2,1)S(1)}, bf16[16,1024]{1,0:T(8,128)(2,1)S(1)}, u32[]{:S(2)}, u32[]{:S(2)}) %collective-permute-start.6) | collective-permute-done | bytes 32800 | tf_op jit(solution)/shard_map/ppermute | solution.py:375
  16.5 2.1 %collective-permute-done.5.far_ref = bf16[16,1024]{1,0:T(8,128)(2,1)S(1)} collective-permute-done((bf16[16,1024]{1,0:T(8,128)(2,1)S(1)}, bf16[16,1024]{1,0:T(8,128)(2,1)S(1)}, u32[]{:S(2)}, u32[]{:S(2)}) %collective-permute-start.5) | collective-permute-done | bytes 32800 | tf_op jit(solution)/shard_map/ppermute | solution.py:375
  18.5 0.9 %shard_map.89 = bf16[128,1024]{1,0:T(8,128)(2,1)} custom-call(f32[128,1024]{1,0:T(8,128)S(1)} %shard_map.88.part_ref, bf16[128,1024]{1,0:T(8,128)(2,1)S(1)} %get-tuple-element.43._.carry_ref, bf16[16,1024]{1,0:T(8,128)(2,1)S(1)} %collective-permute-done.4.first_ref, bf16[16,1024]{1,0:T(8,128)(2,1)S(1)} %collective-permute-done.5.far_ref, ...), custom_call_target="tpu_custom_call" | custom-call | flops 300000000 | tf_op jit(solution)/shard_map/pallas_call | solution.py:345
  (3 shorter events, 0.0 us)
Async XLA Ops:
  0.0 6.5 %collective-permute-start.1 = (bf16[64,512]{1,0:T(8,128)(2,1)}, bf16[64,512]{1,0:T(8,128)(2,1)S(1)}, u32[]{:S(2)}, u32[]{:S(2)}) collective-permute-start(bf16[64,512]{1,0:T(8,128)(2,1)} %bitcast.11), channel_id=1, source_target_pairs={{0,16},{16,0},{1,17},{17,1},{2,18},{18,2},{3,19},{19,3},{4,20},{20... | collective-permute-start | bytes 196616 | tf_op jit(solution)/shard_map/ppermute | solution.py:364
  1.2 3.7 %collective-permute-start.2 = (bf16[16,256]{1,0:T(8,128)(2,1)S(1)}, bf16[16,256]{1,0:T(8,128)(2,1)S(1)}, u32[]{:S(2)}, u32[]{:S(2)}) collective-permute-start(bf16[16,256]{1,0:T(8,128)(2,1)S(1)} %get-tuple-element.35), channel_id=1, source_target_pairs={{0,1},{1,0},{2,3},{3,2},{4,5},{5,4},{6,7},{7,6},{8,9},{9,8},{10,11... | collective-permute-start | bytes 24584 | tf_op jit(solution)/shard_map/ppermute | solution.py:364
  2.8 8.4 %collective-permute-start = (bf16[128,1024]{1,0:T(8,128)(2,1)S(1)}, bf16[128,1024]{1,0:T(8,128)(2,1)S(1)}, u32[]{:S(2)}, u32[]{:S(2)}) collective-permute-start(bf16[128,1024]{1,0:T(8,128)(2,1)S(1)} %get-tuple-element.28.product_ref), channel_id=1, source_target_pairs={{0,4},{4,8},{8,12},{12,0},{1,5},{5,9},{9,13},{13,1},{2,6},{6,10},{... | collective-permute-start | bytes 786440 | tf_op jit(solution)/shard_map/ppermute | solution.py:432
  4.9 3.7 %collective-permute-start.3 = (bf16[32,256]{1,0:T(8,128)(2,1)S(1)}, bf16[32,256]{1,0:T(8,128)(2,1)S(1)}, u32[]{:S(2)}, u32[]{:S(2)}) collective-permute-start(bf16[32,256]{1,0:T(8,128)(2,1)S(1)} %constant_dynamic-update-slice_fusion.modal_ref), channel_id=1, source_target_pairs={{0,2},{1,3},{2,0},{3,1},{4,6},{5,7},{6,4},{7,5},{8,10},{9,11},{10,... | collective-permute-start | bytes 49160 | tf_op jit(solution)/shard_map/ppermute | solution.py:364
  9.3 2.8 %collective-permute-start.4 = (bf16[16,1024]{1,0:T(8,128)(2,1)S(1)}, bf16[16,1024]{1,0:T(8,128)(2,1)S(1)}, u32[]{:S(2)}, u32[]{:S(2)}) collective-permute-start(bf16[16,1024]{1,0:T(8,128)(2,1)S(1)} %get-tuple-element.47), channel_id=1, source_target_pairs={{0,4},{4,0},{8,24},{12,28},{16,20},{20,16},{24,8},{28,12},{1,5},{5... | collective-permute-start | bytes 98312 | tf_op jit(solution)/shard_map/ppermute | solution.py:375
  12.1 4.3 %collective-permute-start.6 = (bf16[16,1024]{1,0:T(8,128)(2,1)S(1)}, bf16[16,1024]{1,0:T(8,128)(2,1)S(1)}, u32[]{:S(2)}, u32[]{:S(2)}) collective-permute-start(bf16[16,1024]{1,0:T(8,128)(2,1)S(1)} %add_convert_fusion), channel_id=1, source_target_pairs={{0,16},{4,8},{8,12},{12,4},{16,0},{20,24},{24,28},{28,20},{1,17},{... | collective-permute-start | bytes 98312 | tf_op jit(solution)/shard_map/ppermute | solution.py:375
  13.7 4.8 %collective-permute-start.5 = (bf16[16,1024]{1,0:T(8,128)(2,1)S(1)}, bf16[16,1024]{1,0:T(8,128)(2,1)S(1)}, u32[]{:S(2)}, u32[]{:S(2)}) collective-permute-start(bf16[16,1024]{1,0:T(8,128)(2,1)S(1)} %add_convert_fusion), channel_id=1, source_target_pairs={{0,16},{4,12},{8,4},{12,8},{16,0},{20,28},{24,20},{28,24},{1,17},{... | collective-permute-start | bytes 98312 | tf_op jit(solution)/shard_map/ppermute | solution.py:375

commit v5 on v4

--- a/solution.py
+++ b/solution.py
@@ -364,13 +364,13 @@
     return lax.ppermute(array, axis, [(i, i ^ bit) for i in range(lax.axis_size(axis))])
 
 
-def cycled(array, cycle):
+def cycled(array, cycle, crossing=()):
     fsdp_size, ctx_size = lax.axis_size("fsdp"), lax.axis_size("ctx")
     after = dict(zip(cycle, cycle[1:] + cycle[:1]))
     moves = []
     for core in range(fsdp_size):
         for place in range(ctx_size):
-            other = (core, after[place]) if place in after else (core ^ 1, place)
+            other = (core ^ (place in crossing), after[place]) if place in after else (core ^ 1, place)
             moves.append((core * ctx_size + place, other[0] * ctx_size + other[1]))
     return lax.ppermute(array, ("fsdp", "ctx"), moves)
 
@@ -493,8 +493,8 @@
     if four:
         both = state.astype(jnp.float32) + first_through * first.astype(jnp.float32)
         both = both.astype(half)
-        near = cycled(both, [1, 2, 3])
-        far = cycled(both, [1, 3, 2])
+        near = cycled(both, [1, 2, 3], (3,))
+        far = cycled(both, [1, 3, 2], (2,))
     else:
         near = far = entering_states(state, through)
     (part,) = call(local_kernel, [((tokens, width), jnp.float32)], gated, long, gain)

time: 19.6 us -> 19 us (0.969)
  the two profiles are of different devices: /device:TPU:24 before, /device:TPU:8 now
where the time goes in v5:
time: 19 us; the launch traced here: 18.7 us
  Pallas kernels  7.48 us (39%)
  starting transfers between devices  6.27 us (33%)
  waiting for transfers between devices  4.82 us (25%)
    pallas_call x8, Pallas kernels, call(): pl.pallas_call(kernel, out_shape=[jax.ShapeDtypeStruct(shape, dtype) for...  7.48 us
    ppermute x3, starting transfers between devices, exchanged(): lax.ppermute(array, axis, [(i, i ^ bit) for i in range(lax.axis_size(axis...  3.08 us
    ppermute x3, waiting for transfers between devices, cycled(): return lax.ppermute(array, ('fsdp', 'ctx'), moves)  2.99 us
    ppermute x3, starting transfers between devices, cycled(): return lax.ppermute(array, ('fsdp', 'ctx'), moves)  1.61 us
    ppermute x1, starting transfers between devices, body(): lax.ppermute(product, 'ctx', [(i, (i + 1) % ctx_size) for i in range(ctx_...  1.58 us
    ppermute x3, waiting for transfers between devices, exchanged(): lax.ppermute(array, axis, [(i, i ^ bit) for i in range(lax.axis_size(axis...  1.15 us
    ppermute x1, waiting for transfers between devices, body(): lax.ppermute(product, 'ctx', [(i, (i + 1) % ctx_size) for i in range(ctx_...  0.68 us
  transfers between devices with their start and end apart: 7, of which 5 were waited for; matrix products, arithmetic and copies ran while one was open for 0% of the time, Pallas kernels for 35%

profile of v5, /device:TPU:8, one launch (start us, length us, event | category | flops | bytes accessed | tf_op | source)
XLA Modules:
  0.0 18.7 jit_solution(8512318936032577366)
XLA Ops:
  0.0 0.0 collective-permute-start.1
  0.0 1.2 %shard_map.82 = (bf16[128,1024]{1,0:T(8,128)(2,1)S(1)}, bf16[16,256]{1,0:T(8,128)(2,1)S(1)}, bf16[128,1024]{1,0:T(8,128)(2,1)S(1)}, bf16[32,64]{1,0:T(8,128)(2,1...) custom-call(bf16[128,1024]{1,0:T(8,128)(2,1)} %bitcast.8, ...), custom_call_target="tpu_custom_call" | custom-call | flops 300000000 | tf_op jit(solution)/shard_map/pallas_call | solution.py:345
  1.2 1.6 %collective-permute-start.2 = (bf16[16,256]{1,0:T(8,128)(2,1)S(1)}, bf16[16,256]{1,0:T(8,128)(2,1)S(1)}, u32[]{:S(2)}, u32[]{:S(2)}) collective-permute-start(bf16[16,256]{1,0:T(8,128)(2,1)S(1)} %get-tuple-element.35), channel_id=1, source_target_pairs={{0,1},{1,0},{2,3},{3,2},{4,5},{5,4},{6,7},{7,6},{8,9},{9,8},{10,11... | collective-permute-start | bytes 24584 | tf_op jit(solution)/shard_map/ppermute | solution.py:364
  2.8 1.6 %collective-permute-start = (bf16[128,1024]{1,0:T(8,128)(2,1)S(1)}, bf16[128,1024]{1,0:T(8,128)(2,1)S(1)}, u32[]{:S(2)}, u32[]{:S(2)}) collective-permute-start(bf16[128,1024]{1,0:T(8,128)(2,1)S(1)} %get-tuple-element.28.product_ref), channel_id=1, source_target_pairs={{0,4},{4,8},{8,12},{12,0},{1,5},{5,9},{9,13},{13,1},{2,6},{6,10},{... | collective-permute-start | bytes 786440 | tf_op jit(solution)/shard_map/ppermute | solution.py:432
  4.4 0.6 %collective-permute-done.2 = bf16[16,256]{1,0:T(8,128)(2,1)S(1)} collective-permute-done((bf16[16,256]{1,0:T(8,128)(2,1)S(1)}, bf16[16,256]{1,0:T(8,128)(2,1)S(1)}, u32[]{:S(2)}, u32[]{:S(2)}) %collective-permute-start.2) | collective-permute-done | bytes 8224 | tf_op jit(solution)/shard_map/ppermute | solution.py:364
  4.9 1.5 %collective-permute-start.3 = (bf16[32,256]{1,0:T(8,128)(2,1)S(1)}, bf16[32,256]{1,0:T(8,128)(2,1)S(1)}, u32[]{:S(2)}, u32[]{:S(2)}) collective-permute-start(bf16[32,256]{1,0:T(8,128)(2,1)S(1)} %constant_dynamic-update-slice_fusion.modal_ref), channel_id=1, source_target_pairs={{0,2},{1,3},{2,0},{3,1},{4,6},{5,7},{6,4},{7,5},{8,10},{9,11},{10,... | collective-permute-start | bytes 49160 | tf_op jit(solution)/shard_map/ppermute | solution.py:364
  6.5 0.0 collective-permute-done.1.other_taps_ref
  6.5 0.9 %shard_map.83 = (bf16[64,128,128]{2,1,0:T(8,128)(2,1)S(1)}, bf16[64,128,128]{2,1,0:T(8,128)(2,1)S(1)}, bf16[128,128]{1,0:T(8,128)(2,1)S(1)}, f32[128,128]{1,0:T(8,128)S(1)}) custom-call(bf16[64,512]{1,0:T(8,128)(2,1)S(1)} %get-tuple-element.30.taps_ref, bf16[64,512]{1,0:T(8,128)(2,1)S(1)} %collective-permute-done.1.other_taps_ref, ...), custom_call_target="tpu_custom_call" | custom-call | flops 300000000 | tf_op jit(solution)/shard_map/pallas_call | solution.py:345
  7.4 0.7 %shard_map.84 = (f32[128,1024]{1,0:T(8,128)S(1)}, bf16[128,1024]{1,0:T(8,128)(2,1)S(1)}) custom-call(bf16[128,1024]{1,0:T(8,128)(2,1)S(1)} %get-tuple-element.28.product_ref, bf16[128,1024]{1,0:T(8,128)(2,1)S(1)} %get-tuple-element.29.query_ref, bf16[64,128,128]{2,1,0:T(8,128)(2,1)S(1)} %get-tuple-element.33.current_ref), custom_call_target="tpu_custom_call" | custom-call | flops 300000000 | tf_op jit(solution)/shard_map/pallas_call | solution.py:345
  8.1 0.6 %collective-permute-done.3.modal_rest_ref = bf16[32,256]{1,0:T(8,128)(2,1)S(1)} collective-permute-done((bf16[32,256]{1,0:T(8,128)(2,1)S(1)}, bf16[32,256]{1,0:T(8,128)(2,1)S(1)}, u32[]{:S(2)}, u32[]{:S(2)}) %collective-permute-start.3) | collective-permute-done | bytes 16416 | tf_op jit(solution)/shard_map/ppermute | solution.py:364
  8.7 0.6 %shard_map.85 = (bf16[128,1024]{1,0:T(8,128)(2,1)S(1)}, f32[32,1024]{1,0:T(8,128)S(1)}, bf16[16,1024]{1,0:T(8,128)(2,1)S(1)}) custom-call(bf16[32,256]{1,0:T(8,128)(2,1)S(1)} %constant_dynamic-update-slice_fusion.modal_ref, bf16[32,256]{1,0:T(8,128)(2,1)S(1)} %collective-permute-done.3.modal_rest_ref, bf16[32,64]{1,0:T(8,128)(2,1)S(1)} %get-tuple-element.36.select_ref, ...), custom_call_target="tpu_custom_call" | custom-call | flops 300000000 | tf_op jit(solution)/shard_map/pallas_call | solution.py:345
  9.3 0.1 collective-permute-start.4
  9.4 1.5 %shard_map.86 = (bf16[64,128,128]{2,1,0:T(8,128)(2,1)S(1)}, bf16[128,1024]{1,0:T(8,128)(2,1)S(1)}, f32[16,1024]{1,0:T(8,128)}, f32[16,1024]{1,0:T(8,128)S(1)}, f32[16,1024]{1,0:T(8,128)S(1)}) custom-call(f32[32,1024]{1,0:T(8,128)S(1)} %get-tuple-element.41.channels_ref, s32[1,512]{1,0:T(1,128)S(1)} %get-tuple-element.31.starts_ref, ...), custom_call_target="tpu_custom_call" | custom-call | flops 300000000 | tf_op jit(solution)/shard_map/pallas_call | solution.py:345
  10.9 0.7 %collective-permute-done.halo_ref = bf16[128,1024]{1,0:T(8,128)(2,1)S(1)} collective-permute-done((bf16[128,1024]{1,0:T(8,128)(2,1)S(1)}, bf16[128,1024]{1,0:T(8,128)(2,1)S(1)}, u32[]{:S(2)}, u32[]{:S(2)}) %collective-permute-start) | collective-permute-done | bytes 262176 | tf_op jit(solution)/shard_map/ppermute | solution.py:432
  11.6 0.9 %shard_map.87 = (bf16[128,1024]{1,0:T(8,128)(2,1)S(1)}, bf16[16,1024]{1,0:T(8,128)(2,1)S(1)}) custom-call(bf16[128,1024]{1,0:T(8,128)(2,1)S(1)} %collective-permute-done.halo_ref, bf16[128,1024]{1,0:T(8,128)(2,1)S(1)} %get-tuple-element.29.query_ref, bf16[64,128,128]{2,1,0:T(8,128)(2,1)S(1)} %get-tuple-element.32.previous_ref, ...), custom_call_target="tpu_custom_call" | custom-call | flops 300000000 | tf_op jit(solution)/shard_map/pallas_call | solution.py:345
  12.4 0.8 %collective-permute-done.4.first_ref = bf16[16,1024]{1,0:T(8,128)(2,1)S(1)} collective-permute-done((bf16[16,1024]{1,0:T(8,128)(2,1)S(1)}, bf16[16,1024]{1,0:T(8,128)(2,1)S(1)}, u32[]{:S(2)}, u32[]{:S(2)}) %collective-permute-start.4) | collective-permute-done | bytes 32800 | tf_op jit(solution)/shard_map/ppermute | solution.py:375
  13.3 0.5 %collective-permute-start.6 = (bf16[16,1024]{1,0:T(8,128)(2,1)S(1)}, bf16[16,1024]{1,0:T(8,128)(2,1)S(1)}, u32[]{:S(2)}, u32[]{:S(2)}) collective-permute-start(bf16[16,1024]{1,0:T(8,128)(2,1)S(1)} %add_convert_fusion), channel_id=1, source_target_pairs={{0,16},{4,8},{8,12},{12,20},{16,0},{20,24},{24,28},{28,4},{1,17},{... | collective-permute-start | bytes 98312 | tf_op jit(solution)/shard_map/ppermute | solution.py:375
  13.8 1.1 %collective-permute-start.5 = (bf16[16,1024]{1,0:T(8,128)(2,1)S(1)}, bf16[16,1024]{1,0:T(8,128)(2,1)S(1)}, u32[]{:S(2)}, u32[]{:S(2)}) collective-permute-start(bf16[16,1024]{1,0:T(8,128)(2,1)S(1)} %add_convert_fusion), channel_id=1, source_target_pairs={{0,16},{4,12},{8,20},{12,8},{16,0},{20,28},{24,4},{28,24},{1,17},{... | collective-permute-start | bytes 98312 | tf_op jit(solution)/shard_map/ppermute | solution.py:375
  14.9 0.7 %shard_map.88.part_ref = f32[128,1024]{1,0:T(8,128)S(1)} custom-call(bf16[128,1024]{1,0:T(8,128)(2,1)S(1)} %get-tuple-element.44.gated_ref, bf16[64,128,128]{2,1,0:T(8,128)(2,1)S(1)} %get-tuple-element.45.long_ref, f32[1,1024]{1,0:T(1,128)S(1)} %get-tuple-element.46.gain_ref), custom_call_target="tpu_custom_call" | custom-call | flops 300000000 | tf_op jit(solution)/shard_map/pallas_call | solution.py:345
  15.6 2.1 %collective-permute-done.6.near_ref = bf16[16,1024]{1,0:T(8,128)(2,1)S(1)} collective-permute-done((bf16[16,1024]{1,0:T(8,128)(2,1)S(1)}, bf16[16,1024]{1,0:T(8,128)(2,1)S(1)}, u32[]{:S(2)}, u32[]{:S(2)}) %collective-permute-start.6) | collective-permute-done | bytes 32800 | tf_op jit(solution)/shard_map/ppermute | solution.py:375
  17.7 0.0 collective-permute-done.5.far_ref
  17.7 0.9 %shard_map.89 = bf16[128,1024]{1,0:T(8,128)(2,1)} custom-call(f32[128,1024]{1,0:T(8,128)S(1)} %shard_map.88.part_ref, bf16[128,1024]{1,0:T(8,128)(2,1)S(1)} %get-tuple-element.43._.carry_ref, bf16[16,1024]{1,0:T(8,128)(2,1)S(1)} %collective-permute-done.4.first_ref, bf16[16,1024]{1,0:T(8,128)(2,1)S(1)} %collective-permute-done.5.far_ref, ...), custom_call_target="tpu_custom_call" | custom-call | flops 300000000 | tf_op jit(solution)/shard_map/pallas_call | solution.py:345
  (3 shorter events, 0.0 us)
Async XLA Ops:
  0.0 6.5 %collective-permute-start.1 = (bf16[64,512]{1,0:T(8,128)(2,1)}, bf16[64,512]{1,0:T(8,128)(2,1)S(1)}, u32[]{:S(2)}, u32[]{:S(2)}) collective-permute-start(bf16[64,512]{1,0:T(8,128)(2,1)} %bitcast.11), channel_id=1, source_target_pairs={{0,16},{16,0},{1,17},{17,1},{2,18},{18,2},{3,19},{19,3},{4,20},{20... | collective-permute-start | bytes 196616 | tf_op jit(solution)/shard_map/ppermute | solution.py:364
  1.2 3.7 %collective-permute-start.2 = (bf16[16,256]{1,0:T(8,128)(2,1)S(1)}, bf16[16,256]{1,0:T(8,128)(2,1)S(1)}, u32[]{:S(2)}, u32[]{:S(2)}) collective-permute-start(bf16[16,256]{1,0:T(8,128)(2,1)S(1)} %get-tuple-element.35), channel_id=1, source_target_pairs={{0,1},{1,0},{2,3},{3,2},{4,5},{5,4},{6,7},{7,6},{8,9},{9,8},{10,11... | collective-permute-start | bytes 24584 | tf_op jit(solution)/shard_map/ppermute | solution.py:364
  2.8 8.8 %collective-permute-start = (bf16[128,1024]{1,0:T(8,128)(2,1)S(1)}, bf16[128,1024]{1,0:T(8,128)(2,1)S(1)}, u32[]{:S(2)}, u32[]{:S(2)}) collective-permute-start(bf16[128,1024]{1,0:T(8,128)(2,1)S(1)} %get-tuple-element.28.product_ref), channel_id=1, source_target_pairs={{0,4},{4,8},{8,12},{12,0},{1,5},{5,9},{9,13},{13,1},{2,6},{6,10},{... | collective-permute-start | bytes 786440 | tf_op jit(solution)/shard_map/ppermute | solution.py:432
  4.9 3.7 %collective-permute-start.3 = (bf16[32,256]{1,0:T(8,128)(2,1)S(1)}, bf16[32,256]{1,0:T(8,128)(2,1)S(1)}, u32[]{:S(2)}, u32[]{:S(2)}) collective-permute-start(bf16[32,256]{1,0:T(8,128)(2,1)S(1)} %constant_dynamic-update-slice_fusion.modal_ref), channel_id=1, source_target_pairs={{0,2},{1,3},{2,0},{3,1},{4,6},{5,7},{6,4},{7,5},{8,10},{9,11},{10,... | collective-permute-start | bytes 49160 | tf_op jit(solution)/shard_map/ppermute | solution.py:364
  9.3 4.0 %collective-permute-start.4 = (bf16[16,1024]{1,0:T(8,128)(2,1)S(1)}, bf16[16,1024]{1,0:T(8,128)(2,1)S(1)}, u32[]{:S(2)}, u32[]{:S(2)}) collective-permute-start(bf16[16,1024]{1,0:T(8,128)(2,1)S(1)} %get-tuple-element.47), channel_id=1, source_target_pairs={{0,4},{4,0},{8,24},{12,28},{16,20},{20,16},{24,8},{28,12},{1,5},{5... | collective-permute-start | bytes 98312 | tf_op jit(solution)/shard_map/ppermute | solution.py:375
  13.3 4.4 %collective-permute-start.6 = (bf16[16,1024]{1,0:T(8,128)(2,1)S(1)}, bf16[16,1024]{1,0:T(8,128)(2,1)S(1)}, u32[]{:S(2)}, u32[]{:S(2)}) collective-permute-start(bf16[16,1024]{1,0:T(8,128)(2,1)S(1)} %add_convert_fusion), channel_id=1, source_target_pairs={{0,16},{4,8},{8,12},{12,20},{16,0},{20,24},{24,28},{28,4},{1,17},{... | collective-permute-start | bytes 98312 | tf_op jit(solution)/shard_map/ppermute | solution.py:375
  13.8 3.9 %collective-permute-start.5 = (bf16[16,1024]{1,0:T(8,128)(2,1)S(1)}, bf16[16,1024]{1,0:T(8,128)(2,1)S(1)}, u32[]{:S(2)}, u32[]{:S(2)}) collective-permute-start(bf16[16,1024]{1,0:T(8,128)(2,1)S(1)} %add_convert_fusion), channel_id=1, source_target_pairs={{0,16},{4,12},{8,20},{12,8},{16,0},{20,28},{24,4},{28,24},{1,17},{... | collective-permute-start | bytes 98312 | tf_op jit(solution)/shard_map/ppermute | solution.py:375

commit v6 on v5

--- a/solution.py
+++ b/solution.py
@@ -33,6 +33,7 @@
     modal_ref,
     spread_ref,
     select_ref,
+    rates_ref,
     query_ref,
     taps_ref,
     starts_ref,
@@ -69,6 +70,12 @@
     owner = jnp.bitwise_xor(dp_place, line // 16)
     wanted = owner * per_part + held == jnp.where(mode < modes, mode, mode - modes)
     select_ref[...] = ((held >= 0) & (held < per_part) & wanted).astype(jnp.bfloat16)
+    line, mode = iota((lines, width), 0), iota((lines, width), 1) % modes
+    within = line % 16
+    owner = jnp.bitwise_xor(dp_place, line // 16)
+    rates_ref[...] = ((within < per_part) & (owner * per_part + within == mode)).astype(
+        jnp.float32
+    )
     first = dp_place * (width // modes) % LANES
     spread_ref[...] = (
         iota((LANES, width), 0) == first + iota((LANES, width), 1) // modes
@@ -183,17 +190,47 @@
 
 
 def own_kernel(product_ref, query_ref, current_ref, medium_ref, gated_ref):
-    per_slab = LANES // GROUP_CH
     for slab, lanes in enumerate(slabs_of(product_ref.shape[1])):
-        medium = grouped(
-            current_ref[slab * per_slab : (slab + 1) * per_slab], product_ref[:, lanes]
-        )
+        medium = grouped(stored_halves(current_ref, slab), product_ref[:, lanes])
         medium_ref[:, lanes] = medium
         gated_ref[:, lanes] = gated_by(query_ref[:, lanes], medium)
 
 
 def on_line(modes, width):
     return iota((modes, width), 0) == iota((modes, width), 1) % modes
+
+
+def modal_parts(modal_refs, spread_ref, groups):
+    first = lax.axis_index("dp") * groups
+    base = pl.multiple_of(first // LANES * LANES, LANES)
+    pieces = jnp.concatenate([ref[:, pl.ds(base, LANES)] for ref in modal_refs], axis=0)
+    return dot(pieces, spread_ref[...])
+
+
+def end_weights(lines, rates_ref, doc_ref, end_ref):
+    block, width = end_ref.shape
+    rate_line = jnp.sum(lines * rates_ref[...], axis=0, keepdims=True)
+    left = (block - 1 - iota((block, LANES), 0)).astype(jnp.float32)
+    keeps = doc_ref[...] == doc_ref[block - 1 : block, :]
+    for lanes in slabs_of(width):
+        weight = jnp.exp(-rate_line[:, lanes] * left)
+        end_ref[:, lanes] = jnp.where(keeps, weight, 0.0).astype(jnp.bfloat16)
+
+
+def first_kernel(
+    modal_ref, modal_rest_ref, spread_ref, rates_ref, doc_ref, gated_ref, state_ref, end_ref
+):
+    modes, width = state_ref.shape
+
+    @pl.when(lax.axis_index("ctx") == 0)
+    def _():
+        lines = modal_parts([modal_ref, modal_rest_ref], spread_ref, width // modes)
+        end_weights(lines, rates_ref, doc_ref, end_ref)
+        end_states(end_ref, gated_ref, state_ref)
+
+    @pl.when(lax.axis_index("ctx") != 0)
+    def _():
+        state_ref[...] = jnp.zeros_like(state_ref)
 
 
 def modal_kernel(
@@ -201,76 +238,42 @@
     modal_rest_ref,
     select_ref,
     spread_ref,
+    rates_ref,
     doc_ref,
-    gated_ref,
+    _,
     end_ref,
     channels_ref,
-    state_ref,
-):
-    block, width = end_ref.shape
-    modes = state_ref.shape[0]
-    first = lax.axis_index("dp") * (width // modes)
-    base = pl.multiple_of(first // LANES * LANES, LANES)
-    pieces = jnp.concatenate(
-        [modal_ref[:, pl.ds(base, LANES)], modal_rest_ref[:, pl.ds(base, LANES)]], axis=0
-    )
-    ordered = dot(select_ref[...], pieces)
-    by_channel = dot(ordered.astype(jnp.bfloat16), spread_ref[...])
-    channels_ref[...] = by_channel
-    rate_line = jnp.sum(
-        jnp.where(on_line(modes, width), by_channel[:modes], 0.0), axis=0, keepdims=True
-    )
-    left = (block - 1 - iota((block, LANES), 0)).astype(jnp.float32)
-    keeps = doc_ref[...] == doc_ref[block - 1 : block, :]
-    for lanes in slabs_of(width):
-        weight = jnp.exp(-rate_line[:, lanes] * left)
-        end_ref[:, lanes] = jnp.where(keeps, weight, 0.0).astype(jnp.bfloat16)
-    end_states(end_ref, gated_ref, state_ref)
-
-
-def long_kernel(
-    channels_ref,
-    starts_ref,
-    same_ref,
-    doc_ref,
-    long_ref,
-    carry_ref,
-    through_ref,
-    first_ref,
-    far_ref,
-    rows_ref,
-):
-    groups, block = long_ref.shape[0], long_ref.shape[1]
-    modes, width = through_ref.shape
-    ctx_place = lax.axis_index("ctx")
+):
+    modes, width = channels_ref.shape[0] // 2, channels_ref.shape[1]
+    lines = modal_parts([modal_ref, modal_rest_ref], spread_ref, width // modes)
+    end_weights(lines, rates_ref, doc_ref, end_ref)
+    channels_ref[...] = dot(select_ref[...], lines.astype(jnp.bfloat16))
+
+
+def modal_lines(channels_ref, modes, width):
     rate = channels_ref[:modes]
     scaled = channels_ref[modes:] * jnp.sqrt((1.0 - jnp.exp(-2.0 * rate)) / modes)
     chosen = on_line(modes, width)
-    rate_line = jnp.sum(jnp.where(chosen, rate, 0.0), axis=0, keepdims=True)
-    scaled_line = jnp.sum(jnp.where(chosen, scaled, 0.0), axis=0, keepdims=True)
+    return [
+        jnp.sum(jnp.where(chosen, part, 0.0), axis=0, keepdims=True) for part in (rate, scaled)
+    ]
+
+
+def response_kernel(channels_ref, starts_ref, rows_ref, through_ref, first_ref, far_ref):
+    groups, block = rows_ref.shape
+    modes, width = through_ref.shape
+    ctx_place = lax.axis_index("ctx")
+    rate_line, scaled_line = modal_lines(channels_ref, modes, width)
     lag = ((block - iota((block, LANES), 0)) % block).astype(jnp.float32)
-    response = jnp.zeros((groups, block), jnp.float32)
-    for lanes in slabs_of(width):
+    per_slab = LANES // modes
+    gather = (iota((LANES, LANES), 0) // modes == iota((LANES, LANES), 1)).astype(jnp.bfloat16)
+    for slab, lanes in enumerate(slabs_of(width)):
         terms = scaled_line[:, lanes] * jnp.exp(-rate_line[:, lanes] * lag)
         high = terms.astype(jnp.bfloat16)
         low = (terms - high.astype(jnp.float32)).astype(jnp.bfloat16)
-        member = (
-            iota((groups, LANES), 0) == (lanes.start + iota((groups, LANES), 1)) // modes
-        ).astype(jnp.bfloat16)
-        response += dot(member, high, ((1,), (1,))) + dot(member, low, ((1,), (1,)))
-    rows_ref[...] = response
-    since = (iota((block, LANES), 0) + 1).astype(jnp.float32)
-    continues = doc_ref[...] == 0.0
-    for lanes in slabs_of(width):
-        weight = scaled_line[:, lanes] * jnp.exp(-rate_line[:, lanes] * since)
-        carry_ref[:, lanes] = jnp.where(continues, weight, 0.0).astype(jnp.bfloat16)
-    halves = [slice(0, block // 2), slice(block // 2, block)]
-    same = [same_ref[rows, :] for rows in halves]
-    for group in range(groups):
-        turned = circulant(rows_ref[group : group + 1, :], block)
-        for part, rows in enumerate(halves):
-            long_ref[group, rows, :] = turned * same[part]
-    decay = jnp.exp(-rate * block)
+        sums = jnp.transpose(dot(high, gather) + dot(low, gather))
+        rows_ref[slab * per_slab : (slab + 1) * per_slab, :] = sums[:per_slab]
+    decay = jnp.exp(-channels_ref[:modes] * block)
     own, prior = block_starts(starts_ref, ctx_place, block)
     none_own = jnp.sum(own, axis=1, keepdims=True) == 0.0
     none_prior = jnp.sum(prior, axis=1, keepdims=True) == 0.0
@@ -279,47 +282,65 @@
     far_ref[...] = jnp.where(none_prior, decay, 0.0)
 
 
-def grouped(matrices, values):
-    count, rows, _ = matrices.shape
+def grouped(halves, values):
+    rows = values.shape[0]
     half = rows // 2
     lane = iota((half, LANES), 1) // GROUP_CH
     results = []
-    for part in range(2):
+    for part, chosen in enumerate(halves):
         turned = values if part == 0 else jnp.concatenate([values[half:], values[:half]], axis=0)
-        chosen = matrices[:, part * half : (part + 1) * half].reshape(count * half, rows)
         product = dot(chosen, turned)
         result = product[:half]
-        for k in range(1, count):
+        for k in range(1, chosen.shape[0] // half):
             result = jnp.where(lane == k, product[k * half : (k + 1) * half], result)
         results.append(result)
     return jnp.concatenate(results, axis=0)
 
 
+def stored_halves(matrices_ref, slab):
+    per_slab = LANES // GROUP_CH
+    groups = slice(slab * per_slab, (slab + 1) * per_slab)
+    half = matrices_ref.shape[1] // 2
+    return [
+        matrices_ref[groups, part * half : (part + 1) * half].reshape(per_slab * half, 2 * half)
+        for part in range(2)
+    ]
+
+
 def gate_kernel(
     halo_ref, query_ref, previous_ref, medium_ref, end_ref, _, gated_ref, state_ref
 ):
-    per_slab = LANES // GROUP_CH
     for slab, lanes in enumerate(slabs_of(halo_ref.shape[1])):
         medium = medium_ref[:, lanes] + grouped(
-            previous_ref[slab * per_slab : (slab + 1) * per_slab], halo_ref[:, lanes]
+            stored_halves(previous_ref, slab), halo_ref[:, lanes]
         )
         gated_ref[:, lanes] = gated_by(query_ref[:, lanes], medium)
     end_states(end_ref, gated_ref, state_ref)
 
 
-def local_kernel(gated_ref, long_ref, gain_ref, part_ref):
-    width = gated_ref.shape[1]
+def local_kernel(gated_ref, rows_ref, same_ref, doc_ref, channels_ref, gain_ref, part_ref, carry_ref):
+    block, width = part_ref.shape
+    modes = channels_ref.shape[0] // 2
     per_slab = LANES // GROUP_CH
-    for slab in range(width // LANES):
-        lanes = slice(slab * LANES, (slab + 1) * LANES)
+    half = block // 2
+    same = [same_ref[:half, :], same_ref[half:, :]]
+    rate_line, scaled_line = modal_lines(channels_ref, modes, width)
+    since = (iota((block, LANES), 0) + 1).astype(jnp.float32)
+    continues = doc_ref[...] == 0.0
+    for slab, lanes in enumerate(slabs_of(width)):
+        turned = [
+            circulant(rows_ref[group : group + 1, :], block)
+            for group in range(slab * per_slab, (slab + 1) * per_slab)
+        ]
+        halves = [jnp.concatenate([line * mask for line in turned], axis=0) for mask in same]
         gated = gated_ref[:, lanes]
-        part_ref[:, lanes] = grouped(
-            long_ref[slab * per_slab : (slab + 1) * per_slab], gated
-        ) + gain_ref[:, lanes] * gated.astype(jnp.float32)
+        part_ref[:, lanes] = grouped(halves, gated) + gain_ref[:, lanes] * gated.astype(jnp.float32)
+        weight = scaled_line[:, lanes] * jnp.exp(-rate_line[:, lanes] * since)
+        carry_ref[:, lanes] = jnp.where(continues, weight, 0.0).astype(jnp.bfloat16)
 
 
 def finish_kernel(
-    four, part_ref, carry_ref, first_ref, far_ref, near_ref, through_ref, out_ref
+    four, part_ref, carry_ref, first_ref, near_ref, far_ref, through_ref, out_ref
 ):
     width = part_ref.shape[1]
     modes = near_ref.shape[0]
@@ -415,13 +436,14 @@
         document_starts,
         skip_gain.reshape(1, width),
     ]
-    product, modal, spread, select, query, own_taps, starts, gain = call(
+    product, modal, spread, select, rates, query, own_taps, starts, gain = call(
         prepare_kernel,
         [
             ((tokens, width), half),
             ((16, rows), half),
             ((LANES, width), half),
             ((2 * modes, 16 * dp_size), half),
+            ((16 * dp_size, width), jnp.float32),
         ]
         + [(a.shape, a.dtype) for a in inputs[4:]],
         *[pltpu.with_memory_space_constraint(a, pltpu.HBM) for a in inputs],
@@ -453,32 +475,35 @@
         current,
     )
     states = ((modes, width), jnp.float32)
-    end, channels, state_own = call(
+    (state_own,) = call(
+        first_kernel,
+        [((modes, width), half)],
+        modal,
+        modal_rest,
+        spread,
+        rates,
+        documents,
+        gated_own,
+        scratch=[pltpu.VMEM((tokens, width), half)],
+    )
+    end, channels = call(
         modal_kernel,
-        [
-            ((tokens, width), half),
-            ((2 * modes, width), jnp.float32),
-            ((modes, width), half),
-        ],
+        [((tokens, width), half), ((2 * modes, width), jnp.float32)],
         modal,
         modal_rest,
         select,
         spread,
+        rates,
         documents,
-        gated_own,
+        state_own,
     )
     four = ctx_size == 4
     first = cycled(state_own, [0, 1]) if four else state_own
-    long, carry, through, first_through, far_through = call(
-        long_kernel,
-        [square, ((tokens, width), half), states, states, states],
+    response, through, first_through, far_through = call(
+        response_kernel,
+        [((groups, tokens), jnp.float32), states, states, states],
         channels,
         starts,
-        same,
-        documents,
-        scratch=[
-            pltpu.VMEM((groups, tokens), jnp.float32),
-        ],
     )
     gated, state = call(
         gate_kernel,
@@ -488,24 +513,33 @@
         previous,
         medium,
         end,
-        carry,
+        response,
     )
     if four:
         both = state.astype(jnp.float32) + first_through * first.astype(jnp.float32)
         both = both.astype(half)
-        near = cycled(both, [1, 2, 3], (3,))
-        far = cycled(both, [1, 3, 2], (2,))
+        near = cycled(both, [1, 2, 3], (3, ))
+        far = cycled(both, [1, 3, 2], (3, ))
     else:
         near = far = entering_states(state, through)
-    (part,) = call(local_kernel, [((tokens, width), jnp.float32)], gated, long, gain)
+    part, carry = call(
+        local_kernel,
+        [((tokens, width), jnp.float32), ((tokens, width), half)],
+        gated,
+        response,
+        same,
+        documents,
+        channels,
+        gain,
+    )
     (out,) = call(
         functools.partial(finish_kernel, four),
         [((tokens, width), half)],
         part,
         carry,
         first,
+        near,
         far,
-        near,
         far_through,
     )
     return out[None]

time: 19 us -> 18.8 us (0.989); the launches traced: 18.7 us -> 18.6 us
  starting transfers between devices: 6.27 us -> 7.43 us
  Pallas kernels: 7.48 us -> 6.81 us
  waiting for transfers between devices: 4.82 us -> 4.33 us
    ppermute x3, starting transfers between devices: 1.61 us -> 2.78 us  [cycled(): return lax.ppermute(array, ('fsdp', 'ctx'), moves)]
    ppermute x3, waiting for transfers between devices: 2.99 us -> 2.07 us  [cycled(): return lax.ppermute(array, ('fsdp', 'ctx'), moves)]
    pallas_call x8 -> x9, Pallas kernels: 7.48 us -> 6.81 us  [call(): pl.pallas_call(kernel, out_shape=[jax.ShapeDtypeStruct(shape, dtype) for...]
    ppermute x1, waiting for transfers between devices: 0.68 us -> 1.12 us  [body(): lax.ppermute(product, 'ctx', [(i, (i + 1) % ctx_size) for i in range(ctx_...]
  transfers between devices with their start and end apart: 7 -> 7, of which waited for: 5 -> 6; matrix products, arithmetic and copies ran while one was open for 0% -> 0% of each run, Pallas kernels for 35% -> 32%
where the time goes in v6:
time: 18.8 us; the launch traced here: 18.6 us
  starting transfers between devices  7.43 us (40%)
  Pallas kernels  6.81 us (36%)
  waiting for transfers between devices  4.33 us (23%)
    pallas_call x9, Pallas kernels, call(): pl.pallas_call(kernel, out_shape=[jax.ShapeDtypeStruct(shape, dtype) for...  6.81 us
    ppermute x3, starting transfers between devices, exchanged(): lax.ppermute(array, axis, [(i, i ^ bit) for i in range(lax.axis_size(axis...  3.08 us
    ppermute x3, starting transfers between devices, cycled(): return lax.ppermute(array, ('fsdp', 'ctx'), moves)  2.78 us
    ppermute x3, waiting for transfers between devices, cycled(): return lax.ppermute(array, ('fsdp', 'ctx'), moves)  2.07 us
    ppermute x1, starting transfers between devices, body(): lax.ppermute(product, 'ctx', [(i, (i + 1) % ctx_size) for i in range(ctx_...  1.58 us
    ppermute x3, waiting for transfers between devices, exchanged(): lax.ppermute(array, axis, [(i, i ^ bit) for i in range(lax.axis_size(axis...  1.14 us
    ppermute x1, waiting for transfers between devices, body(): lax.ppermute(product, 'ctx', [(i, (i + 1) % ctx_size) for i in range(ctx_...  1.12 us
  transfers between devices with their start and end apart: 7, of which 6 were waited for; matrix products, arithmetic and copies ran while one was open for 0% of the time, Pallas kernels for 32%

profile of v6, /device:TPU:8, one launch (start us, length us, event | category | flops | bytes accessed | tf_op | source)
XLA Modules:
  0.0 18.6 jit_solution(1223412716404621775)
XLA Ops:
  0.0 0.0 collective-permute-start.1
  0.0 1.2 %shard_map.82 = (bf16[128,1024]{1,0:T(8,128)(2,1)S(1)}, bf16[16,256]{1,0:T(8,128)(2,1)S(1)}, bf16[128,1024]{1,0:T(8,128)(2,1)S(1)}, bf16[32,64]{1,0:T(8,128)(2,1...) custom-call(bf16[128,1024]{1,0:T(8,128)(2,1)} %bitcast.8, ...), custom_call_target="tpu_custom_call" | custom-call | flops 300000000 | tf_op jit(solution)/shard_map/pallas_call | solution.py:366
  1.2 1.6 %collective-permute-start.2 = (bf16[16,256]{1,0:T(8,128)(2,1)S(1)}, bf16[16,256]{1,0:T(8,128)(2,1)S(1)}, u32[]{:S(2)}, u32[]{:S(2)}) collective-permute-start(bf16[16,256]{1,0:T(8,128)(2,1)S(1)} %get-tuple-element.36), channel_id=1, source_target_pairs={{0,1},{1,0},{2,3},{3,2},{4,5},{5,4},{6,7},{7,6},{8,9},{9,8},{10,11... | collective-permute-start | bytes 24584 | tf_op jit(solution)/shard_map/ppermute | solution.py:385
  2.8 1.6 %collective-permute-start = (bf16[128,1024]{1,0:T(8,128)(2,1)S(1)}, bf16[128,1024]{1,0:T(8,128)(2,1)S(1)}, u32[]{:S(2)}, u32[]{:S(2)}) collective-permute-start(bf16[128,1024]{1,0:T(8,128)(2,1)S(1)} %get-tuple-element.29.product_ref), channel_id=1, source_target_pairs={{0,4},{4,8},{8,12},{12,0},{1,5},{5,9},{9,13},{13,1},{2,6},{6,10},{... | collective-permute-start | bytes 786440 | tf_op jit(solution)/shard_map/ppermute | solution.py:454
  4.4 0.6 %collective-permute-done.2 = bf16[16,256]{1,0:T(8,128)(2,1)S(1)} collective-permute-done((bf16[16,256]{1,0:T(8,128)(2,1)S(1)}, bf16[16,256]{1,0:T(8,128)(2,1)S(1)}, u32[]{:S(2)}, u32[]{:S(2)}) %collective-permute-start.2) | collective-permute-done | bytes 8224 | tf_op jit(solution)/shard_map/ppermute | solution.py:385
  4.9 1.5 %collective-permute-start.3 = (bf16[32,256]{1,0:T(8,128)(2,1)S(1)}, bf16[32,256]{1,0:T(8,128)(2,1)S(1)}, u32[]{:S(2)}, u32[]{:S(2)}) collective-permute-start(bf16[32,256]{1,0:T(8,128)(2,1)S(1)} %constant_dynamic-update-slice_fusion.modal_ref), channel_id=1, source_target_pairs={{0,2},{1,3},{2,0},{3,1},{4,6},{5,7},{6,4},{7,5},{8,10},{9,11},{10,... | collective-permute-start | bytes 49160 | tf_op jit(solution)/shard_map/ppermute | solution.py:385
  6.5 0.0 collective-permute-done.1.other_taps_ref
  6.5 0.9 %shard_map.83 = (bf16[64,128,128]{2,1,0:T(8,128)(2,1)S(1)}, bf16[64,128,128]{2,1,0:T(8,128)(2,1)S(1)}, bf16[128,128]{1,0:T(8,128)(2,1)S(1)}, f32[128,128]{1,0:T(8,128)S(1)}) custom-call(bf16[64,512]{1,0:T(8,128)(2,1)S(1)} %get-tuple-element.31.taps_ref, bf16[64,512]{1,0:T(8,128)(2,1)S(1)} %collective-permute-done.1.other_taps_ref, ...), custom_call_target="tpu_custom_call" | custom-call | flops 300000000 | tf_op jit(solution)/shard_map/pallas_call | solution.py:366
  7.4 0.7 %shard_map.84 = (f32[128,1024]{1,0:T(8,128)S(1)}, bf16[128,1024]{1,0:T(8,128)(2,1)S(1)}) custom-call(bf16[128,1024]{1,0:T(8,128)(2,1)S(1)} %get-tuple-element.29.product_ref, bf16[128,1024]{1,0:T(8,128)(2,1)S(1)} %get-tuple-element.30.query_ref, bf16[64,128,128]{2,1,0:T(8,128)(2,1)S(1)} %get-tuple-element.34.current_ref), custom_call_target="tpu_custom_call" | custom-call | flops 300000000 | tf_op jit(solution)/shard_map/pallas_call | solution.py:366
  8.1 0.6 %collective-permute-done.3.modal_rest_ref = bf16[32,256]{1,0:T(8,128)(2,1)S(1)} collective-permute-done((bf16[32,256]{1,0:T(8,128)(2,1)S(1)}, bf16[32,256]{1,0:T(8,128)(2,1)S(1)}, u32[]{:S(2)}, u32[]{:S(2)}) %collective-permute-start.3) | collective-permute-done | bytes 16416 | tf_op jit(solution)/shard_map/ppermute | solution.py:385
  8.7 0.5 %collective-permute-start.4 = (bf16[16,1024]{1,0:T(8,128)(2,1)S(1)}, bf16[16,1024]{1,0:T(8,128)(2,1)S(1)}, u32[]{:S(2)}, u32[]{:S(2)}) collective-permute-start(bf16[16,1024]{1,0:T(8,128)(2,1)S(1)} %shard_map.85._), channel_id=1, source_target_pairs={{0,4},{4,0},{8,24},{12,28},{16,20},{20,16},{24,8},{28,12},{1,5},{5... | collective-permute-start | bytes 98312 | tf_op jit(solution)/shard_map/ppermute | solution.py:396
  9.2 0.4 %shard_map.86 = (bf16[128,1024]{1,0:T(8,128)(2,1)S(1)}, f32[32,1024]{1,0:T(8,128)S(1)}) custom-call(bf16[32,256]{1,0:T(8,128)(2,1)S(1)} %constant_dynamic-update-slice_fusion.modal_ref, bf16[32,256]{1,0:T(8,128)(2,1)S(1)} %collective-permute-done.3.modal_rest_ref, bf16[32,64]{1,0:T(8,128)(2,1)S(1)} %get-tuple-element.37.select_ref, ...), custom_call_target="tpu_custom_call" | custom-call | flops 300000000 | tf_op jit(solution)/shard_map/pallas_call | solution.py:366
  9.6 0.9 %shard_map.87 = (f32[64,128]{1,0:T(8,128)S(1)}, f32[16,1024]{1,0:T(8,128)}, f32[16,1024]{1,0:T(8,128)S(1)}, f32[16,1024]{1,0:T(8,128)S(1)}) custom-call(f32[32,1024]{1,0:T(8,128)S(1)} %get-tuple-element.43.channels_ref, s32[1,512]{1,0:T(1,128)S(1)} %get-tuple-element.32.starts_ref), custom_call_target="tpu_custom_call" | custom-call | flops 300000000 | tf_op jit(solution)/shard_map/pallas_call | solution.py:366
  10.5 1.1 %collective-permute-done.halo_ref = bf16[128,1024]{1,0:T(8,128)(2,1)S(1)} collective-permute-done((bf16[128,1024]{1,0:T(8,128)(2,1)S(1)}, bf16[128,1024]{1,0:T(8,128)(2,1)S(1)}, u32[]{:S(2)}, u32[]{:S(2)}) %collective-permute-start) | collective-permute-done | bytes 262176 | tf_op jit(solution)/shard_map/ppermute | solution.py:454
  11.6 0.9 %shard_map.88 = (bf16[128,1024]{1,0:T(8,128)(2,1)S(1)}, bf16[16,1024]{1,0:T(8,128)(2,1)S(1)}) custom-call(bf16[128,1024]{1,0:T(8,128)(2,1)S(1)} %collective-permute-done.halo_ref, bf16[128,1024]{1,0:T(8,128)(2,1)S(1)} %get-tuple-element.30.query_ref, bf16[64,128,128]{2,1,0:T(8,128)(2,1)S(1)} %get-tuple-element.33.previous_ref, ...), custom_call_target="tpu_custom_call" | custom-call | flops 300000000 | tf_op jit(solution)/shard_map/pallas_call | solution.py:366
  12.5 0.1 collective-permute-done.4.first_ref
  12.6 1.2 %collective-permute-start.5 = (bf16[16,1024]{1,0:T(8,128)(2,1)S(1)}, bf16[16,1024]{1,0:T(8,128)(2,1)S(1)}, u32[]{:S(2)}, u32[]{:S(2)}) collective-permute-start(bf16[16,1024]{1,0:T(8,128)(2,1)S(1)} %add_convert_fusion), channel_id=1, source_target_pairs={{0,16},{4,8},{8,12},{12,20},{16,0},{20,24},{24,28},{28,4},{1,17},{... | collective-permute-start | bytes 98312 | tf_op jit(solution)/shard_map/ppermute | solution.py:396
  13.8 1.1 %collective-permute-start.6 = (bf16[16,1024]{1,0:T(8,128)(2,1)S(1)}, bf16[16,1024]{1,0:T(8,128)(2,1)S(1)}, u32[]{:S(2)}, u32[]{:S(2)}) collective-permute-start(bf16[16,1024]{1,0:T(8,128)(2,1)S(1)} %add_convert_fusion), channel_id=1, source_target_pairs={{0,16},{4,12},{8,4},{12,24},{16,0},{20,28},{24,20},{28,8},{1,17},{... | collective-permute-start | bytes 98312 | tf_op jit(solution)/shard_map/ppermute | solution.py:396
  14.9 0.9 %shard_map.89 = (f32[128,1024]{1,0:T(8,128)S(1)}, bf16[128,1024]{1,0:T(8,128)(2,1)S(1)}) custom-call(bf16[128,1024]{1,0:T(8,128)(2,1)S(1)} %get-tuple-element.45.gated_ref, f32[64,128]{1,0:T(8,128)S(1)} %get-tuple-element.44._.rows_ref, bf16[128,128]{1,0:T(8,128)(2,1)S(1)} %get-tuple-element.46.same_ref, f32[128,128]{1,0:T(8,128)S(1)} %get-tuple-element.40.doc_ref, ...), custom_call_target="tpu_custom_call" | custom-call | flops 300000000 | tf_op jit(solution)/shard_map/pallas_call | solution.py:366
  15.8 1.3 %collective-permute-done.5.near_ref = bf16[16,1024]{1,0:T(8,128)(2,1)S(1)} collective-permute-done((bf16[16,1024]{1,0:T(8,128)(2,1)S(1)}, bf16[16,1024]{1,0:T(8,128)(2,1)S(1)}, u32[]{:S(2)}, u32[]{:S(2)}) %collective-permute-start.5) | collective-permute-done | bytes 32800 | tf_op jit(solution)/shard_map/ppermute | solution.py:396
  17.0 0.7 %collective-permute-done.6.far_ref = bf16[16,1024]{1,0:T(8,128)(2,1)S(1)} collective-permute-done((bf16[16,1024]{1,0:T(8,128)(2,1)S(1)}, bf16[16,1024]{1,0:T(8,128)(2,1)S(1)}, u32[]{:S(2)}, u32[]{:S(2)}) %collective-permute-start.6) | collective-permute-done | bytes 32800 | tf_op jit(solution)/shard_map/ppermute | solution.py:396
  17.7 0.9 %shard_map.90 = bf16[128,1024]{1,0:T(8,128)(2,1)} custom-call(f32[128,1024]{1,0:T(8,128)S(1)} %get-tuple-element.48.part_ref, bf16[128,1024]{1,0:T(8,128)(2,1)S(1)} %get-tuple-element.49.carry_ref, bf16[16,1024]{1,0:T(8,128)(2,1)S(1)} %collective-permute-done.4.first_ref, bf16[16,1024]{1,0:T(8,128)(2,1)S(1)} %collective-permute-done.5.near_ref, ...), custom_call_target="tpu_custom_call" | custom-call | flops 300000000 | tf_op jit(solution)/shard_map/pallas_call | solution.py:366
  (4 shorter events, 0.0 us)
Async XLA Ops:
  0.0 6.5 %collective-permute-start.1 = (bf16[64,512]{1,0:T(8,128)(2,1)}, bf16[64,512]{1,0:T(8,128)(2,1)S(1)}, u32[]{:S(2)}, u32[]{:S(2)}) collective-permute-start(bf16[64,512]{1,0:T(8,128)(2,1)} %bitcast.11), channel_id=1, source_target_pairs={{0,16},{16,0},{1,17},{17,1},{2,18},{18,2},{3,19},{19,3},{4,20},{20... | collective-permute-start | bytes 196616 | tf_op jit(solution)/shard_map/ppermute | solution.py:385
  1.2 3.7 %collective-permute-start.2 = (bf16[16,256]{1,0:T(8,128)(2,1)S(1)}, bf16[16,256]{1,0:T(8,128)(2,1)S(1)}, u32[]{:S(2)}, u32[]{:S(2)}) collective-permute-start(bf16[16,256]{1,0:T(8,128)(2,1)S(1)} %get-tuple-element.36), channel_id=1, source_target_pairs={{0,1},{1,0},{2,3},{3,2},{4,5},{5,4},{6,7},{7,6},{8,9},{9,8},{10,11... | collective-permute-start | bytes 24584 | tf_op jit(solution)/shard_map/ppermute | solution.py:385
  2.8 8.8 %collective-permute-start = (bf16[128,1024]{1,0:T(8,128)(2,1)S(1)}, bf16[128,1024]{1,0:T(8,128)(2,1)S(1)}, u32[]{:S(2)}, u32[]{:S(2)}) collective-permute-start(bf16[128,1024]{1,0:T(8,128)(2,1)S(1)} %get-tuple-element.29.product_ref), channel_id=1, source_target_pairs={{0,4},{4,8},{8,12},{12,0},{1,5},{5,9},{9,13},{13,1},{2,6},{6,10},{... | collective-permute-start | bytes 786440 | tf_op jit(solution)/shard_map/ppermute | solution.py:454
  4.9 3.7 %collective-permute-start.3 = (bf16[32,256]{1,0:T(8,128)(2,1)S(1)}, bf16[32,256]{1,0:T(8,128)(2,1)S(1)}, u32[]{:S(2)}, u32[]{:S(2)}) collective-permute-start(bf16[32,256]{1,0:T(8,128)(2,1)S(1)} %constant_dynamic-update-slice_fusion.modal_ref), channel_id=1, source_target_pairs={{0,2},{1,3},{2,0},{3,1},{4,6},{5,7},{6,4},{7,5},{8,10},{9,11},{10,... | collective-permute-start | bytes 49160 | tf_op jit(solution)/shard_map/ppermute | solution.py:385
  8.7 3.9 %collective-permute-start.4 = (bf16[16,1024]{1,0:T(8,128)(2,1)S(1)}, bf16[16,1024]{1,0:T(8,128)(2,1)S(1)}, u32[]{:S(2)}, u32[]{:S(2)}) collective-permute-start(bf16[16,1024]{1,0:T(8,128)(2,1)S(1)} %shard_map.85._), channel_id=1, source_target_pairs={{0,4},{4,0},{8,24},{12,28},{16,20},{20,16},{24,8},{28,12},{1,5},{5... | collective-permute-start | bytes 98312 | tf_op jit(solution)/shard_map/ppermute | solution.py:396
  12.6 4.4 %collective-permute-start.5 = (bf16[16,1024]{1,0:T(8,128)(2,1)S(1)}, bf16[16,1024]{1,0:T(8,128)(2,1)S(1)}, u32[]{:S(2)}, u32[]{:S(2)}) collective-permute-start(bf16[16,1024]{1,0:T(8,128)(2,1)S(1)} %add_convert_fusion), channel_id=1, source_target_pairs={{0,16},{4,8},{8,12},{12,20},{16,0},{20,24},{24,28},{28,4},{1,17},{... | collective-permute-start | bytes 98312 | tf_op jit(solution)/shard_map/ppermute | solution.py:396
  13.8 3.9 %collective-permute-start.6 = (bf16[16,1024]{1,0:T(8,128)(2,1)S(1)}, bf16[16,1024]{1,0:T(8,128)(2,1)S(1)}, u32[]{:S(2)}, u32[]{:S(2)}) collective-permute-start(bf16[16,1024]{1,0:T(8,128)(2,1)S(1)} %add_convert_fusion), channel_id=1, source_target_pairs={{0,16},{4,12},{8,4},{12,24},{16,0},{20,28},{24,20},{28,8},{1,17},{... | collective-permute-start | bytes 98312 | tf_op jit(solution)/shard_map/ppermute | solution.py:396

commit v7 on v6

--- a/solution.py
+++ b/solution.py
@@ -64,15 +64,16 @@
     modes, width = select_ref.shape[0] // 2, spread_ref.shape[1]
     per_part = rate_ref.shape[0]
     lines = select_ref.shape[1]
+    pieces = lines // 16
     line, mode = iota((2 * modes, lines), 1), iota((2 * modes, lines), 0)
     within = line % 16
     held = jnp.where(mode < modes, within, within - 8)
-    owner = jnp.bitwise_xor(dp_place, line // 16)
+    owner = jnp.bitwise_xor(dp_place, (pieces - line // 16) % pieces)
     wanted = owner * per_part + held == jnp.where(mode < modes, mode, mode - modes)
     select_ref[...] = ((held >= 0) & (held < per_part) & wanted).astype(jnp.bfloat16)
     line, mode = iota((lines, width), 0), iota((lines, width), 1) % modes
     within = line % 16
-    owner = jnp.bitwise_xor(dp_place, line // 16)
+    owner = jnp.bitwise_xor(dp_place, (pieces - line // 16) % pieces)
     rates_ref[...] = ((within < per_part) & (owner * per_part + within == mode)).astype(
         jnp.float32
     )
@@ -217,14 +218,13 @@
         end_ref[:, lanes] = jnp.where(keeps, weight, 0.0).astype(jnp.bfloat16)
 
 
-def first_kernel(
-    modal_ref, modal_rest_ref, spread_ref, rates_ref, doc_ref, gated_ref, state_ref, end_ref
-):
+def first_kernel(*refs):
+    *modal_refs, spread_ref, rates_ref, doc_ref, gated_ref, state_ref, end_ref = refs
     modes, width = state_ref.shape
 
     @pl.when(lax.axis_index("ctx") == 0)
     def _():
-        lines = modal_parts([modal_ref, modal_rest_ref], spread_ref, width // modes)
+        lines = modal_parts(modal_refs, spread_ref, width // modes)
         end_weights(lines, rates_ref, doc_ref, end_ref)
         end_states(end_ref, gated_ref, state_ref)
 
@@ -233,19 +233,10 @@
         state_ref[...] = jnp.zeros_like(state_ref)
 
 
-def modal_kernel(
-    modal_ref,
-    modal_rest_ref,
-    select_ref,
-    spread_ref,
-    rates_ref,
-    doc_ref,
-    _,
-    end_ref,
-    channels_ref,
-):
+def modal_kernel(*refs):
+    *modal_refs, select_ref, spread_ref, rates_ref, doc_ref, _, end_ref, channels_ref = refs
     modes, width = channels_ref.shape[0] // 2, channels_ref.shape[1]
-    lines = modal_parts([modal_ref, modal_rest_ref], spread_ref, width // modes)
+    lines = modal_parts(modal_refs, spread_ref, width // modes)
     end_weights(lines, rates_ref, doc_ref, end_ref)
     channels_ref[...] = dot(select_ref[...], lines.astype(jnp.bfloat16))
 
@@ -340,7 +331,7 @@
 
 
 def finish_kernel(
-    four, part_ref, carry_ref, first_ref, near_ref, far_ref, through_ref, out_ref
+    four, part_ref, carry_ref, first_ref, far_ref, middle_ref, near_ref, through_ref, out_ref
 ):
     width = part_ref.shape[1]
     modes = near_ref.shape[0]
@@ -349,9 +340,10 @@
     entering = near_ref[...].astype(jnp.float32)
     if four:
         place = lax.axis_index("ctx")
-        entering = jnp.where(place >= 2, entering, 0.0)
-        entering += jnp.where(place == 3, through_ref[...] * far_ref[...].astype(jnp.float32), 0.0)
+        entering += through_ref[...] * far_ref[...].astype(jnp.float32)
+        entering = jnp.where(place == 3, entering, 0.0)
         entering += jnp.where(place == 1, first_ref[...].astype(jnp.float32), 0.0)
+        entering += jnp.where(place == 2, middle_ref[...].astype(jnp.float32), 0.0)
     for slab in range(width // LANES):
         lanes = slice(slab * LANES, (slab + 1) * LANES)
         state = jnp.concatenate([entering[:, lanes]] * per_slab, axis=0)
@@ -453,11 +445,7 @@
     )
     halo = lax.ppermute(product, "ctx", [(i, (i + 1) % ctx_size) for i in range(ctx_size)])
     other_taps = exchanged(taps, "fsdp", 1)
-    bit = 1
-    while 2 * bit < dp_size:
-        modal = jnp.concatenate([modal, exchanged(modal, "dp", bit)], axis=0)
-        bit *= 2
-    modal_rest = exchanged(modal, "dp", bit)
+    modal = [modal] + [exchanged(modal, "dp", bit) for bit in reversed(range(1, dp_size))]
     square = ((groups, tokens, tokens), half)
     previous, current, same, documents = call(
         medium_kernel,
@@ -478,8 +466,7 @@
     (state_own,) = call(
         first_kernel,
         [((modes, width), half)],
-        modal,
-        modal_rest,
+        *modal,
         spread,
         rates,
         documents,
@@ -489,8 +476,7 @@
     end, channels = call(
         modal_kernel,
         [((tokens, width), half), ((2 * modes, width), jnp.float32)],
-        modal,
-        modal_rest,
+        *modal,
         select,
         spread,
         rates,
@@ -518,10 +504,11 @@
     if four:
         both = state.astype(jnp.float32) + first_through * first.astype(jnp.float32)
         both = both.astype(half)
-        near = cycled(both, [1, 2, 3], (3, ))
-        far = cycled(both, [1, 3, 2], (3, ))
+        near = cycled(state, [2, 3], ())
+        middle = cycled(both, [1, 2], (2, ))
+        far = cycled(both, [1, 3, 2], (2, ))
     else:
-        near = far = entering_states(state, through)
+        near = middle = far = entering_states(state, through)
     part, carry = call(
         local_kernel,
         [((tokens, width), jnp.float32), ((tokens, width), half)],
@@ -538,8 +525,9 @@
         part,
         carry,
         first,
+        far,
+        middle,
         near,
-        far,
         far_through,
     )
     return out[None]

time: 18.8 us -> 18.6 us (0.989)
  waiting for transfers between devices: 4.33 us -> 3.37 us
  starting transfers between devices: 7.43 us -> 8.06 us
    ppermute x1, waiting for transfers between devices: 1.12 us -> 0.01 us  [body(): lax.ppermute(product, 'ctx', [(i, (i + 1) % ctx_size) for i in range(ctx_...]
    ppermute x3 -> x4, starting transfers between devices: 3.08 us -> 3.49 us  [exchanged(): lax.ppermute(array, axis, [(i, i ^ bit) for i in range(lax.axis_size(axis...]
    ppermute x3 -> x4, waiting for transfers between devices: 1.14 us -> 1.46 us  [exchanged(): lax.ppermute(array, axis, [(i, i ^ bit) for i in range(lax.axis_size(axis...]
    ppermute x3 -> x4, starting transfers between devices: 2.78 us -> 2.94 us  [cycled(): return lax.ppermute(array, ('fsdp', 'ctx'), moves)]
    ppermute x3 -> x4, waiting for transfers between devices: 2.07 us -> 1.91 us  [cycled(): return lax.ppermute(array, ('fsdp', 'ctx'), moves)]
  transfers between devices with their start and end apart: 7 -> 9, of which waited for: 6 -> 5; matrix products, arithmetic and copies ran while one was open for 0% -> 0% of each run, Pallas kernels for 32% -> 25%
where the time goes in v7:
time: 18.6 us; the launch traced here: 18.3 us
  starting transfers between devices  8.06 us (43%)
  Pallas kernels  6.81 us (37%)
  waiting for transfers between devices  3.37 us (18%)
    pallas_call x9, Pallas kernels, call(): pl.pallas_call(kernel, out_shape=[jax.ShapeDtypeStruct(shape, dtype) for...  6.81 us
    ppermute x4, starting transfers between devices, exchanged(): lax.ppermute(array, axis, [(i, i ^ bit) for i in range(lax.axis_size(axis...  3.49 us
    ppermute x4, starting transfers between devices, cycled(): return lax.ppermute(array, ('fsdp', 'ctx'), moves)  2.94 us
    ppermute x4, waiting for transfers between devices, cycled(): return lax.ppermute(array, ('fsdp', 'ctx'), moves)  1.91 us
    ppermute x1, starting transfers between devices, body(): lax.ppermute(product, 'ctx', [(i, (i + 1) % ctx_size) for i in range(ctx_...  1.63 us
    ppermute x4, waiting for transfers between devices, exchanged(): lax.ppermute(array, axis, [(i, i ^ bit) for i in range(lax.axis_size(axis...  1.46 us
  transfers between devices with their start and end apart: 9, of which 5 were waited for; matrix products, arithmetic and copies ran while one was open for 0% of the time, Pallas kernels for 25%

profile of v7, /device:TPU:8, one launch (start us, length us, event | category | flops | bytes accessed | tf_op | source)
XLA Modules:
  0.0 18.3 jit_solution(14793565973780170238)
XLA Ops:
  0.0 1.2 %shard_map.82 = (bf16[128,1024]{1,0:T(8,128)(2,1)S(1)}, bf16[16,256]{1,0:T(8,128)(2,1)S(1)}, bf16[128,1024]{1,0:T(8,128)(2,1)S(1)}, bf16[32,64]{1,0:T(8,128)(2,1...) custom-call(bf16[128,1024]{1,0:T(8,128)(2,1)} %bitcast.8, ...), custom_call_target="tpu_custom_call" | custom-call | flops 300000000 | tf_op jit(solution)/shard_map/pallas_call | solution.py:358
  1.2 1.6 %collective-permute-start = (bf16[128,1024]{1,0:T(8,128)(2,1)S(1)}, bf16[128,1024]{1,0:T(8,128)(2,1)S(1)}, u32[]{:S(2)}, u32[]{:S(2)}) collective-permute-start(bf16[128,1024]{1,0:T(8,128)(2,1)S(1)} %get-tuple-element.29.product_ref), channel_id=1, source_target_pairs={{0,4},{4,8},{8,12},{12,0},{1,5},{5,9},{9,13},{13,1},{2,6},{6,10},{... | collective-permute-start | bytes 786440 | tf_op jit(solution)/shard_map/ppermute | solution.py:446
  2.9 0.0 collective-permute-start.1
  2.9 2.4 %collective-permute-start.2 = (bf16[16,256]{1,0:T(8,128)(2,1)S(1)}, bf16[16,256]{1,0:T(8,128)(2,1)S(1)}, u32[]{:S(2)}, u32[]{:S(2)}) collective-permute-start(bf16[16,256]{1,0:T(8,128)(2,1)S(1)} %get-tuple-element.36.refs_0_), channel_id=1, source_target_pairs={{0,3},{1,2},{2,1},{3,0},{4,7},{5,6},{6,5},{7,4},{8,11},{9,10},{10,... | collective-permute-start | bytes 24584 | tf_op jit(solution)/shard_map/ppermute | solution.py:377
  5.3 0.5 %collective-permute-start.3 = (bf16[16,256]{1,0:T(8,128)(2,1)S(1)}, bf16[16,256]{1,0:T(8,128)(2,1)S(1)}, u32[]{:S(2)}, u32[]{:S(2)}) collective-permute-start(bf16[16,256]{1,0:T(8,128)(2,1)S(1)} %get-tuple-element.36.refs_0_), channel_id=1, source_target_pairs={{0,2},{1,3},{2,0},{3,1},{4,6},{5,7},{6,4},{7,5},{8,10},{9,11},{10,... | collective-permute-start | bytes 24584 | tf_op jit(solution)/shard_map/ppermute | solution.py:377
  5.8 0.5 %collective-permute-start.4 = (bf16[16,256]{1,0:T(8,128)(2,1)S(1)}, bf16[16,256]{1,0:T(8,128)(2,1)S(1)}, u32[]{:S(2)}, u32[]{:S(2)}) collective-permute-start(bf16[16,256]{1,0:T(8,128)(2,1)S(1)} %get-tuple-element.36.refs_0_), channel_id=1, source_target_pairs={{0,1},{1,0},{2,3},{3,2},{4,5},{5,4},{6,7},{7,6},{8,9},{9,8},{10,11... | collective-permute-start | bytes 24584 | tf_op jit(solution)/shard_map/ppermute | solution.py:377
  6.3 0.0 collective-permute-done.1.other_taps_ref
  6.4 0.9 %shard_map.83 = (bf16[64,128,128]{2,1,0:T(8,128)(2,1)S(1)}, bf16[64,128,128]{2,1,0:T(8,128)(2,1)S(1)}, bf16[128,128]{1,0:T(8,128)(2,1)S(1)}, f32[128,128]{1,0:T(8,128)S(1)}) custom-call(bf16[64,512]{1,0:T(8,128)(2,1)S(1)} %get-tuple-element.31.taps_ref, bf16[64,512]{1,0:T(8,128)(2,1)S(1)} %collective-permute-done.1.other_taps_ref, ...), custom_call_target="tpu_custom_call" | custom-call | flops 300000000 | tf_op jit(solution)/shard_map/pallas_call | solution.py:358
  7.3 0.7 %shard_map.84 = (f32[128,1024]{1,0:T(8,128)S(1)}, bf16[128,1024]{1,0:T(8,128)(2,1)S(1)}) custom-call(bf16[128,1024]{1,0:T(8,128)(2,1)S(1)} %get-tuple-element.29.product_ref, bf16[128,1024]{1,0:T(8,128)(2,1)S(1)} %get-tuple-element.30.query_ref, bf16[64,128,128]{2,1,0:T(8,128)(2,1)S(1)} %get-tuple-element.34.current_ref), custom_call_target="tpu_custom_call" | custom-call | flops 300000000 | tf_op jit(solution)/shard_map/pallas_call | solution.py:358
  8.0 0.0 collective-permute-done.2.refs_1_
  8.0 0.9 %collective-permute-done.3.refs_2_ = bf16[16,256]{1,0:T(8,128)(2,1)S(1)} collective-permute-done((bf16[16,256]{1,0:T(8,128)(2,1)S(1)}, bf16[16,256]{1,0:T(8,128)(2,1)S(1)}, u32[]{:S(2)}, u32[]{:S(2)}) %collective-permute-start.3) | collective-permute-done | bytes 8224 | tf_op jit(solution)/shard_map/ppermute | solution.py:377
  9.0 0.5 %collective-permute-done.4.refs_3_ = bf16[16,256]{1,0:T(8,128)(2,1)S(1)} collective-permute-done((bf16[16,256]{1,0:T(8,128)(2,1)S(1)}, bf16[16,256]{1,0:T(8,128)(2,1)S(1)}, u32[]{:S(2)}, u32[]{:S(2)}) %collective-permute-start.4) | collective-permute-done | bytes 8224 | tf_op jit(solution)/shard_map/ppermute | solution.py:377
  9.5 1.0 %collective-permute-start.5 = (bf16[16,1024]{1,0:T(8,128)(2,1)S(1)}, bf16[16,1024]{1,0:T(8,128)(2,1)S(1)}, u32[]{:S(2)}, u32[]{:S(2)}) collective-permute-start(bf16[16,1024]{1,0:T(8,128)(2,1)S(1)} %shard_map.85.refs_8_), channel_id=1, source_target_pairs={{0,4},{4,0},{8,24},{12,28},{16,20},{20,16},{24,8},{28,12},{1,5},{5... | collective-permute-start | bytes 98312 | tf_op jit(solution)/shard_map/ppermute | solution.py:388
  10.5 0.4 %shard_map.86 = (bf16[128,1024]{1,0:T(8,128)(2,1)S(1)}, f32[32,1024]{1,0:T(8,128)S(1)}) custom-call(bf16[16,256]{1,0:T(8,128)(2,1)S(1)} %get-tuple-element.36.refs_0_, bf16[16,256]{1,0:T(8,128)(2,1)S(1)} %collective-permute-done.2.refs_1_, bf16[16,256]{1,0:T(8,128)(2,1)S(1)} %collective-permute-done.3.refs_2_, ...), custom_call_target="tpu_custom_call" | custom-call | flops 300000000 | tf_op jit(solution)/shard_map/pallas_call | solution.py:358
  10.9 0.9 %shard_map.87 = (f32[64,128]{1,0:T(8,128)S(1)}, f32[16,1024]{1,0:T(8,128)}, f32[16,1024]{1,0:T(8,128)S(1)}, f32[16,1024]{1,0:T(8,128)S(1)}) custom-call(f32[32,1024]{1,0:T(8,128)S(1)} %get-tuple-element.43.channels_ref, s32[1,512]{1,0:T(1,128)S(1)} %get-tuple-element.32.starts_ref), custom_call_target="tpu_custom_call" | custom-call | flops 300000000 | tf_op jit(solution)/shard_map/pallas_call | solution.py:358
  11.8 0.9 %shard_map.88 = (bf16[128,1024]{1,0:T(8,128)(2,1)S(1)}, bf16[16,1024]{1,0:T(8,128)(2,1)S(1)}) custom-call(bf16[128,1024]{1,0:T(8,128)(2,1)S(1)} %collective-permute-done.halo_ref, bf16[128,1024]{1,0:T(8,128)(2,1)S(1)} %get-tuple-element.30.query_ref, bf16[64,128,128]{2,1,0:T(8,128)(2,1)S(1)} %get-tuple-element.33.previous_ref, ...), custom_call_target="tpu_custom_call" | custom-call | flops 300000000 | tf_op jit(solution)/shard_map/pallas_call | solution.py:358
  12.6 0.7 %collective-permute-done.5.first_ref = bf16[16,1024]{1,0:T(8,128)(2,1)S(1)} collective-permute-done((bf16[16,1024]{1,0:T(8,128)(2,1)S(1)}, bf16[16,1024]{1,0:T(8,128)(2,1)S(1)}, u32[]{:S(2)}, u32[]{:S(2)}) %collective-permute-start.5) | collective-permute-done | bytes 32800 | tf_op jit(solution)/shard_map/ppermute | solution.py:388
  13.4 0.1 collective-permute-start.6
  13.5 0.1 collective-permute-start.7
  13.5 1.8 %collective-permute-start.8 = (bf16[16,1024]{1,0:T(8,128)(2,1)S(1)}, bf16[16,1024]{1,0:T(8,128)(2,1)S(1)}, u32[]{:S(2)}, u32[]{:S(2)}) collective-permute-start(bf16[16,1024]{1,0:T(8,128)(2,1)S(1)} %get-tuple-element.50), channel_id=1, source_target_pairs={{0,16},{4,20},{8,12},{12,8},{16,0},{20,4},{24,28},{28,24},{1,17},{... | collective-permute-start | bytes 98312 | tf_op jit(solution)/shard_map/ppermute | solution.py:388
  15.3 0.9 %shard_map.89 = (f32[128,1024]{1,0:T(8,128)S(1)}, bf16[128,1024]{1,0:T(8,128)(2,1)S(1)}) custom-call(bf16[128,1024]{1,0:T(8,128)(2,1)S(1)} %get-tuple-element.45.gated_ref, f32[64,128]{1,0:T(8,128)S(1)} %get-tuple-element.44._.rows_ref, bf16[128,128]{1,0:T(8,128)(2,1)S(1)} %get-tuple-element.46.same_ref, ...), custom_call_target="tpu_custom_call" | custom-call | flops 300000000 | tf_op jit(solution)/shard_map/pallas_call | solution.py:358
  16.2 0.8 %collective-permute-done.6.far_ref = bf16[16,1024]{1,0:T(8,128)(2,1)S(1)} collective-permute-done((bf16[16,1024]{1,0:T(8,128)(2,1)S(1)}, bf16[16,1024]{1,0:T(8,128)(2,1)S(1)}, u32[]{:S(2)}, u32[]{:S(2)}) %collective-permute-start.6) | collective-permute-done | bytes 32800 | tf_op jit(solution)/shard_map/ppermute | solution.py:388
  17.0 0.4 %collective-permute-done.7.middle_ref = bf16[16,1024]{1,0:T(8,128)(2,1)S(1)} collective-permute-done((bf16[16,1024]{1,0:T(8,128)(2,1)S(1)}, bf16[16,1024]{1,0:T(8,128)(2,1)S(1)}, u32[]{:S(2)}, u32[]{:S(2)}) %collective-permute-start.7) | collective-permute-done | bytes 32800 | tf_op jit(solution)/shard_map/ppermute | solution.py:388
  17.4 0.9 %shard_map.90 = bf16[128,1024]{1,0:T(8,128)(2,1)} custom-call(f32[128,1024]{1,0:T(8,128)S(1)} %get-tuple-element.48.part_ref, bf16[128,1024]{1,0:T(8,128)(2,1)S(1)} %get-tuple-element.49.carry_ref, bf16[16,1024]{1,0:T(8,128)(2,1)S(1)} %collective-permute-done.5.first_ref, bf16[16,1024]{1,0:T(8,128)(2,1)S(1)} %collective-permute-done.6.far_ref, ...), custom_call_target="tpu_custom_call" | custom-call | flops 300000000 | tf_op jit(solution)/shard_map/pallas_call | solution.py:358
  (4 shorter events, 0.0 us)
Async XLA Ops:
  1.2 10.5 %collective-permute-start = (bf16[128,1024]{1,0:T(8,128)(2,1)S(1)}, bf16[128,1024]{1,0:T(8,128)(2,1)S(1)}, u32[]{:S(2)}, u32[]{:S(2)}) collective-permute-start(bf16[128,1024]{1,0:T(8,128)(2,1)S(1)} %get-tuple-element.29.product_ref), channel_id=1, source_target_pairs={{0,4},{4,8},{8,12},{12,0},{1,5},{5,9},{9,13},{13,1},{2,6},{6,10},{... | collective-permute-start | bytes 786440 | tf_op jit(solution)/shard_map/ppermute | solution.py:446
  2.9 3.5 %collective-permute-start.1 = (bf16[64,512]{1,0:T(8,128)(2,1)}, bf16[64,512]{1,0:T(8,128)(2,1)S(1)}, u32[]{:S(2)}, u32[]{:S(2)}) collective-permute-start(bf16[64,512]{1,0:T(8,128)(2,1)} %bitcast.12), channel_id=1, source_target_pairs={{0,16},{16,0},{1,17},{17,1},{2,18},{18,2},{3,19},{19,3},{4,20},{20... | collective-permute-start | bytes 196616 | tf_op jit(solution)/shard_map/ppermute | solution.py:377
  2.9 5.1 %collective-permute-start.2 = (bf16[16,256]{1,0:T(8,128)(2,1)S(1)}, bf16[16,256]{1,0:T(8,128)(2,1)S(1)}, u32[]{:S(2)}, u32[]{:S(2)}) collective-permute-start(bf16[16,256]{1,0:T(8,128)(2,1)S(1)} %get-tuple-element.36.refs_0_), channel_id=1, source_target_pairs={{0,3},{1,2},{2,1},{3,0},{4,7},{5,6},{6,5},{7,4},{8,11},{9,10},{10,... | collective-permute-start | bytes 24584 | tf_op jit(solution)/shard_map/ppermute | solution.py:377
  5.3 3.7 %collective-permute-start.3 = (bf16[16,256]{1,0:T(8,128)(2,1)S(1)}, bf16[16,256]{1,0:T(8,128)(2,1)S(1)}, u32[]{:S(2)}, u32[]{:S(2)}) collective-permute-start(bf16[16,256]{1,0:T(8,128)(2,1)S(1)} %get-tuple-element.36.refs_0_), channel_id=1, source_target_pairs={{0,2},{1,3},{2,0},{3,1},{4,6},{5,7},{6,4},{7,5},{8,10},{9,11},{10,... | collective-permute-start | bytes 24584 | tf_op jit(solution)/shard_map/ppermute | solution.py:377
  5.8 3.7 %collective-permute-start.4 = (bf16[16,256]{1,0:T(8,128)(2,1)S(1)}, bf16[16,256]{1,0:T(8,128)(2,1)S(1)}, u32[]{:S(2)}, u32[]{:S(2)}) collective-permute-start(bf16[16,256]{1,0:T(8,128)(2,1)S(1)} %get-tuple-element.36.refs_0_), channel_id=1, source_target_pairs={{0,1},{1,0},{2,3},{3,2},{4,5},{5,4},{6,7},{7,6},{8,9},{9,8},{10,11... | collective-permute-start | bytes 24584 | tf_op jit(solution)/shard_map/ppermute | solution.py:377
  9.5 3.9 %collective-permute-start.5 = (bf16[16,1024]{1,0:T(8,128)(2,1)S(1)}, bf16[16,1024]{1,0:T(8,128)(2,1)S(1)}, u32[]{:S(2)}, u32[]{:S(2)}) collective-permute-start(bf16[16,1024]{1,0:T(8,128)(2,1)S(1)} %shard_map.85.refs_8_), channel_id=1, source_target_pairs={{0,4},{4,0},{8,24},{12,28},{16,20},{20,16},{24,8},{28,12},{1,5},{5... | collective-permute-start | bytes 98312 | tf_op jit(solution)/shard_map/ppermute | solution.py:388
  13.4 3.6 %collective-permute-start.6 = (bf16[16,1024]{1,0:T(8,128)(2,1)S(1)}, bf16[16,1024]{1,0:T(8,128)(2,1)S(1)}, u32[]{:S(2)}, u32[]{:S(2)}) collective-permute-start(bf16[16,1024]{1,0:T(8,128)(2,1)S(1)} %add_convert_fusion), channel_id=1, source_target_pairs={{0,16},{4,12},{8,20},{12,8},{16,0},{20,28},{24,4},{28,24},{1,17},{... | collective-permute-start | bytes 98312 | tf_op jit(solution)/shard_map/ppermute | solution.py:388
  13.5 3.9 %collective-permute-start.7 = (bf16[16,1024]{1,0:T(8,128)(2,1)S(1)}, bf16[16,1024]{1,0:T(8,128)(2,1)S(1)}, u32[]{:S(2)}, u32[]{:S(2)}) collective-permute-start(bf16[16,1024]{1,0:T(8,128)(2,1)S(1)} %add_convert_fusion), channel_id=1, source_target_pairs={{0,16},{4,8},{8,20},{12,28},{16,0},{20,24},{24,4},{28,12},{1,17},{... | collective-permute-start | bytes 98312 | tf_op jit(solution)/shard_map/ppermute | solution.py:388
  13.5 3.8 %collective-permute-start.8 = (bf16[16,1024]{1,0:T(8,128)(2,1)S(1)}, bf16[16,1024]{1,0:T(8,128)(2,1)S(1)}, u32[]{:S(2)}, u32[]{:S(2)}) collective-permute-start(bf16[16,1024]{1,0:T(8,128)(2,1)S(1)} %get-tuple-element.50), channel_id=1, source_target_pairs={{0,16},{4,20},{8,12},{12,8},{16,0},{20,4},{24,28},{28,24},{1,17},{... | collective-permute-start | bytes 98312 | tf_op jit(solution)/shard_map/ppermute | solution.py:388

commit v8 on v7

--- a/solution.py
+++ b/solution.py
@@ -138,6 +138,7 @@
     current_ref,
     same_ref,
     doc_ref,
+    clear_ref,
     rows_ref,
 ):
     fsdp_place, ctx_place, dp_place = (lax.axis_index(axis) for axis in ("fsdp", "ctx", "dp"))
@@ -158,6 +159,9 @@
     previous = folded((previous & (ctx_place > 0)).astype(jnp.float32), block)
     halves = [slice(0, block // 2), slice(block // 2, block)]
     doc_ref[...] = doc_col
+    for line, begun in enumerate((own, prior)):
+        none = jnp.sum(begun, axis=1, keepdims=True) == 0.0
+        clear_ref[line : line + 1, :] = jnp.where(none, jnp.ones((1, block), jnp.float32), 0.0)
     for part, rows in enumerate(halves):
         same_ref[rows, :] = current[part]
     for group in range(groups):
@@ -233,12 +237,19 @@
         state_ref[...] = jnp.zeros_like(state_ref)
 
 
-def modal_kernel(*refs):
-    *modal_refs, select_ref, spread_ref, rates_ref, doc_ref, _, end_ref, channels_ref = refs
+def modal_kernel(four, *refs):
+    *refs, end_ref, channels_ref, through_ref, far_ref = refs
+    *modal_refs, select_ref, spread_ref, rates_ref, doc_ref, clear_ref, _ = refs
     modes, width = channels_ref.shape[0] // 2, channels_ref.shape[1]
     lines = modal_parts(modal_refs, spread_ref, width // modes)
     end_weights(lines, rates_ref, doc_ref, end_ref)
-    channels_ref[...] = dot(select_ref[...], lines.astype(jnp.bfloat16))
+    by_channel = dot(select_ref[...], lines.astype(jnp.bfloat16))
+    channels_ref[...] = by_channel
+    wanted = (lax.axis_index("ctx") == 1).astype(jnp.float32) if four else 1.0
+    for lanes in slabs_of(width):
+        decay = jnp.exp(-by_channel[:modes, lanes] * end_ref.shape[0])
+        through_ref[:, lanes] = decay * (clear_ref[0:1, :] * wanted)
+        far_ref[:, lanes] = decay * clear_ref[1:2, :]
 
 
 def modal_lines(channels_ref, modes, width):
@@ -250,10 +261,9 @@
     ]
 
 
-def response_kernel(channels_ref, starts_ref, rows_ref, through_ref, first_ref, far_ref):
+def response_kernel(channels_ref, _, rows_ref):
     groups, block = rows_ref.shape
-    modes, width = through_ref.shape
-    ctx_place = lax.axis_index("ctx")
+    modes, width = channels_ref.shape[0] // 2, channels_ref.shape[1]
     rate_line, scaled_line = modal_lines(channels_ref, modes, width)
     lag = ((block - iota((block, LANES), 0)) % block).astype(jnp.float32)
     per_slab = LANES // modes
@@ -264,13 +274,6 @@
         low = (terms - high.astype(jnp.float32)).astype(jnp.bfloat16)
         sums = jnp.transpose(dot(high, gather) + dot(low, gather))
         rows_ref[slab * per_slab : (slab + 1) * per_slab, :] = sums[:per_slab]
-    decay = jnp.exp(-channels_ref[:modes] * block)
-    own, prior = block_starts(starts_ref, ctx_place, block)
-    none_own = jnp.sum(own, axis=1, keepdims=True) == 0.0
-    none_prior = jnp.sum(prior, axis=1, keepdims=True) == 0.0
-    through_ref[...] = jnp.where(none_own, decay, 0.0)
-    first_ref[...] = jnp.where(none_own & (ctx_place == 1), decay, 0.0)
-    far_ref[...] = jnp.where(none_prior, decay, 0.0)
 
 
 def grouped(halves, values):
@@ -309,7 +312,9 @@
     end_states(end_ref, gated_ref, state_ref)
 
 
-def local_kernel(gated_ref, rows_ref, same_ref, doc_ref, channels_ref, gain_ref, part_ref, carry_ref):
+def local_kernel(
+    gated_ref, rows_ref, same_ref, doc_ref, channels_ref, gain_ref, part_ref, carry_ref
+):
     block, width = part_ref.shape
     modes = channels_ref.shape[0] // 2
     per_slab = LANES // GROUP_CH
@@ -447,9 +452,15 @@
     other_taps = exchanged(taps, "fsdp", 1)
     modal = [modal] + [exchanged(modal, "dp", bit) for bit in reversed(range(1, dp_size))]
     square = ((groups, tokens, tokens), half)
-    previous, current, same, documents = call(
+    previous, current, same, documents, clear = call(
         medium_kernel,
-        [square, square, ((tokens, tokens), half), ((tokens, tokens), jnp.float32)],
+        [
+            square,
+            square,
+            ((tokens, tokens), half),
+            ((tokens, tokens), jnp.float32),
+            ((2, tokens), jnp.float32),
+        ],
         own_taps,
         other_taps,
         starts,
@@ -463,6 +474,7 @@
         current,
     )
     states = ((modes, width), jnp.float32)
+    four = ctx_size == 4
     (state_own,) = call(
         first_kernel,
         [((modes, width), half)],
@@ -473,23 +485,20 @@
         gated_own,
         scratch=[pltpu.VMEM((tokens, width), half)],
     )
-    end, channels = call(
-        modal_kernel,
-        [((tokens, width), half), ((2 * modes, width), jnp.float32)],
+    end, channels, through, far_through = call(
+        functools.partial(modal_kernel, four),
+        [((tokens, width), half), ((2 * modes, width), jnp.float32), states, states],
         *modal,
         select,
         spread,
         rates,
         documents,
+        clear,
         state_own,
     )
-    four = ctx_size == 4
-    first = cycled(state_own, [0, 1]) if four else state_own
-    response, through, first_through, far_through = call(
-        response_kernel,
-        [((groups, tokens), jnp.float32), states, states, states],
-        channels,
-        starts,
+    first = cycled(state_own, [0, 1], (1,)) if four else state_own
+    (response,) = call(
+        response_kernel, [((groups, tokens), jnp.float32)], channels, state_own
     )
     gated, state = call(
         gate_kernel,
@@ -502,7 +511,7 @@
         response,
     )
     if four:
-        both = state.astype(jnp.float32) + first_through * first.astype(jnp.float32)
+        both = state.astype(jnp.float32) + through * first.astype(jnp.float32)
         both = both.astype(half)
         near = cycled(state, [2, 3], ())
         middle = cycled(both, [1, 2], (2, ))

time: 18.6 us -> 18.2 us (0.978)
  waiting for transfers between devices: 3.37 us -> 4.59 us
  starting transfers between devices: 8.06 us -> 7.03 us
  Pallas kernels: 6.81 us -> 6.38 us
    ppermute x4, waiting for transfers between devices: 1.91 us -> 3.16 us  [cycled(): return lax.ppermute(array, ('fsdp', 'ctx'), moves)]
    ppermute x4, starting transfers between devices: 2.94 us -> 1.91 us  [cycled(): return lax.ppermute(array, ('fsdp', 'ctx'), moves)]
    pallas_call x9, Pallas kernels: 6.81 us -> 6.38 us  [call(): pl.pallas_call(kernel, out_shape=[jax.ShapeDtypeStruct(shape, dtype) for...]
  transfers between devices with their start and end apart: 9 -> 9, of which waited for: 5 -> 5; matrix products, arithmetic and copies ran while one was open for 0% -> 0% of each run, Pallas kernels for 25% -> 23%
where the time goes in v8:
time: 18.2 us; the launch traced here: 18.1 us
  starting transfers between devices  7.03 us (39%)
  Pallas kernels  6.38 us (35%)
  waiting for transfers between devices  4.59 us (25%)
    pallas_call x9, Pallas kernels, call(): pl.pallas_call(kernel, out_shape=[jax.ShapeDtypeStruct(shape, dtype) for...  6.38 us
    ppermute x4, starting transfers between devices, exchanged(): lax.ppermute(array, axis, [(i, i ^ bit) for i in range(lax.axis_size(axis...  3.49 us
    ppermute x4, waiting for transfers between devices, cycled(): return lax.ppermute(array, ('fsdp', 'ctx'), moves)  3.16 us
    ppermute x4, starting transfers between devices, cycled(): return lax.ppermute(array, ('fsdp', 'ctx'), moves)  1.91 us
    ppermute x1, starting transfers between devices, body(): lax.ppermute(product, 'ctx', [(i, (i + 1) % ctx_size) for i in range(ctx_...  1.63 us
    ppermute x4, waiting for transfers between devices, exchanged(): lax.ppermute(array, axis, [(i, i ^ bit) for i in range(lax.axis_size(axis...  1.43 us
  transfers between devices with their start and end apart: 9, of which 5 were waited for; matrix products, arithmetic and copies ran while one was open for 0% of the time, Pallas kernels for 23%

profile of v8, /device:TPU:8, one launch (start us, length us, event | category | flops | bytes accessed | tf_op | source)
XLA Modules:
  0.0 18.1 jit_solution(5614760333734052909)
XLA Ops:
  0.0 1.2 %shard_map.82 = (bf16[128,1024]{1,0:T(8,128)(2,1)S(1)}, bf16[16,256]{1,0:T(8,128)(2,1)S(1)}, bf16[128,1024]{1,0:T(8,128)(2,1)S(1)}, bf16[32,64]{1,0:T(8,128)(2,1...) custom-call(bf16[128,1024]{1,0:T(8,128)(2,1)} %bitcast.8, ...), custom_call_target="tpu_custom_call" | custom-call | flops 300000000 | tf_op jit(solution)/shard_map/pallas_call | solution.py:363
  1.2 1.6 %collective-permute-start = (bf16[128,1024]{1,0:T(8,128)(2,1)S(1)}, bf16[128,1024]{1,0:T(8,128)(2,1)S(1)}, u32[]{:S(2)}, u32[]{:S(2)}) collective-permute-start(bf16[128,1024]{1,0:T(8,128)(2,1)S(1)} %get-tuple-element.29.product_ref), channel_id=1, source_target_pairs={{0,4},{4,8},{8,12},{12,0},{1,5},{5,9},{9,13},{13,1},{2,6},{6,10},{... | collective-permute-start | bytes 786440 | tf_op jit(solution)/shard_map/ppermute | solution.py:451
  2.9 0.0 collective-permute-start.1
  2.9 2.4 %collective-permute-start.2 = (bf16[16,256]{1,0:T(8,128)(2,1)S(1)}, bf16[16,256]{1,0:T(8,128)(2,1)S(1)}, u32[]{:S(2)}, u32[]{:S(2)}) collective-permute-start(bf16[16,256]{1,0:T(8,128)(2,1)S(1)} %get-tuple-element.36.refs_0_), channel_id=1, source_target_pairs={{0,3},{1,2},{2,1},{3,0},{4,7},{5,6},{6,5},{7,4},{8,11},{9,10},{10,... | collective-permute-start | bytes 24584 | tf_op jit(solution)/shard_map/ppermute | solution.py:382
  5.3 0.5 %collective-permute-start.3 = (bf16[16,256]{1,0:T(8,128)(2,1)S(1)}, bf16[16,256]{1,0:T(8,128)(2,1)S(1)}, u32[]{:S(2)}, u32[]{:S(2)}) collective-permute-start(bf16[16,256]{1,0:T(8,128)(2,1)S(1)} %get-tuple-element.36.refs_0_), channel_id=1, source_target_pairs={{0,2},{1,3},{2,0},{3,1},{4,6},{5,7},{6,4},{7,5},{8,10},{9,11},{10,... | collective-permute-start | bytes 24584 | tf_op jit(solution)/shard_map/ppermute | solution.py:382
  5.8 0.5 %collective-permute-start.4 = (bf16[16,256]{1,0:T(8,128)(2,1)S(1)}, bf16[16,256]{1,0:T(8,128)(2,1)S(1)}, u32[]{:S(2)}, u32[]{:S(2)}) collective-permute-start(bf16[16,256]{1,0:T(8,128)(2,1)S(1)} %get-tuple-element.36.refs_0_), channel_id=1, source_target_pairs={{0,1},{1,0},{2,3},{3,2},{4,5},{5,4},{6,7},{7,6},{8,9},{9,8},{10,11... | collective-permute-start | bytes 24584 | tf_op jit(solution)/shard_map/ppermute | solution.py:382
  6.3 0.0 collective-permute-done.1.other_taps_ref
  6.4 0.9 %shard_map.83 = (bf16[64,128,128]{2,1,0:T(8,128)(2,1)S(1)}, bf16[64,128,128]{2,1,0:T(8,128)(2,1)S(1)}, bf16[128,128]{1,0:T(8,128)(2,1)S(1)}, f32[128,128]{1,0:T(8,128)S(1)}, f32[2,128]{1,0:T(2,128)S(1)}) custom-call(bf16[64,512]{1,0:T(8,128)(2,1)S(1)} %get-tuple-element.31.taps_ref, bf16[64,512]{1,0:T(8,128)(2,1)S(1)} %collective-permute-done.1.other_taps_ref, ...), custom_call_target="tpu_custom_call" | custom-call | flops 300000000 | tf_op jit(solution)/shard_map/pallas_call | solution.py:363
  7.3 0.7 %shard_map.84 = (f32[128,1024]{1,0:T(8,128)S(1)}, bf16[128,1024]{1,0:T(8,128)(2,1)S(1)}) custom-call(bf16[128,1024]{1,0:T(8,128)(2,1)S(1)} %get-tuple-element.29.product_ref, bf16[128,1024]{1,0:T(8,128)(2,1)S(1)} %get-tuple-element.30.query_ref, bf16[64,128,128]{2,1,0:T(8,128)(2,1)S(1)} %get-tuple-element.34.current_ref), custom_call_target="tpu_custom_call" | custom-call | flops 300000000 | tf_op jit(solution)/shard_map/pallas_call | solution.py:363
  8.0 0.0 collective-permute-done.2.refs_1_
  8.0 0.9 %collective-permute-done.3.refs_2_ = bf16[16,256]{1,0:T(8,128)(2,1)S(1)} collective-permute-done((bf16[16,256]{1,0:T(8,128)(2,1)S(1)}, bf16[16,256]{1,0:T(8,128)(2,1)S(1)}, u32[]{:S(2)}, u32[]{:S(2)}) %collective-permute-start.3) | collective-permute-done | bytes 8224 | tf_op jit(solution)/shard_map/ppermute | solution.py:382
  9.0 0.5 %collective-permute-done.4.refs_3_ = bf16[16,256]{1,0:T(8,128)(2,1)S(1)} collective-permute-done((bf16[16,256]{1,0:T(8,128)(2,1)S(1)}, bf16[16,256]{1,0:T(8,128)(2,1)S(1)}, u32[]{:S(2)}, u32[]{:S(2)}) %collective-permute-start.4) | collective-permute-done | bytes 8224 | tf_op jit(solution)/shard_map/ppermute | solution.py:382
  9.5 0.4 %shard_map.86 = (bf16[128,1024]{1,0:T(8,128)(2,1)S(1)}, f32[32,1024]{1,0:T(8,128)S(1)}, f32[16,1024]{1,0:T(8,128)S(1)}, f32[16,1024]{1,0:T(8,128)S(1)}) custom-call(bf16[16,256]{1,0:T(8,128)(2,1)S(1)} %get-tuple-element.36.refs_0_, bf16[16,256]{1,0:T(8,128)(2,1)S(1)} %collective-permute-done.2.refs_1_, bf16[16,256]{1,0:T(8,128)(2,1)S(1)} %collective-permute-done.3.refs_2_, ...), custom_call_target="tpu_custom_call" | custom-call | flops 300000000 | tf_op jit(solution)/shard_map/pallas_call | solution.py:363
  9.8 0.4 %shard_map.87._.rows_ref = f32[64,128]{1,0:T(8,128)S(1)} custom-call(f32[32,1024]{1,0:T(8,128)S(1)} %get-tuple-element.44.channels_ref, bf16[16,1024]{1,0:T(8,128)(2,1)S(1)} %shard_map.85.refs_9_._), custom_call_target="tpu_custom_call" | custom-call | flops 300000000 | tf_op jit(solution)/shard_map/pallas_call | solution.py:363
  10.2 0.0 collective-permute-done.halo_ref
  10.2 0.9 %shard_map.88 = (bf16[128,1024]{1,0:T(8,128)(2,1)S(1)}, bf16[16,1024]{1,0:T(8,128)(2,1)S(1)}) custom-call(bf16[128,1024]{1,0:T(8,128)(2,1)S(1)} %collective-permute-done.halo_ref, bf16[128,1024]{1,0:T(8,128)(2,1)S(1)} %get-tuple-element.30.query_ref, bf16[64,128,128]{2,1,0:T(8,128)(2,1)S(1)} %get-tuple-element.33.previous_ref, ...), custom_call_target="tpu_custom_call" | custom-call | flops 300000000 | tf_op jit(solution)/shard_map/pallas_call | solution.py:363
  11.2 2.2 %collective-permute-done.5.first_ref = bf16[16,1024]{1,0:T(8,128)(2,1)S(1)} collective-permute-done((bf16[16,1024]{1,0:T(8,128)(2,1)S(1)}, bf16[16,1024]{1,0:T(8,128)(2,1)S(1)}, u32[]{:S(2)}, u32[]{:S(2)}) %collective-permute-start.5) | collective-permute-done | bytes 32800 | tf_op jit(solution)/shard_map/ppermute | solution.py:393
  13.4 0.1 collective-permute-start.6
  13.5 0.6 %collective-permute-start.7 = (bf16[16,1024]{1,0:T(8,128)(2,1)S(1)}, bf16[16,1024]{1,0:T(8,128)(2,1)S(1)}, u32[]{:S(2)}, u32[]{:S(2)}) collective-permute-start(bf16[16,1024]{1,0:T(8,128)(2,1)S(1)} %add_convert_fusion), channel_id=1, source_target_pairs={{0,16},{4,8},{8,20},{12,28},{16,0},{20,24},{24,4},{28,12},{1,17},{... | collective-permute-start | bytes 98312 | tf_op jit(solution)/shard_map/ppermute | solution.py:393
  14.0 1.3 %collective-permute-start.8 = (bf16[16,1024]{1,0:T(8,128)(2,1)S(1)}, bf16[16,1024]{1,0:T(8,128)(2,1)S(1)}, u32[]{:S(2)}, u32[]{:S(2)}) collective-permute-start(bf16[16,1024]{1,0:T(8,128)(2,1)S(1)} %get-tuple-element.50), channel_id=1, source_target_pairs={{0,16},{4,20},{8,12},{12,8},{16,0},{20,4},{24,28},{28,24},{1,17},{... | collective-permute-start | bytes 98312 | tf_op jit(solution)/shard_map/ppermute | solution.py:393
  15.3 0.9 %shard_map.89 = (f32[128,1024]{1,0:T(8,128)S(1)}, bf16[128,1024]{1,0:T(8,128)(2,1)S(1)}) custom-call(bf16[128,1024]{1,0:T(8,128)(2,1)S(1)} %get-tuple-element.45.gated_ref, f32[64,128]{1,0:T(8,128)S(1)} %shard_map.87._.rows_ref, bf16[128,128]{1,0:T(8,128)(2,1)S(1)} %get-tuple-element.46.same_ref, f32[128,128]{1,0:T(8,128)S(1)} %get-tuple-element.40.refs_6_.refs_7_.doc_ref, ...), custom_call_target="tpu_custom_call" | custom-call | flops 300000000 | tf_op jit(solution)/shard_map/pallas_call | solution.py:363
  16.2 0.6 %collective-permute-done.6.far_ref = bf16[16,1024]{1,0:T(8,128)(2,1)S(1)} collective-permute-done((bf16[16,1024]{1,0:T(8,128)(2,1)S(1)}, bf16[16,1024]{1,0:T(8,128)(2,1)S(1)}, u32[]{:S(2)}, u32[]{:S(2)}) %collective-permute-start.6) | collective-permute-done | bytes 32800 | tf_op jit(solution)/shard_map/ppermute | solution.py:393
  16.8 0.4 %collective-permute-done.7.middle_ref = bf16[16,1024]{1,0:T(8,128)(2,1)S(1)} collective-permute-done((bf16[16,1024]{1,0:T(8,128)(2,1)S(1)}, bf16[16,1024]{1,0:T(8,128)(2,1)S(1)}, u32[]{:S(2)}, u32[]{:S(2)}) %collective-permute-start.7) | collective-permute-done | bytes 32800 | tf_op jit(solution)/shard_map/ppermute | solution.py:393
  17.2 0.9 %shard_map.90 = bf16[128,1024]{1,0:T(8,128)(2,1)} custom-call(f32[128,1024]{1,0:T(8,128)S(1)} %get-tuple-element.48.part_ref, bf16[128,1024]{1,0:T(8,128)(2,1)S(1)} %get-tuple-element.49.carry_ref, bf16[16,1024]{1,0:T(8,128)(2,1)S(1)} %collective-permute-done.5.first_ref, bf16[16,1024]{1,0:T(8,128)(2,1)S(1)} %collective-permute-done.6.far_ref, ...), custom_call_target="tpu_custom_call" | custom-call | flops 300000000 | tf_op jit(solution)/shard_map/pallas_call | solution.py:363
  (4 shorter events, 0.0 us)
Async XLA Ops:
  1.2 9.0 %collective-permute-start = (bf16[128,1024]{1,0:T(8,128)(2,1)S(1)}, bf16[128,1024]{1,0:T(8,128)(2,1)S(1)}, u32[]{:S(2)}, u32[]{:S(2)}) collective-permute-start(bf16[128,1024]{1,0:T(8,128)(2,1)S(1)} %get-tuple-element.29.product_ref), channel_id=1, source_target_pairs={{0,4},{4,8},{8,12},{12,0},{1,5},{5,9},{9,13},{13,1},{2,6},{6,10},{... | collective-permute-start | bytes 786440 | tf_op jit(solution)/shard_map/ppermute | solution.py:451
  2.9 3.5 %collective-permute-start.1 = (bf16[64,512]{1,0:T(8,128)(2,1)}, bf16[64,512]{1,0:T(8,128)(2,1)S(1)}, u32[]{:S(2)}, u32[]{:S(2)}) collective-permute-start(bf16[64,512]{1,0:T(8,128)(2,1)} %bitcast.12), channel_id=1, source_target_pairs={{0,16},{16,0},{1,17},{17,1},{2,18},{18,2},{3,19},{19,3},{4,20},{20... | collective-permute-start | bytes 196616 | tf_op jit(solution)/shard_map/ppermute | solution.py:382
  2.9 5.2 %collective-permute-start.2 = (bf16[16,256]{1,0:T(8,128)(2,1)S(1)}, bf16[16,256]{1,0:T(8,128)(2,1)S(1)}, u32[]{:S(2)}, u32[]{:S(2)}) collective-permute-start(bf16[16,256]{1,0:T(8,128)(2,1)S(1)} %get-tuple-element.36.refs_0_), channel_id=1, source_target_pairs={{0,3},{1,2},{2,1},{3,0},{4,7},{5,6},{6,5},{7,4},{8,11},{9,10},{10,... | collective-permute-start | bytes 24584 | tf_op jit(solution)/shard_map/ppermute | solution.py:382
  5.3 3.7 %collective-permute-start.3 = (bf16[16,256]{1,0:T(8,128)(2,1)S(1)}, bf16[16,256]{1,0:T(8,128)(2,1)S(1)}, u32[]{:S(2)}, u32[]{:S(2)}) collective-permute-start(bf16[16,256]{1,0:T(8,128)(2,1)S(1)} %get-tuple-element.36.refs_0_), channel_id=1, source_target_pairs={{0,2},{1,3},{2,0},{3,1},{4,6},{5,7},{6,4},{7,5},{8,10},{9,11},{10,... | collective-permute-start | bytes 24584 | tf_op jit(solution)/shard_map/ppermute | solution.py:382
  5.8 3.7 %collective-permute-start.4 = (bf16[16,256]{1,0:T(8,128)(2,1)S(1)}, bf16[16,256]{1,0:T(8,128)(2,1)S(1)}, u32[]{:S(2)}, u32[]{:S(2)}) collective-permute-start(bf16[16,256]{1,0:T(8,128)(2,1)S(1)} %get-tuple-element.36.refs_0_), channel_id=1, source_target_pairs={{0,1},{1,0},{2,3},{3,2},{4,5},{5,4},{6,7},{7,6},{8,9},{9,8},{10,11... | collective-permute-start | bytes 24584 | tf_op jit(solution)/shard_map/ppermute | solution.py:382
  9.5 3.9 %collective-permute-start.5 = (bf16[16,1024]{1,0:T(8,128)(2,1)S(1)}, bf16[16,1024]{1,0:T(8,128)(2,1)S(1)}, u32[]{:S(2)}, u32[]{:S(2)}) collective-permute-start(bf16[16,1024]{1,0:T(8,128)(2,1)S(1)} %shard_map.85.refs_9_._), channel_id=1, source_target_pairs={{0,4},{4,16},{8,24},{12,28},{16,20},{20,0},{24,8},{28,12},{1,5},{5... | collective-permute-start | bytes 98312 | tf_op jit(solution)/shard_map/ppermute | solution.py:393
  13.4 3.4 %collective-permute-start.6 = (bf16[16,1024]{1,0:T(8,128)(2,1)S(1)}, bf16[16,1024]{1,0:T(8,128)(2,1)S(1)}, u32[]{:S(2)}, u32[]{:S(2)}) collective-permute-start(bf16[16,1024]{1,0:T(8,128)(2,1)S(1)} %add_convert_fusion), channel_id=1, source_target_pairs={{0,16},{4,12},{8,20},{12,8},{16,0},{20,28},{24,4},{28,24},{1,17},{... | collective-permute-start | bytes 98312 | tf_op jit(solution)/shard_map/ppermute | solution.py:393
  13.5 3.7 %collective-permute-start.7 = (bf16[16,1024]{1,0:T(8,128)(2,1)S(1)}, bf16[16,1024]{1,0:T(8,128)(2,1)S(1)}, u32[]{:S(2)}, u32[]{:S(2)}) collective-permute-start(bf16[16,1024]{1,0:T(8,128)(2,1)S(1)} %add_convert_fusion), channel_id=1, source_target_pairs={{0,16},{4,8},{8,20},{12,28},{16,0},{20,24},{24,4},{28,12},{1,17},{... | collective-permute-start | bytes 98312 | tf_op jit(solution)/shard_map/ppermute | solution.py:393
  14.0 3.1 %collective-permute-start.8 = (bf16[16,1024]{1,0:T(8,128)(2,1)S(1)}, bf16[16,1024]{1,0:T(8,128)(2,1)S(1)}, u32[]{:S(2)}, u32[]{:S(2)}) collective-permute-start(bf16[16,1024]{1,0:T(8,128)(2,1)S(1)} %get-tuple-element.50), channel_id=1, source_target_pairs={{0,16},{4,20},{8,12},{12,8},{16,0},{20,4},{24,28},{28,24},{1,17},{... | collective-permute-start | bytes 98312 | tf_op jit(solution)/shard_map/ppermute | solution.py:393

commit v9 on v8

--- a/solution.py
+++ b/solution.py
@@ -336,7 +336,7 @@
 
 
 def finish_kernel(
-    four, part_ref, carry_ref, first_ref, far_ref, middle_ref, near_ref, through_ref, out_ref
+    four, part_ref, carry_ref, first_ref, far_ref, middle_ref, near_ref, through_ref, out_hbm, out_ref, leaving
 ):
     width = part_ref.shape[1]
     modes = near_ref.shape[0]
@@ -349,22 +349,32 @@
         entering = jnp.where(place == 3, entering, 0.0)
         entering += jnp.where(place == 1, first_ref[...].astype(jnp.float32), 0.0)
         entering += jnp.where(place == 2, middle_ref[...].astype(jnp.float32), 0.0)
-    for slab in range(width // LANES):
-        lanes = slice(slab * LANES, (slab + 1) * LANES)
+    copies = []
+    for slab, lanes in enumerate(slabs_of(width)):
         state = jnp.concatenate([entering[:, lanes]] * per_slab, axis=0)
         spread = jnp.where(diagonal, state, 0.0).astype(jnp.bfloat16)
         out_ref[:, lanes] = (part_ref[:, lanes] + dot(carry_ref[:, lanes], spread)).astype(
             out_ref.dtype
         )
-
-
-def call(kernel, outs, *args, spaces=None, scratch=(), micros=0.3):
+        if slab % 2 == 1:
+            pair = pl.ds((slab - 1) * LANES, 2 * LANES)
+            copies.append(
+                pltpu.make_async_copy(
+                    out_ref.at[:, pair], out_hbm.at[:, pair], leaving.at[slab // 2]
+                )
+            )
+            copies[-1].start()
+    for copy in copies:
+        copy.wait()
+
+
+def call(kernel, outs, *args, spaces=None, scratch=(), micros=0.3, result=pltpu.VMEM):
     spaces = spaces or [pltpu.VMEM] * len(args)
     return pl.pallas_call(
         kernel,
         out_shape=[jax.ShapeDtypeStruct(shape, dtype) for shape, dtype in outs],
         in_specs=[pl.BlockSpec(memory_space=space) for space in spaces],
-        out_specs=[pl.BlockSpec(memory_space=pltpu.VMEM)] * len(outs),
+        out_specs=[pl.BlockSpec(memory_space=result)] * len(outs),
         scratch_shapes=list(scratch),
         cost_estimate=pl.CostEstimate(
             flops=int(micros * 1e9), bytes_accessed=0, transcendentals=0
@@ -538,6 +548,11 @@
         middle,
         near,
         far_through,
+        scratch=[
+            pltpu.VMEM((tokens, width), half),
+            pltpu.SemaphoreType.DMA((width // LANES // 2,)),
+        ],
+        result=pltpu.HBM,
     )
     return out[None]
 

time: 18.2 us -> 18.2 us (level)
  no operation moved by 1% of the time
where the time goes in v9:
time: 18.2 us; the launch traced here: 18.1 us
  starting transfers between devices  7.03 us (39%)
  Pallas kernels  6.35 us (35%)
  waiting for transfers between devices  4.59 us (25%)
    pallas_call x9, Pallas kernels, call(): pl.pallas_call(kernel, out_shape=[jax.ShapeDtypeStruct(shape, dtype) for...  6.35 us
    ppermute x4, starting transfers between devices, exchanged(): lax.ppermute(array, axis, [(i, i ^ bit) for i in range(lax.axis_size(axis...  3.49 us
    ppermute x4, waiting for transfers between devices, cycled(): return lax.ppermute(array, ('fsdp', 'ctx'), moves)  3.16 us
    ppermute x4, starting transfers between devices, cycled(): return lax.ppermute(array, ('fsdp', 'ctx'), moves)  1.91 us
    ppermute x1, starting transfers between devices, body(): lax.ppermute(product, 'ctx', [(i, (i + 1) % ctx_size) for i in range(ctx_...  1.63 us
    ppermute x4, waiting for transfers between devices, exchanged(): lax.ppermute(array, axis, [(i, i ^ bit) for i in range(lax.axis_size(axis...  1.43 us
  transfers between devices with their start and end apart: 9, of which 5 were waited for; matrix products, arithmetic and copies ran while one was open for 0% of the time, Pallas kernels for 23%

profile of v9, /device:TPU:8, one launch (start us, length us, event | category | flops | bytes accessed | tf_op | source)
XLA Modules:
  0.0 18.1 jit_solution(16129441561939047814)
XLA Ops:
  0.0 1.2 %shard_map.82 = (bf16[128,1024]{1,0:T(8,128)(2,1)S(1)}, bf16[16,256]{1,0:T(8,128)(2,1)S(1)}, bf16[128,1024]{1,0:T(8,128)(2,1)S(1)}, bf16[32,64]{1,0:T(8,128)(2,1...) custom-call(bf16[128,1024]{1,0:T(8,128)(2,1)} %bitcast.8, ...), custom_call_target="tpu_custom_call" | custom-call | flops 300000000 | tf_op jit(solution)/shard_map/pallas_call | solution.py:373
  1.2 1.6 %collective-permute-start = (bf16[128,1024]{1,0:T(8,128)(2,1)S(1)}, bf16[128,1024]{1,0:T(8,128)(2,1)S(1)}, u32[]{:S(2)}, u32[]{:S(2)}) collective-permute-start(bf16[128,1024]{1,0:T(8,128)(2,1)S(1)} %get-tuple-element.29.product_ref), channel_id=1, source_target_pairs={{0,4},{4,8},{8,12},{12,0},{1,5},{5,9},{9,13},{13,1},{2,6},{6,10},{... | collective-permute-start | bytes 786440 | tf_op jit(solution)/shard_map/ppermute | solution.py:461
  2.9 0.0 collective-permute-start.1
  2.9 2.4 %collective-permute-start.2 = (bf16[16,256]{1,0:T(8,128)(2,1)S(1)}, bf16[16,256]{1,0:T(8,128)(2,1)S(1)}, u32[]{:S(2)}, u32[]{:S(2)}) collective-permute-start(bf16[16,256]{1,0:T(8,128)(2,1)S(1)} %get-tuple-element.36.refs_0_), channel_id=1, source_target_pairs={{0,3},{1,2},{2,1},{3,0},{4,7},{5,6},{6,5},{7,4},{8,11},{9,10},{10,... | collective-permute-start | bytes 24584 | tf_op jit(solution)/shard_map/ppermute | solution.py:392
  5.3 0.5 %collective-permute-start.3 = (bf16[16,256]{1,0:T(8,128)(2,1)S(1)}, bf16[16,256]{1,0:T(8,128)(2,1)S(1)}, u32[]{:S(2)}, u32[]{:S(2)}) collective-permute-start(bf16[16,256]{1,0:T(8,128)(2,1)S(1)} %get-tuple-element.36.refs_0_), channel_id=1, source_target_pairs={{0,2},{1,3},{2,0},{3,1},{4,6},{5,7},{6,4},{7,5},{8,10},{9,11},{10,... | collective-permute-start | bytes 24584 | tf_op jit(solution)/shard_map/ppermute | solution.py:392
  5.8 0.5 %collective-permute-start.4 = (bf16[16,256]{1,0:T(8,128)(2,1)S(1)}, bf16[16,256]{1,0:T(8,128)(2,1)S(1)}, u32[]{:S(2)}, u32[]{:S(2)}) collective-permute-start(bf16[16,256]{1,0:T(8,128)(2,1)S(1)} %get-tuple-element.36.refs_0_), channel_id=1, source_target_pairs={{0,1},{1,0},{2,3},{3,2},{4,5},{5,4},{6,7},{7,6},{8,9},{9,8},{10,11... | collective-permute-start | bytes 24584 | tf_op jit(solution)/shard_map/ppermute | solution.py:392
  6.3 0.0 collective-permute-done.1.other_taps_ref
  6.4 0.9 %shard_map.83 = (bf16[64,128,128]{2,1,0:T(8,128)(2,1)S(1)}, bf16[64,128,128]{2,1,0:T(8,128)(2,1)S(1)}, bf16[128,128]{1,0:T(8,128)(2,1)S(1)}, f32[128,128]{1,0:T(8,128)S(1)}, f32[2,128]{1,0:T(2,128)S(1)}) custom-call(bf16[64,512]{1,0:T(8,128)(2,1)S(1)} %get-tuple-element.31.taps_ref, bf16[64,512]{1,0:T(8,128)(2,1)S(1)} %collective-permute-done.1.other_taps_ref, ...), custom_call_target="tpu_custom_call" | custom-call | flops 300000000 | tf_op jit(solution)/shard_map/pallas_call | solution.py:373
  7.3 0.7 %shard_map.84 = (f32[128,1024]{1,0:T(8,128)S(1)}, bf16[128,1024]{1,0:T(8,128)(2,1)S(1)}) custom-call(bf16[128,1024]{1,0:T(8,128)(2,1)S(1)} %get-tuple-element.29.product_ref, bf16[128,1024]{1,0:T(8,128)(2,1)S(1)} %get-tuple-element.30.query_ref, bf16[64,128,128]{2,1,0:T(8,128)(2,1)S(1)} %get-tuple-element.34.current_ref), custom_call_target="tpu_custom_call" | custom-call | flops 300000000 | tf_op jit(solution)/shard_map/pallas_call | solution.py:373
  8.0 0.0 collective-permute-done.2.refs_1_
  8.0 0.9 %collective-permute-done.3.refs_2_ = bf16[16,256]{1,0:T(8,128)(2,1)S(1)} collective-permute-done((bf16[16,256]{1,0:T(8,128)(2,1)S(1)}, bf16[16,256]{1,0:T(8,128)(2,1)S(1)}, u32[]{:S(2)}, u32[]{:S(2)}) %collective-permute-start.3) | collective-permute-done | bytes 8224 | tf_op jit(solution)/shard_map/ppermute | solution.py:392
  9.0 0.5 %collective-permute-done.4.refs_3_ = bf16[16,256]{1,0:T(8,128)(2,1)S(1)} collective-permute-done((bf16[16,256]{1,0:T(8,128)(2,1)S(1)}, bf16[16,256]{1,0:T(8,128)(2,1)S(1)}, u32[]{:S(2)}, u32[]{:S(2)}) %collective-permute-start.4) | collective-permute-done | bytes 8224 | tf_op jit(solution)/shard_map/ppermute | solution.py:392
  9.5 0.0 collective-permute-start.5
  9.5 0.4 %shard_map.86 = (bf16[128,1024]{1,0:T(8,128)(2,1)S(1)}, f32[32,1024]{1,0:T(8,128)S(1)}, f32[16,1024]{1,0:T(8,128)S(1)}, f32[16,1024]{1,0:T(8,128)S(1)}) custom-call(bf16[16,256]{1,0:T(8,128)(2,1)S(1)} %get-tuple-element.36.refs_0_, bf16[16,256]{1,0:T(8,128)(2,1)S(1)} %collective-permute-done.2.refs_1_, bf16[16,256]{1,0:T(8,128)(2,1)S(1)} %collective-permute-done.3.refs_2_, ...), custom_call_target="tpu_custom_call" | custom-call | flops 300000000 | tf_op jit(solution)/shard_map/pallas_call | solution.py:373
  9.8 0.4 %shard_map.87._.rows_ref = f32[64,128]{1,0:T(8,128)S(1)} custom-call(f32[32,1024]{1,0:T(8,128)S(1)} %get-tuple-element.44.channels_ref, bf16[16,1024]{1,0:T(8,128)(2,1)S(1)} %shard_map.85.refs_9_._), custom_call_target="tpu_custom_call" | custom-call | flops 300000000 | tf_op jit(solution)/shard_map/pallas_call | solution.py:373
  10.2 0.9 %shard_map.88 = (bf16[128,1024]{1,0:T(8,128)(2,1)S(1)}, bf16[16,1024]{1,0:T(8,128)(2,1)S(1)}) custom-call(bf16[128,1024]{1,0:T(8,128)(2,1)S(1)} %collective-permute-done.halo_ref, bf16[128,1024]{1,0:T(8,128)(2,1)S(1)} %get-tuple-element.30.query_ref, bf16[64,128,128]{2,1,0:T(8,128)(2,1)S(1)} %get-tuple-element.33.previous_ref, ...), custom_call_target="tpu_custom_call" | custom-call | flops 300000000 | tf_op jit(solution)/shard_map/pallas_call | solution.py:373
  11.2 2.2 %collective-permute-done.5.first_ref = bf16[16,1024]{1,0:T(8,128)(2,1)S(1)} collective-permute-done((bf16[16,1024]{1,0:T(8,128)(2,1)S(1)}, bf16[16,1024]{1,0:T(8,128)(2,1)S(1)}, u32[]{:S(2)}, u32[]{:S(2)}) %collective-permute-start.5) | collective-permute-done | bytes 32800 | tf_op jit(solution)/shard_map/ppermute | solution.py:403
  13.4 0.1 collective-permute-start.6
  13.5 0.6 %collective-permute-start.7 = (bf16[16,1024]{1,0:T(8,128)(2,1)S(1)}, bf16[16,1024]{1,0:T(8,128)(2,1)S(1)}, u32[]{:S(2)}, u32[]{:S(2)}) collective-permute-start(bf16[16,1024]{1,0:T(8,128)(2,1)S(1)} %add_convert_fusion), channel_id=1, source_target_pairs={{0,16},{4,8},{8,20},{12,28},{16,0},{20,24},{24,4},{28,12},{1,17},{... | collective-permute-start | bytes 98312 | tf_op jit(solution)/shard_map/ppermute | solution.py:403
  14.0 1.3 %collective-permute-start.8 = (bf16[16,1024]{1,0:T(8,128)(2,1)S(1)}, bf16[16,1024]{1,0:T(8,128)(2,1)S(1)}, u32[]{:S(2)}, u32[]{:S(2)}) collective-permute-start(bf16[16,1024]{1,0:T(8,128)(2,1)S(1)} %get-tuple-element.50), channel_id=1, source_target_pairs={{0,16},{4,20},{8,12},{12,8},{16,0},{20,4},{24,28},{28,24},{1,17},{... | collective-permute-start | bytes 98312 | tf_op jit(solution)/shard_map/ppermute | solution.py:403
  15.3 0.9 %shard_map.89 = (f32[128,1024]{1,0:T(8,128)S(1)}, bf16[128,1024]{1,0:T(8,128)(2,1)S(1)}) custom-call(bf16[128,1024]{1,0:T(8,128)(2,1)S(1)} %get-tuple-element.45.gated_ref, f32[64,128]{1,0:T(8,128)S(1)} %shard_map.87._.rows_ref, bf16[128,128]{1,0:T(8,128)(2,1)S(1)} %get-tuple-element.46.same_ref, f32[128,128]{1,0:T(8,128)S(1)} %get-tuple-element.40.refs_6_.refs_7_.doc_ref, ...), custom_call_target="tpu_custom_call" | custom-call | flops 300000000 | tf_op jit(solution)/shard_map/pallas_call | solution.py:373
  16.2 0.6 %collective-permute-done.6.far_ref = bf16[16,1024]{1,0:T(8,128)(2,1)S(1)} collective-permute-done((bf16[16,1024]{1,0:T(8,128)(2,1)S(1)}, bf16[16,1024]{1,0:T(8,128)(2,1)S(1)}, u32[]{:S(2)}, u32[]{:S(2)}) %collective-permute-start.6) | collective-permute-done | bytes 32800 | tf_op jit(solution)/shard_map/ppermute | solution.py:403
  16.8 0.4 %collective-permute-done.7.middle_ref = bf16[16,1024]{1,0:T(8,128)(2,1)S(1)} collective-permute-done((bf16[16,1024]{1,0:T(8,128)(2,1)S(1)}, bf16[16,1024]{1,0:T(8,128)(2,1)S(1)}, u32[]{:S(2)}, u32[]{:S(2)}) %collective-permute-start.7) | collective-permute-done | bytes 32800 | tf_op jit(solution)/shard_map/ppermute | solution.py:403
  17.2 0.9 %shard_map.90 = bf16[128,1024]{1,0:T(8,128)(2,1)} custom-call(f32[128,1024]{1,0:T(8,128)S(1)} %get-tuple-element.48.part_ref, bf16[128,1024]{1,0:T(8,128)(2,1)S(1)} %get-tuple-element.49.carry_ref, bf16[16,1024]{1,0:T(8,128)(2,1)S(1)} %collective-permute-done.5.first_ref, bf16[16,1024]{1,0:T(8,128)(2,1)S(1)} %collective-permute-done.6.far_ref, ...), custom_call_target="tpu_custom_call" | custom-call | flops 300000000 | tf_op jit(solution)/shard_map/pallas_call | solution.py:373
  (4 shorter events, 0.0 us)
Async XLA Ops:
  1.2 9.0 %collective-permute-start = (bf16[128,1024]{1,0:T(8,128)(2,1)S(1)}, bf16[128,1024]{1,0:T(8,128)(2,1)S(1)}, u32[]{:S(2)}, u32[]{:S(2)}) collective-permute-start(bf16[128,1024]{1,0:T(8,128)(2,1)S(1)} %get-tuple-element.29.product_ref), channel_id=1, source_target_pairs={{0,4},{4,8},{8,12},{12,0},{1,5},{5,9},{9,13},{13,1},{2,6},{6,10},{... | collective-permute-start | bytes 786440 | tf_op jit(solution)/shard_map/ppermute | solution.py:461
  2.9 3.5 %collective-permute-start.1 = (bf16[64,512]{1,0:T(8,128)(2,1)}, bf16[64,512]{1,0:T(8,128)(2,1)S(1)}, u32[]{:S(2)}, u32[]{:S(2)}) collective-permute-start(bf16[64,512]{1,0:T(8,128)(2,1)} %bitcast.12), channel_id=1, source_target_pairs={{0,16},{16,0},{1,17},{17,1},{2,18},{18,2},{3,19},{19,3},{4,20},{20... | collective-permute-start | bytes 196616 | tf_op jit(solution)/shard_map/ppermute | solution.py:392
  2.9 5.2 %collective-permute-start.2 = (bf16[16,256]{1,0:T(8,128)(2,1)S(1)}, bf16[16,256]{1,0:T(8,128)(2,1)S(1)}, u32[]{:S(2)}, u32[]{:S(2)}) collective-permute-start(bf16[16,256]{1,0:T(8,128)(2,1)S(1)} %get-tuple-element.36.refs_0_), channel_id=1, source_target_pairs={{0,3},{1,2},{2,1},{3,0},{4,7},{5,6},{6,5},{7,4},{8,11},{9,10},{10,... | collective-permute-start | bytes 24584 | tf_op jit(solution)/shard_map/ppermute | solution.py:392
  5.3 3.7 %collective-permute-start.3 = (bf16[16,256]{1,0:T(8,128)(2,1)S(1)}, bf16[16,256]{1,0:T(8,128)(2,1)S(1)}, u32[]{:S(2)}, u32[]{:S(2)}) collective-permute-start(bf16[16,256]{1,0:T(8,128)(2,1)S(1)} %get-tuple-element.36.refs_0_), channel_id=1, source_target_pairs={{0,2},{1,3},{2,0},{3,1},{4,6},{5,7},{6,4},{7,5},{8,10},{9,11},{10,... | collective-permute-start | bytes 24584 | tf_op jit(solution)/shard_map/ppermute | solution.py:392
  5.8 3.7 %collective-permute-start.4 = (bf16[16,256]{1,0:T(8,128)(2,1)S(1)}, bf16[16,256]{1,0:T(8,128)(2,1)S(1)}, u32[]{:S(2)}, u32[]{:S(2)}) collective-permute-start(bf16[16,256]{1,0:T(8,128)(2,1)S(1)} %get-tuple-element.36.refs_0_), channel_id=1, source_target_pairs={{0,1},{1,0},{2,3},{3,2},{4,5},{5,4},{6,7},{7,6},{8,9},{9,8},{10,11... | collective-permute-start | bytes 24584 | tf_op jit(solution)/shard_map/ppermute | solution.py:392
  9.5 3.9 %collective-permute-start.5 = (bf16[16,1024]{1,0:T(8,128)(2,1)S(1)}, bf16[16,1024]{1,0:T(8,128)(2,1)S(1)}, u32[]{:S(2)}, u32[]{:S(2)}) collective-permute-start(bf16[16,1024]{1,0:T(8,128)(2,1)S(1)} %shard_map.85.refs_9_._), channel_id=1, source_target_pairs={{0,4},{4,16},{8,24},{12,28},{16,20},{20,0},{24,8},{28,12},{1,5},{5... | collective-permute-start | bytes 98312 | tf_op jit(solution)/shard_map/ppermute | solution.py:403
  13.4 3.4 %collective-permute-start.6 = (bf16[16,1024]{1,0:T(8,128)(2,1)S(1)}, bf16[16,1024]{1,0:T(8,128)(2,1)S(1)}, u32[]{:S(2)}, u32[]{:S(2)}) collective-permute-start(bf16[16,1024]{1,0:T(8,128)(2,1)S(1)} %add_convert_fusion), channel_id=1, source_target_pairs={{0,16},{4,12},{8,20},{12,8},{16,0},{20,28},{24,4},{28,24},{1,17},{... | collective-permute-start | bytes 98312 | tf_op jit(solution)/shard_map/ppermute | solution.py:403
  13.5 3.7 %collective-permute-start.7 = (bf16[16,1024]{1,0:T(8,128)(2,1)S(1)}, bf16[16,1024]{1,0:T(8,128)(2,1)S(1)}, u32[]{:S(2)}, u32[]{:S(2)}) collective-permute-start(bf16[16,1024]{1,0:T(8,128)(2,1)S(1)} %add_convert_fusion), channel_id=1, source_target_pairs={{0,16},{4,8},{8,20},{12,28},{16,0},{20,24},{24,4},{28,12},{1,17},{... | collective-permute-start | bytes 98312 | tf_op jit(solution)/shard_map/ppermute | solution.py:403
  14.0 3.1 %collective-permute-start.8 = (bf16[16,1024]{1,0:T(8,128)(2,1)S(1)}, bf16[16,1024]{1,0:T(8,128)(2,1)S(1)}, u32[]{:S(2)}, u32[]{:S(2)}) collective-permute-start(bf16[16,1024]{1,0:T(8,128)(2,1)S(1)} %get-tuple-element.50), channel_id=1, source_target_pairs={{0,16},{4,20},{8,12},{12,8},{16,0},{20,4},{24,28},{28,24},{1,17},{... | collective-permute-start | bytes 98312 | tf_op jit(solution)/shard_map/ppermute | solution.py:403

commit v10 on v8

--- a/solution.py
+++ b/solution.py
@@ -515,7 +515,7 @@
         both = both.astype(half)
         near = cycled(state, [2, 3], ())
         middle = cycled(both, [1, 2], (2, ))
-        far = cycled(both, [1, 3, 2], (2, ))
+        far = cycled(both, [1, 3, 2], (2, 3))
     else:
         near = middle = far = entering_states(state, through)
     part, carry = call(

time: 18.2 us -> 18.2 us (level)
  no operation moved by 1% of the time
where the time goes in v10:
time: 18.2 us; the launch traced here: 18.1 us
  starting transfers between devices  7.03 us (39%)
  Pallas kernels  6.38 us (35%)
  waiting for transfers between devices  4.59 us (25%)
    pallas_call x9, Pallas kernels, call(): pl.pallas_call(kernel, out_shape=[jax.ShapeDtypeStruct(shape, dtype) for...  6.38 us
    ppermute x4, starting transfers between devices, exchanged(): lax.ppermute(array, axis, [(i, i ^ bit) for i in range(lax.axis_size(axis...  3.49 us
    ppermute x4, waiting for transfers between devices, cycled(): return lax.ppermute(array, ('fsdp', 'ctx'), moves)  3.16 us
    ppermute x4, starting transfers between devices, cycled(): return lax.ppermute(array, ('fsdp', 'ctx'), moves)  1.91 us
    ppermute x1, starting transfers between devices, body(): lax.ppermute(product, 'ctx', [(i, (i + 1) % ctx_size) for i in range(ctx_...  1.63 us
    ppermute x4, waiting for transfers between devices, exchanged(): lax.ppermute(array, axis, [(i, i ^ bit) for i in range(lax.axis_size(axis...  1.43 us
  transfers between devices with their start and end apart: 9, of which 5 were waited for; matrix products, arithmetic and copies ran while one was open for 0% of the time, Pallas kernels for 23%

profile of v10, /device:TPU:8, one launch (start us, length us, event | category | flops | bytes accessed | tf_op | source)
XLA Modules:
  0.0 18.1 jit_solution(3227663321815660319)
XLA Ops:
  0.0 1.2 %shard_map.82 = (bf16[128,1024]{1,0:T(8,128)(2,1)S(1)}, bf16[16,256]{1,0:T(8,128)(2,1)S(1)}, bf16[128,1024]{1,0:T(8,128)(2,1)S(1)}, bf16[32,64]{1,0:T(8,128)(2,1...) custom-call(bf16[128,1024]{1,0:T(8,128)(2,1)} %bitcast.8, ...), custom_call_target="tpu_custom_call" | custom-call | flops 300000000 | tf_op jit(solution)/shard_map/pallas_call | solution.py:363
  1.2 1.6 %collective-permute-start = (bf16[128,1024]{1,0:T(8,128)(2,1)S(1)}, bf16[128,1024]{1,0:T(8,128)(2,1)S(1)}, u32[]{:S(2)}, u32[]{:S(2)}) collective-permute-start(bf16[128,1024]{1,0:T(8,128)(2,1)S(1)} %get-tuple-element.29.product_ref), channel_id=1, source_target_pairs={{0,4},{4,8},{8,12},{12,0},{1,5},{5,9},{9,13},{13,1},{2,6},{6,10},{... | collective-permute-start | bytes 786440 | tf_op jit(solution)/shard_map/ppermute | solution.py:451
  2.9 0.0 collective-permute-start.1
  2.9 2.4 %collective-permute-start.2 = (bf16[16,256]{1,0:T(8,128)(2,1)S(1)}, bf16[16,256]{1,0:T(8,128)(2,1)S(1)}, u32[]{:S(2)}, u32[]{:S(2)}) collective-permute-start(bf16[16,256]{1,0:T(8,128)(2,1)S(1)} %get-tuple-element.36.refs_0_), channel_id=1, source_target_pairs={{0,3},{1,2},{2,1},{3,0},{4,7},{5,6},{6,5},{7,4},{8,11},{9,10},{10,... | collective-permute-start | bytes 24584 | tf_op jit(solution)/shard_map/ppermute | solution.py:382
  5.3 0.5 %collective-permute-start.3 = (bf16[16,256]{1,0:T(8,128)(2,1)S(1)}, bf16[16,256]{1,0:T(8,128)(2,1)S(1)}, u32[]{:S(2)}, u32[]{:S(2)}) collective-permute-start(bf16[16,256]{1,0:T(8,128)(2,1)S(1)} %get-tuple-element.36.refs_0_), channel_id=1, source_target_pairs={{0,2},{1,3},{2,0},{3,1},{4,6},{5,7},{6,4},{7,5},{8,10},{9,11},{10,... | collective-permute-start | bytes 24584 | tf_op jit(solution)/shard_map/ppermute | solution.py:382
  5.8 0.5 %collective-permute-start.4 = (bf16[16,256]{1,0:T(8,128)(2,1)S(1)}, bf16[16,256]{1,0:T(8,128)(2,1)S(1)}, u32[]{:S(2)}, u32[]{:S(2)}) collective-permute-start(bf16[16,256]{1,0:T(8,128)(2,1)S(1)} %get-tuple-element.36.refs_0_), channel_id=1, source_target_pairs={{0,1},{1,0},{2,3},{3,2},{4,5},{5,4},{6,7},{7,6},{8,9},{9,8},{10,11... | collective-permute-start | bytes 24584 | tf_op jit(solution)/shard_map/ppermute | solution.py:382
  6.3 0.0 collective-permute-done.1.other_taps_ref
  6.4 0.9 %shard_map.83 = (bf16[64,128,128]{2,1,0:T(8,128)(2,1)S(1)}, bf16[64,128,128]{2,1,0:T(8,128)(2,1)S(1)}, bf16[128,128]{1,0:T(8,128)(2,1)S(1)}, f32[128,128]{1,0:T(8,128)S(1)}, f32[2,128]{1,0:T(2,128)S(1)}) custom-call(bf16[64,512]{1,0:T(8,128)(2,1)S(1)} %get-tuple-element.31.taps_ref, bf16[64,512]{1,0:T(8,128)(2,1)S(1)} %collective-permute-done.1.other_taps_ref, ...), custom_call_target="tpu_custom_call" | custom-call | flops 300000000 | tf_op jit(solution)/shard_map/pallas_call | solution.py:363
  7.3 0.7 %shard_map.84 = (f32[128,1024]{1,0:T(8,128)S(1)}, bf16[128,1024]{1,0:T(8,128)(2,1)S(1)}) custom-call(bf16[128,1024]{1,0:T(8,128)(2,1)S(1)} %get-tuple-element.29.product_ref, bf16[128,1024]{1,0:T(8,128)(2,1)S(1)} %get-tuple-element.30.query_ref, bf16[64,128,128]{2,1,0:T(8,128)(2,1)S(1)} %get-tuple-element.34.current_ref), custom_call_target="tpu_custom_call" | custom-call | flops 300000000 | tf_op jit(solution)/shard_map/pallas_call | solution.py:363
  8.0 0.0 collective-permute-done.2.refs_1_
  8.0 0.9 %collective-permute-done.3.refs_2_ = bf16[16,256]{1,0:T(8,128)(2,1)S(1)} collective-permute-done((bf16[16,256]{1,0:T(8,128)(2,1)S(1)}, bf16[16,256]{1,0:T(8,128)(2,1)S(1)}, u32[]{:S(2)}, u32[]{:S(2)}) %collective-permute-start.3) | collective-permute-done | bytes 8224 | tf_op jit(solution)/shard_map/ppermute | solution.py:382
  9.0 0.5 %collective-permute-done.4.refs_3_ = bf16[16,256]{1,0:T(8,128)(2,1)S(1)} collective-permute-done((bf16[16,256]{1,0:T(8,128)(2,1)S(1)}, bf16[16,256]{1,0:T(8,128)(2,1)S(1)}, u32[]{:S(2)}, u32[]{:S(2)}) %collective-permute-start.4) | collective-permute-done | bytes 8224 | tf_op jit(solution)/shard_map/ppermute | solution.py:382
  9.5 0.0 collective-permute-start.5
  9.5 0.4 %shard_map.86 = (bf16[128,1024]{1,0:T(8,128)(2,1)S(1)}, f32[32,1024]{1,0:T(8,128)S(1)}, f32[16,1024]{1,0:T(8,128)S(1)}, f32[16,1024]{1,0:T(8,128)S(1)}) custom-call(bf16[16,256]{1,0:T(8,128)(2,1)S(1)} %get-tuple-element.36.refs_0_, bf16[16,256]{1,0:T(8,128)(2,1)S(1)} %collective-permute-done.2.refs_1_, bf16[16,256]{1,0:T(8,128)(2,1)S(1)} %collective-permute-done.3.refs_2_, ...), custom_call_target="tpu_custom_call" | custom-call | flops 300000000 | tf_op jit(solution)/shard_map/pallas_call | solution.py:363
  9.8 0.4 %shard_map.87._.rows_ref = f32[64,128]{1,0:T(8,128)S(1)} custom-call(f32[32,1024]{1,0:T(8,128)S(1)} %get-tuple-element.44.channels_ref, bf16[16,1024]{1,0:T(8,128)(2,1)S(1)} %shard_map.85.refs_9_._), custom_call_target="tpu_custom_call" | custom-call | flops 300000000 | tf_op jit(solution)/shard_map/pallas_call | solution.py:363
  10.2 0.9 %shard_map.88 = (bf16[128,1024]{1,0:T(8,128)(2,1)S(1)}, bf16[16,1024]{1,0:T(8,128)(2,1)S(1)}) custom-call(bf16[128,1024]{1,0:T(8,128)(2,1)S(1)} %collective-permute-done.halo_ref, bf16[128,1024]{1,0:T(8,128)(2,1)S(1)} %get-tuple-element.30.query_ref, bf16[64,128,128]{2,1,0:T(8,128)(2,1)S(1)} %get-tuple-element.33.previous_ref, ...), custom_call_target="tpu_custom_call" | custom-call | flops 300000000 | tf_op jit(solution)/shard_map/pallas_call | solution.py:363
  11.2 2.2 %collective-permute-done.5.first_ref = bf16[16,1024]{1,0:T(8,128)(2,1)S(1)} collective-permute-done((bf16[16,1024]{1,0:T(8,128)(2,1)S(1)}, bf16[16,1024]{1,0:T(8,128)(2,1)S(1)}, u32[]{:S(2)}, u32[]{:S(2)}) %collective-permute-start.5) | collective-permute-done | bytes 32800 | tf_op jit(solution)/shard_map/ppermute | solution.py:393
  13.4 0.1 collective-permute-start.6
  13.5 0.6 %collective-permute-start.7 = (bf16[16,1024]{1,0:T(8,128)(2,1)S(1)}, bf16[16,1024]{1,0:T(8,128)(2,1)S(1)}, u32[]{:S(2)}, u32[]{:S(2)}) collective-permute-start(bf16[16,1024]{1,0:T(8,128)(2,1)S(1)} %add_convert_fusion), channel_id=1, source_target_pairs={{0,16},{4,8},{8,20},{12,28},{16,0},{20,24},{24,4},{28,12},{1,17},{... | collective-permute-start | bytes 98312 | tf_op jit(solution)/shard_map/ppermute | solution.py:393
  14.0 1.3 %collective-permute-start.8 = (bf16[16,1024]{1,0:T(8,128)(2,1)S(1)}, bf16[16,1024]{1,0:T(8,128)(2,1)S(1)}, u32[]{:S(2)}, u32[]{:S(2)}) collective-permute-start(bf16[16,1024]{1,0:T(8,128)(2,1)S(1)} %get-tuple-element.50), channel_id=1, source_target_pairs={{0,16},{4,20},{8,12},{12,8},{16,0},{20,4},{24,28},{28,24},{1,17},{... | collective-permute-start | bytes 98312 | tf_op jit(solution)/shard_map/ppermute | solution.py:393
  15.3 0.9 %shard_map.89 = (f32[128,1024]{1,0:T(8,128)S(1)}, bf16[128,1024]{1,0:T(8,128)(2,1)S(1)}) custom-call(bf16[128,1024]{1,0:T(8,128)(2,1)S(1)} %get-tuple-element.45.gated_ref, f32[64,128]{1,0:T(8,128)S(1)} %shard_map.87._.rows_ref, bf16[128,128]{1,0:T(8,128)(2,1)S(1)} %get-tuple-element.46.same_ref, f32[128,128]{1,0:T(8,128)S(1)} %get-tuple-element.40.refs_6_.refs_7_.doc_ref, ...), custom_call_target="tpu_custom_call" | custom-call | flops 300000000 | tf_op jit(solution)/shard_map/pallas_call | solution.py:363
  16.2 0.6 %collective-permute-done.6.far_ref = bf16[16,1024]{1,0:T(8,128)(2,1)S(1)} collective-permute-done((bf16[16,1024]{1,0:T(8,128)(2,1)S(1)}, bf16[16,1024]{1,0:T(8,128)(2,1)S(1)}, u32[]{:S(2)}, u32[]{:S(2)}) %collective-permute-start.6) | collective-permute-done | bytes 32800 | tf_op jit(solution)/shard_map/ppermute | solution.py:393
  16.8 0.4 %collective-permute-done.7.middle_ref = bf16[16,1024]{1,0:T(8,128)(2,1)S(1)} collective-permute-done((bf16[16,1024]{1,0:T(8,128)(2,1)S(1)}, bf16[16,1024]{1,0:T(8,128)(2,1)S(1)}, u32[]{:S(2)}, u32[]{:S(2)}) %collective-permute-start.7) | collective-permute-done | bytes 32800 | tf_op jit(solution)/shard_map/ppermute | solution.py:393
  17.2 0.9 %shard_map.90 = bf16[128,1024]{1,0:T(8,128)(2,1)} custom-call(f32[128,1024]{1,0:T(8,128)S(1)} %get-tuple-element.48.part_ref, bf16[128,1024]{1,0:T(8,128)(2,1)S(1)} %get-tuple-element.49.carry_ref, bf16[16,1024]{1,0:T(8,128)(2,1)S(1)} %collective-permute-done.5.first_ref, bf16[16,1024]{1,0:T(8,128)(2,1)S(1)} %collective-permute-done.6.far_ref, ...), custom_call_target="tpu_custom_call" | custom-call | flops 300000000 | tf_op jit(solution)/shard_map/pallas_call | solution.py:363
  (4 shorter events, 0.0 us)
Async XLA Ops:
  1.2 9.0 %collective-permute-start = (bf16[128,1024]{1,0:T(8,128)(2,1)S(1)}, bf16[128,1024]{1,0:T(8,128)(2,1)S(1)}, u32[]{:S(2)}, u32[]{:S(2)}) collective-permute-start(bf16[128,1024]{1,0:T(8,128)(2,1)S(1)} %get-tuple-element.29.product_ref), channel_id=1, source_target_pairs={{0,4},{4,8},{8,12},{12,0},{1,5},{5,9},{9,13},{13,1},{2,6},{6,10},{... | collective-permute-start | bytes 786440 | tf_op jit(solution)/shard_map/ppermute | solution.py:451
  2.9 3.5 %collective-permute-start.1 = (bf16[64,512]{1,0:T(8,128)(2,1)}, bf16[64,512]{1,0:T(8,128)(2,1)S(1)}, u32[]{:S(2)}, u32[]{:S(2)}) collective-permute-start(bf16[64,512]{1,0:T(8,128)(2,1)} %bitcast.12), channel_id=1, source_target_pairs={{0,16},{16,0},{1,17},{17,1},{2,18},{18,2},{3,19},{19,3},{4,20},{20... | collective-permute-start | bytes 196616 | tf_op jit(solution)/shard_map/ppermute | solution.py:382
  2.9 5.2 %collective-permute-start.2 = (bf16[16,256]{1,0:T(8,128)(2,1)S(1)}, bf16[16,256]{1,0:T(8,128)(2,1)S(1)}, u32[]{:S(2)}, u32[]{:S(2)}) collective-permute-start(bf16[16,256]{1,0:T(8,128)(2,1)S(1)} %get-tuple-element.36.refs_0_), channel_id=1, source_target_pairs={{0,3},{1,2},{2,1},{3,0},{4,7},{5,6},{6,5},{7,4},{8,11},{9,10},{10,... | collective-permute-start | bytes 24584 | tf_op jit(solution)/shard_map/ppermute | solution.py:382
  5.3 3.7 %collective-permute-start.3 = (bf16[16,256]{1,0:T(8,128)(2,1)S(1)}, bf16[16,256]{1,0:T(8,128)(2,1)S(1)}, u32[]{:S(2)}, u32[]{:S(2)}) collective-permute-start(bf16[16,256]{1,0:T(8,128)(2,1)S(1)} %get-tuple-element.36.refs_0_), channel_id=1, source_target_pairs={{0,2},{1,3},{2,0},{3,1},{4,6},{5,7},{6,4},{7,5},{8,10},{9,11},{10,... | collective-permute-start | bytes 24584 | tf_op jit(solution)/shard_map/ppermute | solution.py:382
  5.8 3.7 %collective-permute-start.4 = (bf16[16,256]{1,0:T(8,128)(2,1)S(1)}, bf16[16,256]{1,0:T(8,128)(2,1)S(1)}, u32[]{:S(2)}, u32[]{:S(2)}) collective-permute-start(bf16[16,256]{1,0:T(8,128)(2,1)S(1)} %get-tuple-element.36.refs_0_), channel_id=1, source_target_pairs={{0,1},{1,0},{2,3},{3,2},{4,5},{5,4},{6,7},{7,6},{8,9},{9,8},{10,11... | collective-permute-start | bytes 24584 | tf_op jit(solution)/shard_map/ppermute | solution.py:382
  9.5 3.9 %collective-permute-start.5 = (bf16[16,1024]{1,0:T(8,128)(2,1)S(1)}, bf16[16,1024]{1,0:T(8,128)(2,1)S(1)}, u32[]{:S(2)}, u32[]{:S(2)}) collective-permute-start(bf16[16,1024]{1,0:T(8,128)(2,1)S(1)} %shard_map.85.refs_9_._), channel_id=1, source_target_pairs={{0,4},{4,16},{8,24},{12,28},{16,20},{20,0},{24,8},{28,12},{1,5},{5... | collective-permute-start | bytes 98312 | tf_op jit(solution)/shard_map/ppermute | solution.py:393
  13.4 3.4 %collective-permute-start.6 = (bf16[16,1024]{1,0:T(8,128)(2,1)S(1)}, bf16[16,1024]{1,0:T(8,128)(2,1)S(1)}, u32[]{:S(2)}, u32[]{:S(2)}) collective-permute-start(bf16[16,1024]{1,0:T(8,128)(2,1)S(1)} %add_convert_fusion), channel_id=1, source_target_pairs={{0,16},{4,12},{8,20},{12,24},{16,0},{20,28},{24,4},{28,8},{1,17},{... | collective-permute-start | bytes 98312 | tf_op jit(solution)/shard_map/ppermute | solution.py:393
  13.5 3.7 %collective-permute-start.7 = (bf16[16,1024]{1,0:T(8,128)(2,1)S(1)}, bf16[16,1024]{1,0:T(8,128)(2,1)S(1)}, u32[]{:S(2)}, u32[]{:S(2)}) collective-permute-start(bf16[16,1024]{1,0:T(8,128)(2,1)S(1)} %add_convert_fusion), channel_id=1, source_target_pairs={{0,16},{4,8},{8,20},{12,28},{16,0},{20,24},{24,4},{28,12},{1,17},{... | collective-permute-start | bytes 98312 | tf_op jit(solution)/shard_map/ppermute | solution.py:393
  14.0 3.1 %collective-permute-start.8 = (bf16[16,1024]{1,0:T(8,128)(2,1)S(1)}, bf16[16,1024]{1,0:T(8,128)(2,1)S(1)}, u32[]{:S(2)}, u32[]{:S(2)}) collective-permute-start(bf16[16,1024]{1,0:T(8,128)(2,1)S(1)} %get-tuple-element.50), channel_id=1, source_target_pairs={{0,16},{4,20},{8,12},{12,8},{16,0},{20,4},{24,28},{28,24},{1,17},{... | collective-permute-start | bytes 98312 | tf_op jit(solution)/shard_map/ppermute | solution.py:393
